TPU v7x, 32 devices: a whole 2x2x4 slice. The times are simulated.
32 devices in a mesh: gx: 4 (over z), gy: 4 (over y, x), gz: 2 (over core).
Axes of the slice: x: 2, y: 2, z: 4, core: 2. Of those that a mesh axis runs over, the one named last changes fastest.
Arguments:
- right_side: float32 [192, 192, 256], P('gx', 'gy', 'gz'), may hold values from -6 to 6
- conductance: bfloat16 [192, 192, 256], P('gx', 'gy', 'gz'), may hold values from 0.29882812 to 3
- axis_conductivity: float32 [3], replicated, may hold values from 0.4 to 2.5
- x_vectors: float32 [56, 56], replicated, may hold values from -1 to 2
- y_vectors: float32 [56, 56], replicated, may hold values from -1 to 2
- z_vectors: float32 [72, 72], replicated, may hold values from -1 to 2
- x_values: float32 [56], replicated, may hold values from 0.05 to 4
- y_values: float32 [56], replicated, may hold values from 0.05 to 4
- z_values: float32 [72], replicated, may hold values from 0.05 to 4
- coarse_inverse: float32 [16, 16], replicated, may hold values from -1 to 4
Outputs:
- solution: float32 [192, 192, 256], P('gx', 'gy', 'gz')
- residual: float32 [192, 192, 256], P('gx', 'gy', 'gz')
All inputs are finite; a program needn't handle non-finite values.
Results may differ from a plain program's by a relative error of at most 0.0003.
Values may be sent and summed in bfloat16 or wider, within the bound.
No kernel may reach another device: no remote copies, remote signals or barrier semaphores. Data moves between devices by JAX's collectives and lax.ppermute only.
A program may use at most 64 MiB of HBM per device.

v0:
```python
import jax
import jax.numpy as jnp
from jax import lax
from jax.sharding import PartitionSpec as P

SZ = 64
OV = 4


exact_mode = lax.Precision.HIGHEST


def padded_2(cells, sides, width):
    for axis, dim in sides:
        count = lax.axis_size(axis)
        ends = count - 1
        head = lax.slice_in_dim(cells, 0, width, axis=dim)
        tail = lax.slice_in_dim(cells, cells.shape[dim] - width, cells.shape[dim], axis=dim)
        cells = jnp.concatenate(
            [
                lax.ppermute(tail, axis, [(i, (i + 1) % count) for i in range(ends)]),
                cells,
                lax.ppermute(head, axis, [((i + 1) % count, i) for i in range(ends)]),
            ],
            axis=dim,
        )
    return cells


def apply_operator(padded_field, padded_scale, axis_conductivity):
    center = padded_field[1:-1, 1:-1, 1:-1]
    own_scale = padded_scale[1:-1, 1:-1, 1:-1]
    summed = jnp.zeros(center.shape, jnp.float32)
    for dimension in range(3):
        for offset in (0, 2):
            selection = [slice(1, -1), slice(1, -1), slice(1, -1)]
            selection[dimension] = slice(offset, offset + center.shape[dimension])
            neighbour = padded_field[tuple(selection)]
            other_scale = padded_scale[tuple(selection)]
            weight = axis_conductivity[dimension] * 0.5 * (own_scale + other_scale)
            summed = summed + weight * (center - neighbour)
    return summed


def fold_rims(padded, dimension):
    length = padded.shape[dimension]
    core = length - 4 * OV
    middle = lax.slice_in_dim(padded, 2 * OV, 2 * OV + core, axis=dimension)
    lowers = lax.slice_in_dim(padded, 0, OV, axis=dimension)
    uppers = lax.slice_in_dim(padded, length - OV, length, axis=dimension)
    low_pad = [(0, 0), (0, 0), (0, 0)]
    low_pad[dimension] = (0, core - OV)
    high_pad = [(0, 0), (0, 0), (0, 0)]
    high_pad[dimension] = (core - OV, 0)
    return middle + jnp.pad(lowers, low_pad) + jnp.pad(uppers, high_pad)


def extend(field):
    return padded_2(field, (("gx", 0), ("gy", 1), ("gz", 2)), OV)


def local_part(extended, x_vectors, y_vectors, block_z, denominators):
    first = jnp.einsum("abc,ai->ibc", extended, x_vectors, precision=exact_mode)
    second = jnp.einsum("ibc,bj->ijc", first, y_vectors, precision=exact_mode)
    third = jnp.einsum("ijc,cm->ijm", second, block_z, precision=exact_mode)
    scaled = third / denominators
    back_z = jnp.einsum("ijm,cm->ijc", scaled, block_z, precision=exact_mode)
    back_y = jnp.einsum("ijc,bj->ibc", back_z, y_vectors, precision=exact_mode)
    spread = jnp.einsum("ibc,ai->abc", back_y, x_vectors, precision=exact_mode)
    returned = padded_2(spread, (("gx", 0), ("gy", 1), ("gz", 2)), OV)
    return fold_rims(fold_rims(fold_rims(returned, 0), 1), 2)


def body(
    right_side,
    conductance,
    axis_conductivity,
    x_vectors,
    y_vectors,
    z_vectors,
    x_values,
    y_values,
    z_values,
    coarse_inverse,
):
    extent_x, extent_y, depth_z = right_side.shape
    ez_size = z_vectors.shape[0]
    sub_count = depth_z // SZ
    block_z = jnp.zeros((depth_z + 2 * OV, sub_count, ez_size), jnp.float32)
    for block in range(sub_count):
        block_z = block_z.at[block * SZ : block * SZ + ez_size, block, :].set(z_vectors)
    block_z = block_z.reshape(depth_z + 2 * OV, sub_count * ez_size)
    denominators = (
        axis_conductivity[0] * x_values[:, None, None]
        + axis_conductivity[1] * y_values[None, :, None]
        + axis_conductivity[2] * z_values[None, None, :]
    )
    denominators = jnp.tile(denominators, (1, 1, sub_count))
    flat_index = (
        lax.axis_index("gx") * lax.axis_size("gy") + lax.axis_index("gy")
    ) * lax.axis_size("gz") + lax.axis_index("gz")
    coarse_count = lax.axis_size("gx") * lax.axis_size("gy") * lax.axis_size("gz") // 2
    slots = jnp.arange(coarse_count) == flat_index // 2
    cells_pair = 2.0 * extent_x * extent_y * depth_z
    residual = right_side
    extended = extend(residual)
    scale_pad = padded_2(conductance, (("gx", 0), ("gy", 1), ("gz", 2)), 1).astype(jnp.float32)
    local = local_part(extended, x_vectors, y_vectors, block_z, denominators)
    onehot = jnp.where(slots, jnp.sum(residual), 0.0)
    totals = lax.psum(onehot, ("gx", "gy", "gz"))
    coarse_value = jnp.dot(coarse_inverse, totals / cells_pair, precision=exact_mode)
    shifted = local + jnp.sum(jnp.where(slots, coarse_value, 0.0))
    product = lax.psum(jnp.sum(residual * shifted), ("gx", "gy", "gz"))
    shifted, product_now = (shifted, product)
    padded = padded_2(shifted, (("gx", 0), ("gy", 1), ("gz", 2)), 1)
    applied = apply_operator(padded, scale_pad, axis_conductivity)
    curvature = lax.psum(jnp.sum(shifted * applied), ("gx", "gy", "gz"))
    step_size = product_now / curvature
    solution = step_size * shifted
    residual = residual - step_size * applied
    return (solution, residual)


def solution(mesh):
    in_specs = (P("gx", "gy", "gz"), P("gx", "gy", "gz"), P(), P(), P(), P(), P(), P(), P(), P())
    out_specs = (P("gx", "gy", "gz"), P("gx", "gy", "gz"))
    return jax.shard_map(body, mesh=mesh, in_specs=in_specs, out_specs=out_specs, check_vma=False)
```

profile of v0, /device:TPU:0, one launch (start us, length us, event | category | flops | bytes accessed | tf_op | source)
XLA Modules:
  0.0 277.5 jit_solution(5482724699486668175)
XLA Ops:
  2.4 4.9 %collective-permute-start = (f32[4,48,128]{2,0,1:T(4,128)S(1)}, f32[4,48,128]{2,0,1:T(4,128)S(1)}, u32[]{:S(2)}, u32[]{:S(2)}) collective-permute-start(f32[4,48,128]{2,0,1:T(4,128)S(1)} %get-tuple-element.53), channel_id=1, source_target_pairs={{0,8},{8,16},{16,24},{1,9},{9,17},{17,25},{2,10},{10,18},{18,26},{... | collective-permute-start | bytes 294920 | tf_op jit(solution)/shard_map/ppermute | solution.py:21
  11.3 2.6 collective-permute-done.1
  13.9 3.4 %collective-permute-start.2 = (f32[56,4,128]{2,0,1:T(8,128)S(1)}, f32[56,4,128]{2,0,1:T(8,128)S(1)}, u32[]{:S(2)}, u32[]{:S(2)}) collective-permute-start(f32[56,4,128]{2,0,1:T(8,128)S(1)} %get-tuple-element.47), channel_id=1, source_target_pairs={{0,2},{2,4},{4,6},{1,3},{3,5},{5,7},{8,10},{10,12},{12,14},{9,11},... | collective-permute-start | bytes 344072 | tf_op jit(solution)/shard_map/ppermute | solution.py:21
  20.3 3.7 %collective-permute-done.3 = f32[56,4,128]{2,0,1:T(8,128)S(1)} collective-permute-done((f32[56,4,128]{2,0,1:T(8,128)S(1)}, f32[56,4,128]{2,0,1:T(8,128)S(1)}, u32[]{:S(2)}, u32[]{:S(2)}) %collective-permute-start.3) | collective-permute-done | bytes 114720 | tf_op jit(solution)/shard_map/ppermute | solution.py:23
  31.1 2.5 tile.4
  33.7 3.5 %tile.10 = f32[56,56,144]{2,1,0:T(8,128)} reshape(f32[56,56,2,72]{3,2,1,0:T(2,128)S(1)} %tile.4) | data formatting | bytes 3612672 | tf_op jit(solution)/shard_map/tile | solution.py:98
  40.8 2.6 copy.33
  43.5 5.7 %fusion.38 = f32[56,56,136]{2,0,1:T(8,128)S(1)} fusion(f32[56,56,4]{2,0,1:T(8,128)} %copy.33, f32[56,4,128]{2,0,1:T(8,128)S(1)} %copy-done.25, f32[4,48,128]{2,0,1:T(4,128)S(1)} %copy-done.14, f32[48,48,128]{2,0,1:T(8,128)S(1)} %copy-done.7, f32[4,48,128]{2,0,1:T(4,128)S(1)} %copy-done.12, f32[56,4,128]{2,0,1:T(8,128)S(1)} %copy-done.23, ...), kind=kOutput, calls=%fused_computation.44 | convolution fusion | flops 289164288 | bytes 3424512 | tf_op jit(solution)/shard_map/abc,ai->ibc/dot_general | solution.py:63
  49.2 4.1 %fusion.18 = f32[56,136,56]{1,2,0:T(8,128)S(1)} fusion(f32[56,56,136]{2,0,1:T(8,128)S(1)} %fusion.38, f32[56,56]{1,0:T(8,128)S(1)} %copy-done), kind=kOutput, calls=%fused_computation.20 | convolution fusion | flops 286605312 | bytes 3424512 | tf_op jit(solution)/shard_map/ibc,bj->ijc/dot_general | solution.py:64
  53.3 2.8 %fusion.14 = f32[56,56,144]{2,1,0:T(8,128)S(1)} fusion(f32[136,144,1]{0,1,2:T(8,128)S(1)} %bitcast.43, f32[56,136,56]{1,2,0:T(8,128)S(1)} %fusion.18), kind=kOutput, calls=%fused_computation.16 | convolution fusion | flops 736985088 | bytes 3590656 | tf_op jit(solution)/shard_map/ijc,cm->ijm/dot_general | solution.py:65
  56.2 3.1 %fusion.20 = f32[56,56,136]{2,1,0:T(8,128)S(1)} fusion(f32[136,144,1]{0,1,2:T(8,128)S(1)} %bitcast.44, f32[56,56,144]{2,1,0:T(8,128)S(1)} %fusion.14, f32[56,56,144]{2,1,0:T(8,128)S(1)} %copy-done.10), kind=kOutput, calls=%fused_computation.22 | convolution fusion | flops 737436672 | bytes 5396992 | tf_op jit(solution)/shard_map/ijm,cm->ijc/dot_general | solution.py:67
  59.3 3.1 %convolution_bitcast_fusion = f32[56,56,136]{2,1,0:T(8,128)S(1)} fusion(f32[56,56,136]{2,1,0:T(8,128)S(1)} %fusion.20, f32[56,56]{1,0:T(8,128)S(1)} %copy-done), kind=kOutput, calls=%fused_computation.43 | convolution fusion | flops 286605312 | bytes 3424512 | tf_op jit(solution)/shard_map/ijc,bj->ibc/dot_general | solution.py:68
  62.4 4.1 %fusion.35 = f32[56,56,136]{2,0,1:T(8,128)S(1)} fusion(f32[56,56,136]{2,1,0:T(8,128)S(1)} %convolution_bitcast_fusion, f32[56,56]{1,0:T(8,128)S(1)} %copy-done.26), kind=kOutput, calls=%fused_computation.42 | convolution fusion | flops 286605312 | bytes 3424512 | tf_op jit(solution)/shard_map/ibc,ai->abc/dot_general | solution.py:69
  67.4 3.5 %collective-permute-start.6 = (f32[4,56,136]{2,0,1:T(4,128)}, f32[4,56,136]{2,0,1:T(4,128)S(1)}, u32[]{:S(2)}, u32[]{:S(2)}) collective-permute-start(f32[4,56,136]{2,0,1:T(4,128)} %get-tuple-element.41), channel_id=1, source_target_pairs={{0,8},{8,16},{16,24},{1,9},{9,17},{17,25},{2,10},{10,18},{18,26},{... | collective-permute-start | bytes 365576 | tf_op jit(solution)/shard_map/ppermute | solution.py:21
  73.7 4.5 %collective-permute-start.12 = (bf16[1,48,128]{2,0,1:T(2,128)(2,1)}, bf16[1,48,128]{2,0,1:T(2,128)(2,1)S(1)}, u32[]{:S(2)}, u32[]{:S(2)}) collective-permute-start(bf16[1,48,128]{2,0,1:T(2,128)(2,1)} %get-tuple-element.59), channel_id=1, source_target_pairs={{0,8},{8,16},{16,24},{1,9},{9,17},{17,25},{2,10},{10,18},{18,26},{... | collective-permute-start | bytes 36872 | tf_op jit(solution)/shard_map/ppermute | solution.py:21
  82.7 5.0 %collective-permute-start.8 = (f32[64,4,136]{2,0,1:T(8,128)}, f32[64,4,136]{2,0,1:T(8,128)}, u32[]{:S(2)}, u32[]{:S(2)}) collective-permute-start(f32[64,4,136]{2,0,1:T(8,128)} %get-tuple-element.39), channel_id=1, source_target_pairs={{0,2},{2,4},{4,6},{1,3},{3,5},{5,7},{8,10},{10,12},{12,14},{9,11},... | collective-permute-start | bytes 417800 | tf_op jit(solution)/shard_map/ppermute | solution.py:21
  90.9 41.5 %psum.21 = f32[16]{0:T(128)S(1)} all-reduce(f32[16]{0:T(128)S(1)} %compare_select_fusion), channel_id=1, replica_groups=mesh['gx'=4,'gy'=4,'gz'=2] {'gx','gy','gz'}, use_global_device_ids=true, to_apply=%region_1.0 | all-reduce | flops 16 | bytes 128 | tf_op jit(solution)/shard_map/psum | solution.py:110
  134.9 2.9 %fusion.79 = (f32[64,64,4]{2,0,1:T(8,128)}, f32[64,64,4]{2,0,1:T(8,128)}) fusion(f32[64,64,136]{2,0,1:T(8,128)S(1)} %pad_maximum_fusion), kind=kLoop, calls=%fused_computation.135 | loop fusion | bytes 262144 | tf_op jit(solution)/shard_map/slice | solution.py:18
  137.8 3.3 %copy.41 = f32[64,64,4]{1,0,2:T(8,128)} copy(f32[64,64,4]{2,0,1:T(8,128)} %get-tuple-element.37) | data formatting | bytes 131072 | tf_op jit(solution)/shard_map/slice | solution.py:18
  143.0 3.3 %copy.42 = f32[64,64,4]{1,0,2:T(8,128)} copy(f32[64,64,4]{2,0,1:T(8,128)} %get-tuple-element.38) | data formatting | bytes 131072 | tf_op jit(solution)/shard_map/slice | solution.py:17
  149.0 4.3 %collective-permute-start.14 = (bf16[50,1,128]{2,0,1:T(8,128)(2,1)}, bf16[50,1,128]{2,0,1:T(8,128)(2,1)S(1)}, u32[]{:S(2)}, u32[]{:S(2)}) collective-permute-start(bf16[50,1,128]{2,0,1:T(8,128)(2,1)} %get-tuple-element.57), channel_id=1, source_target_pairs={{0,2},{2,4},{4,6},{1,3},{3,5},{5,7},{8,10},{10,12},{12,14},{9,11},... | collective-permute-start | bytes 38408 | tf_op jit(solution)/shard_map/ppermute | solution.py:21
  154.6 3.8 %copy.43 = f32[64,64,4]{2,0,1:T(8,128)} copy(f32[64,64,4]{1,0,2:T(8,128)} %collective-permute-done.10) | data formatting | bytes 131072 | tf_op jit(solution)/shard_map/ppermute | solution.py:21
  158.5 3.8 %copy.44 = f32[64,64,4]{2,0,1:T(8,128)} copy(f32[64,64,4]{1,0,2:T(8,128)} %collective-permute-done.11) | data formatting | bytes 131072 | tf_op jit(solution)/shard_map/ppermute | solution.py:23
  162.3 6.3 %pad_maximum_fusion.1 = f32[64,64,144]{2,0,1:T(8,128)S(1)} fusion(f32[64,64,4]{2,0,1:T(8,128)} %copy.44, f32[64,4,136]{2,0,1:T(8,128)} %collective-permute-done.9, f32[4,56,136]{2,0,1:T(4,128)} %collective-permute-done.7, f32[56,56,136]{2,0,1:T(8,128)S(1)} %fusion.35, f32[4,56,136]{2,0,1:T(4,128)S(1)} %collective-permute-done.6, ...), kind=kLoop, calls=%fused_computation.1 | loop fusion | flops 3538944 | bytes 4718592 | tf_op jit(solution)/shard_map/concatenate | solution.py:19
  178.0 3.3 %collective-permute-done.19 = f32[1,48,128]{2,0,1:T(1,128)S(1)} collective-permute-done((f32[1,48,128]{2,0,1:T(1,128)S(1)}, f32[1,48,128]{2,0,1:T(1,128)S(1)}, u32[]{:S(2)}, u32[]{:S(2)}) %collective-permute-start.19) | collective-permute-done | bytes 24608 | tf_op jit(solution)/shard_map/ppermute | solution.py:23
  181.3 4.8 %collective-permute-start.20 = (f32[50,1,128]{2,0,1:T(8,128)S(1)}, f32[50,1,128]{2,0,1:T(8,128)S(1)}, u32[]{:S(2)}, u32[]{:S(2)}) collective-permute-start(f32[50,1,128]{2,0,1:T(8,128)S(1)} %get-tuple-element.49), channel_id=1, source_target_pairs={{0,2},{2,4},{4,6},{1,3},{3,5},{5,7},{8,10},{10,12},{12,14},{9,11},... | collective-permute-start | bytes 76808 | tf_op jit(solution)/shard_map/ppermute | solution.py:21
  201.5 3.6 %collective-permute-start.22 = (f32[50,50,1]{1,2,0:T(1,128)}, f32[50,50,1]{1,2,0:T(1,128)}, u32[]{:S(2)}, u32[]{:S(2)}) collective-permute-start(f32[50,50,1]{1,2,0:T(1,128)} %copy.53), channel_id=1, source_target_pairs={{0,1},{2,3},{4,5},{6,7},{8,9},{10,11},{12,13},{14,15},{16,17},{18,... | collective-permute-start | bytes 30008 | tf_op jit(solution)/shard_map/ppermute | solution.py:21
  207.6 2.5 maximum_convert_fusion
  210.1 2.5 copy.54
  212.6 2.5 copy.56
  215.1 12.5 %multiply_reduce_fusion = (f32[]{:T(128)}, f32[]{:T(128)}, f32[48,48,128]{2,0,1:T(8,128)}) fusion(f32[48,48,128]{2,0,1:T(8,128)} %copy-done.2, f32[48,48,128]{2,1,0:T(8,128)} %param.14, f32[50,50,1]{2,0,1:T(8,128)} %copy.56, f32[50,1,128]{2,0,1:T(8,128)S(1)} %copy-done.21, f32[1,48,128]{2,0,1:T(1,128)S(1)} %collective-permute-done.19, ...), kind=kLoop, calls=%fused_computation.100 | loop fusion | flops 15040510 | bytes 11916852 | tf_op jit(solution)/shard_map/reduce_sum | solution.py:117
  227.7 43.6 %all-reduce.4 = (f32[]{:T(128)}, f32[]{:T(128)}) all-reduce(f32[]{:T(128)} %get-tuple-element.33, f32[]{:T(128)} %get-tuple-element.32), channel_id=1, replica_groups=mesh['gx'=4,'gy'=4,'gz'=2] {'gx','gy','gz'}, use_global_device_ids=true, to_apply=%region_4.5 | all-reduce | flops 2 | bytes 16 | tf_op jit(solution)/shard_map/psum | solution.py:113
  (151 shorter events, 68.9 us)
Async XLA Ops:
  0.6 48.6 %copy-start = (f32[56,56]{1,0:T(8,128)S(1)}, f32[56,56]{1,0:T(8,128)}, u32[]{:S(2)}) copy-start(f32[56,56]{1,0:T(8,128)} %param.18) | copy-start | bytes 37636
  2.4 21.6 %copy-start.6 = (f32[48,48,128]{2,0,1:T(8,128)}, f32[48,48,128]{2,0,1:T(8,128)S(1)}, u32[]{:S(2)}) copy-start(f32[48,48,128]{2,0,1:T(8,128)S(1)} %copy.45) | copy-start | bytes 3538948
  2.4 8.9 %collective-permute-start = (f32[4,48,128]{2,0,1:T(4,128)S(1)}, f32[4,48,128]{2,0,1:T(4,128)S(1)}, u32[]{:S(2)}, u32[]{:S(2)}) collective-permute-start(f32[4,48,128]{2,0,1:T(4,128)S(1)} %get-tuple-element.53), channel_id=1, source_target_pairs={{0,8},{8,16},{16,24},{1,9},{9,17},{17,25},{2,10},{10,18},{18,26},{... | collective-permute-start | bytes 294920 | tf_op jit(solution)/shard_map/ppermute | solution.py:21
  7.4 6.5 %collective-permute-start.1 = (f32[4,48,128]{2,0,1:T(4,128)S(1)}, f32[4,48,128]{2,0,1:T(4,128)S(1)}, u32[]{:S(2)}, u32[]{:S(2)}) collective-permute-start(f32[4,48,128]{2,0,1:T(4,128)S(1)} %get-tuple-element.54), channel_id=1, source_target_pairs={{8,0},{16,8},{24,16},{9,1},{17,9},{25,17},{10,2},{18,10},{26,18},{... | collective-permute-start | bytes 294920 | tf_op jit(solution)/shard_map/ppermute | solution.py:23
  11.3 12.7 %copy-start.11 = (f32[4,48,128]{2,0,1:T(4,128)}, f32[4,48,128]{2,0,1:T(4,128)S(1)}, u32[]{:S(2)}) copy-start(f32[4,48,128]{2,0,1:T(4,128)S(1)} %collective-permute-done) | copy-start | bytes 294916
  13.9 6.4 %collective-permute-start.2 = (f32[56,4,128]{2,0,1:T(8,128)S(1)}, f32[56,4,128]{2,0,1:T(8,128)S(1)}, u32[]{:S(2)}, u32[]{:S(2)}) collective-permute-start(f32[56,4,128]{2,0,1:T(8,128)S(1)} %get-tuple-element.47), channel_id=1, source_target_pairs={{0,2},{2,4},{4,6},{1,3},{3,5},{5,7},{8,10},{10,12},{12,14},{9,11},... | collective-permute-start | bytes 344072 | tf_op jit(solution)/shard_map/ppermute | solution.py:21
  17.3 6.7 %collective-permute-start.3 = (f32[56,4,128]{2,0,1:T(8,128)S(1)}, f32[56,4,128]{2,0,1:T(8,128)S(1)}, u32[]{:S(2)}, u32[]{:S(2)}) collective-permute-start(f32[56,4,128]{2,0,1:T(8,128)S(1)} %get-tuple-element.48), channel_id=1, source_target_pairs={{2,0},{4,2},{6,4},{3,1},{5,3},{7,5},{10,8},{12,10},{14,12},{11,9},... | collective-permute-start | bytes 344072 | tf_op jit(solution)/shard_map/ppermute | solution.py:23
  26.6 12.6 %collective-permute-start.4 = (f32[56,56,4]{1,0,2:T(8,128)}, f32[56,56,4]{1,0,2:T(8,128)}, u32[]{:S(2)}, u32[]{:S(2)}) collective-permute-start(f32[56,56,4]{1,0,2:T(8,128)} %copy.30), channel_id=1, source_target_pairs={{0,1},{2,3},{4,5},{6,7},{8,9},{10,11},{12,13},{14,15},{16,17},{18,... | collective-permute-start | bytes 150536 | tf_op jit(solution)/shard_map/ppermute | solution.py:21
  29.7 11.1 %collective-permute-start.5 = (f32[56,56,4]{1,0,2:T(8,128)}, f32[56,56,4]{1,0,2:T(8,128)}, u32[]{:S(2)}, u32[]{:S(2)}) collective-permute-start(f32[56,56,4]{1,0,2:T(8,128)} %copy.31), channel_id=1, source_target_pairs={{1,0},{3,2},{5,4},{7,6},{9,8},{11,10},{13,12},{15,14},{17,16},{19,... | collective-permute-start | bytes 150536 | tf_op jit(solution)/shard_map/ppermute | solution.py:23
  67.4 13.1 %collective-permute-start.6 = (f32[4,56,136]{2,0,1:T(4,128)}, f32[4,56,136]{2,0,1:T(4,128)S(1)}, u32[]{:S(2)}, u32[]{:S(2)}) collective-permute-start(f32[4,56,136]{2,0,1:T(4,128)} %get-tuple-element.41), channel_id=1, source_target_pairs={{0,8},{8,16},{16,24},{1,9},{9,17},{17,25},{2,10},{10,18},{18,26},{... | collective-permute-start | bytes 365576 | tf_op jit(solution)/shard_map/ppermute | solution.py:21
  70.8 10.2 %collective-permute-start.7 = (f32[4,56,136]{2,0,1:T(4,128)}, f32[4,56,136]{2,0,1:T(4,128)}, u32[]{:S(2)}, u32[]{:S(2)}) collective-permute-start(f32[4,56,136]{2,0,1:T(4,128)} %get-tuple-element.42), channel_id=1, source_target_pairs={{8,0},{16,8},{24,16},{9,1},{17,9},{25,17},{10,2},{18,10},{26,18},{... | collective-permute-start | bytes 365576 | tf_op jit(solution)/shard_map/ppermute | solution.py:23
  73.7 73.9 %collective-permute-start.12 = (bf16[1,48,128]{2,0,1:T(2,128)(2,1)}, bf16[1,48,128]{2,0,1:T(2,128)(2,1)S(1)}, u32[]{:S(2)}, u32[]{:S(2)}) collective-permute-start(bf16[1,48,128]{2,0,1:T(2,128)(2,1)} %get-tuple-element.59), channel_id=1, source_target_pairs={{0,8},{8,16},{16,24},{1,9},{9,17},{17,25},{2,10},{10,18},{18,26},{... | collective-permute-start | bytes 36872 | tf_op jit(solution)/shard_map/ppermute | solution.py:21
  80.5 51.9 %copy-start.27 = (f32[16,16]{1,0:T(8,128)S(1)}, f32[16,16]{1,0:T(8,128)}, u32[]{:S(2)}) copy-start(f32[16,16]{1,0:T(8,128)} %param.23) | copy-start | bytes 3076
  82.7 50.5 %collective-permute-start.8 = (f32[64,4,136]{2,0,1:T(8,128)}, f32[64,4,136]{2,0,1:T(8,128)}, u32[]{:S(2)}, u32[]{:S(2)}) collective-permute-start(f32[64,4,136]{2,0,1:T(8,128)} %get-tuple-element.39), channel_id=1, source_target_pairs={{0,2},{2,4},{4,6},{1,3},{3,5},{5,7},{8,10},{10,12},{12,14},{9,11},... | collective-permute-start | bytes 417800 | tf_op jit(solution)/shard_map/ppermute | solution.py:21
  87.7 45.5 %collective-permute-start.9 = (f32[64,4,136]{2,0,1:T(8,128)}, f32[64,4,136]{2,0,1:T(8,128)}, u32[]{:S(2)}, u32[]{:S(2)}) collective-permute-start(f32[64,4,136]{2,0,1:T(8,128)} %get-tuple-element.40), channel_id=1, source_target_pairs={{2,0},{4,2},{6,4},{3,1},{5,3},{7,5},{10,8},{12,10},{14,12},{11,9},... | collective-permute-start | bytes 417800 | tf_op jit(solution)/shard_map/ppermute | solution.py:23
  89.6 58.0 %collective-permute-start.13 = (bf16[1,48,128]{2,0,1:T(2,128)(2,1)S(1)}, bf16[1,48,128]{2,0,1:T(2,128)(2,1)S(1)}, u32[]{:S(2)}, u32[]{:S(2)}) collective-permute-start(bf16[1,48,128]{2,0,1:T(2,128)(2,1)S(1)} %get-tuple-element.60), channel_id=1, source_target_pairs={{8,0},{16,8},{24,16},{9,1},{17,9},{25,17},{10,2},{18,10},{26,18},{... | collective-permute-start | bytes 36872 | tf_op jit(solution)/shard_map/ppermute | solution.py:23
  141.1 13.5 %collective-permute-start.10 = (f32[64,64,4]{1,0,2:T(8,128)}, f32[64,64,4]{1,0,2:T(8,128)}, u32[]{:S(2)}, u32[]{:S(2)}) collective-permute-start(f32[64,64,4]{1,0,2:T(8,128)} %copy.41), channel_id=1, source_target_pairs={{0,1},{2,3},{4,5},{6,7},{8,9},{10,11},{12,13},{14,15},{16,17},{18,... | collective-permute-start | bytes 196616 | tf_op jit(solution)/shard_map/ppermute | solution.py:21
  146.4 12.1 %collective-permute-start.11 = (f32[64,64,4]{1,0,2:T(8,128)}, f32[64,64,4]{1,0,2:T(8,128)}, u32[]{:S(2)}, u32[]{:S(2)}) collective-permute-start(f32[64,64,4]{1,0,2:T(8,128)} %copy.42), channel_id=1, source_target_pairs={{1,0},{3,2},{5,4},{7,6},{9,8},{11,10},{13,12},{15,14},{17,16},{19,... | collective-permute-start | bytes 196616 | tf_op jit(solution)/shard_map/ppermute | solution.py:23
  147.7 14.6 %copy-start.15 = (bf16[1,48,128]{2,0,1:T(2,128)(2,1)}, bf16[1,48,128]{2,0,1:T(2,128)(2,1)S(1)}, u32[]{:S(2)}) copy-start(bf16[1,48,128]{2,0,1:T(2,128)(2,1)S(1)} %collective-permute-done.13) | copy-start | bytes 36868
  149.0 27.8 %collective-permute-start.14 = (bf16[50,1,128]{2,0,1:T(8,128)(2,1)}, bf16[50,1,128]{2,0,1:T(8,128)(2,1)S(1)}, u32[]{:S(2)}, u32[]{:S(2)}) collective-permute-start(bf16[50,1,128]{2,0,1:T(8,128)(2,1)} %get-tuple-element.57), channel_id=1, source_target_pairs={{0,2},{2,4},{4,6},{1,3},{3,5},{5,7},{8,10},{10,12},{12,14},{9,11},... | collective-permute-start | bytes 38408 | tf_op jit(solution)/shard_map/ppermute | solution.py:21
  153.3 23.5 %collective-permute-start.15 = (bf16[50,1,128]{2,0,1:T(8,128)(2,1)}, bf16[50,1,128]{2,0,1:T(8,128)(2,1)}, u32[]{:S(2)}, u32[]{:S(2)}) collective-permute-start(bf16[50,1,128]{2,0,1:T(8,128)(2,1)} %get-tuple-element.58), channel_id=1, source_target_pairs={{2,0},{4,2},{6,4},{3,1},{5,3},{7,5},{10,8},{12,10},{14,12},{11,9},... | collective-permute-start | bytes 38408 | tf_op jit(solution)/shard_map/ppermute | solution.py:23
  173.3 25.2 %copy-start.2 = (f32[48,48,128]{2,0,1:T(8,128)}, f32[48,48,128]{2,0,1:T(8,128)S(1)}, u32[]{:S(2)}) copy-start(f32[48,48,128]{2,0,1:T(8,128)S(1)} %fusion.66) | copy-start | bytes 3538948
  173.4 4.6 %collective-permute-start.18 = (f32[1,48,128]{2,0,1:T(1,128)S(1)}, f32[1,48,128]{2,0,1:T(1,128)S(1)}, u32[]{:S(2)}, u32[]{:S(2)}) collective-permute-start(f32[1,48,128]{2,0,1:T(1,128)S(1)} %get-tuple-element.51), channel_id=1, source_target_pairs={{0,8},{8,16},{16,24},{1,9},{9,17},{17,25},{2,10},{10,18},{18,26},{... | collective-permute-start | bytes 73736 | tf_op jit(solution)/shard_map/ppermute | solution.py:21
  175.5 5.7 %collective-permute-start.19 = (f32[1,48,128]{2,0,1:T(1,128)S(1)}, f32[1,48,128]{2,0,1:T(1,128)S(1)}, u32[]{:S(2)}, u32[]{:S(2)}) collective-permute-start(f32[1,48,128]{2,0,1:T(1,128)S(1)} %get-tuple-element.52), channel_id=1, source_target_pairs={{8,0},{16,8},{24,16},{9,1},{17,9},{25,17},{10,2},{18,10},{26,18},{... | collective-permute-start | bytes 73736 | tf_op jit(solution)/shard_map/ppermute | solution.py:23
  181.3 17.2 %collective-permute-start.20 = (f32[50,1,128]{2,0,1:T(8,128)S(1)}, f32[50,1,128]{2,0,1:T(8,128)S(1)}, u32[]{:S(2)}, u32[]{:S(2)}) collective-permute-start(f32[50,1,128]{2,0,1:T(8,128)S(1)} %get-tuple-element.49), channel_id=1, source_target_pairs={{0,2},{2,4},{4,6},{1,3},{3,5},{5,7},{8,10},{10,12},{12,14},{9,11},... | collective-permute-start | bytes 76808 | tf_op jit(solution)/shard_map/ppermute | solution.py:21
  186.1 12.5 %collective-permute-start.21 = (f32[50,1,128]{2,0,1:T(8,128)S(1)}, f32[50,1,128]{2,0,1:T(8,128)S(1)}, u32[]{:S(2)}, u32[]{:S(2)}) collective-permute-start(f32[50,1,128]{2,0,1:T(8,128)S(1)} %get-tuple-element.50), channel_id=1, source_target_pairs={{2,0},{4,2},{6,4},{3,1},{5,3},{7,5},{10,8},{12,10},{14,12},{11,9},... | collective-permute-start | bytes 76808 | tf_op jit(solution)/shard_map/ppermute | solution.py:23
  190.3 5.4 %collective-permute-start.16 = (bf16[50,50,1]{1,0,2:T(8,128)(2,1)S(1)}, bf16[50,50,1]{1,0,2:T(8,128)(2,1)S(1)}, u32[]{:S(2)}, u32[]{:S(2)}) collective-permute-start(bf16[50,50,1]{1,0,2:T(8,128)(2,1)S(1)} %copy.49), channel_id=1, source_target_pairs={{0,1},{2,3},{4,5},{6,7},{8,9},{10,11},{12,13},{14,15},{16,17},{18,... | collective-permute-start | bytes 15008 | tf_op jit(solution)/shard_map/ppermute | solution.py:21
  192.6 4.5 %collective-permute-start.17 = (bf16[50,50,1]{1,0,2:T(8,128)(2,1)S(1)}, bf16[50,50,1]{1,0,2:T(8,128)(2,1)S(1)}, u32[]{:S(2)}, u32[]{:S(2)}) collective-permute-start(bf16[50,50,1]{1,0,2:T(8,128)(2,1)S(1)} %copy.50), channel_id=1, source_target_pairs={{1,0},{3,2},{5,4},{7,6},{9,8},{11,10},{13,12},{15,14},{17,16},{19,... | collective-permute-start | bytes 15008 | tf_op jit(solution)/shard_map/ppermute | solution.py:23
  201.5 8.6 %collective-permute-start.22 = (f32[50,50,1]{1,2,0:T(1,128)}, f32[50,50,1]{1,2,0:T(1,128)}, u32[]{:S(2)}, u32[]{:S(2)}) collective-permute-start(f32[50,50,1]{1,2,0:T(1,128)} %copy.53), channel_id=1, source_target_pairs={{0,1},{2,3},{4,5},{6,7},{8,9},{10,11},{12,13},{14,15},{16,17},{18,... | collective-permute-start | bytes 30008 | tf_op jit(solution)/shard_map/ppermute | solution.py:21
  206.3 6.3 %collective-permute-start.23 = (f32[50,50,1]{1,2,0:T(1,128)}, f32[50,50,1]{1,2,0:T(1,128)}, u32[]{:S(2)}, u32[]{:S(2)}) collective-permute-start(f32[50,50,1]{1,2,0:T(1,128)} %copy.55), channel_id=1, source_target_pairs={{1,0},{3,2},{5,4},{7,6},{9,8},{11,10},{13,12},{15,14},{17,16},{19,... | collective-permute-start | bytes 30008 | tf_op jit(solution)/shard_map/ppermute | solution.py:23
  227.7 46.3 %copy-start.3 = (f32[48,48,128]{2,1,0:T(8,128)S(1)}, f32[48,48,128]{2,1,0:T(8,128)}, u32[]{:S(2)}) copy-start(f32[48,48,128]{2,1,0:T(8,128)} %param.14) | copy-start | bytes 3538948
  227.7 46.3 %copy-start.9 = (f32[48,48,128]{2,0,1:T(8,128)S(1)}, f32[48,48,128]{2,0,1:T(8,128)}, u32[]{:S(2)}) copy-start(f32[48,48,128]{2,0,1:T(8,128)} %get-tuple-element.36) | copy-start | bytes 3538948
  (26 other events, 131.2 us)
where the time goes:
time: 283 us; the launch traced here: 278 us
  blocking collectives  85 us (30%)
  starting transfers between devices  57.5 us (20%)
  local copies, waits for them, and re-layouts  56.6 us (20%)
  other arithmetic  39.5 us (14%)
  matrix products  23.7 us (8%)
  waiting for transfers between devices  10.2 us (4%)
  between operations  5.04 us (2%)
    psum x1, blocking collectives, body(): product = lax.psum(jnp.sum(residual * shifted), ('gx', 'gy', 'gz'))  43.6 us
    ppermute x12, starting transfers between devices, padded_2(): lax.ppermute(tail, axis, [(i, (i + 1) % count) for i in range(ends)])  41.8 us
    psum x1, blocking collectives, body(): totals = lax.psum(onehot, ('gx', 'gy', 'gz'))  41.5 us
    ppermute x12, starting transfers between devices, padded_2(): lax.ppermute(head, axis, [((i + 1) % count, i) for i in range(ends)])  15.7 us
    slice x12, local copies, waits for them, and re-layouts, padded_2(): lax.slice_in_dim(cells, cells.shape[dim] - width, cells.shape[dim], axis=...  14.8 us
    reduce_sum x1, other arithmetic, body(): curvature = lax.psum(jnp.sum(shifted * applied), ('gx', 'gy', 'gz'))  12.5 us
    ppermute x4, local copies, waits for them, and re-layouts, padded_2(): lax.ppermute(head, axis, [((i + 1) % count, i) for i in range(ends)])  10.3 us
    ppermute x12, waiting for transfers between devices, padded_2(): lax.ppermute(head, axis, [((i + 1) % count, i) for i in range(ends)])  10.2 us
  transfers between devices with their start and end apart: 24, of which 4 were waited for; matrix products, arithmetic and copies ran while one was open for 24% of the time, Pallas kernels for 0%

commit v1 on v0

v1 whole, which is shorter than its diff:
```python
import functools

import jax
import jax.numpy as jnp
from jax import lax
from jax.experimental import pallas as pl
from jax.experimental.pallas import tpu as pltpu
from jax.sharding import PartitionSpec as P

SZ = 64
OV = 4
RIM = OV + 1
LANES = 128
SLOT = 8
GROUP = LANES // SLOT
F32 = jnp.float32
BF16 = jnp.bfloat16
MESH_AXES = ("gx", "gy", "gz")

VMEM = pl.BlockSpec(memory_space=pltpu.VMEM)
SMEM = pl.BlockSpec(memory_space=pltpu.SMEM)
ANY = pl.BlockSpec(memory_space=pl.ANY)


def call(kernel, name, outs, args, spaces, scratch=(), limit=8, out_specs=None, aliases=None, flops=0):
    size = sum(o.size * o.dtype.itemsize for o in outs) + sum(a.size * a.dtype.itemsize for a in args)
    return pl.pallas_call(
        kernel,
        out_shape=outs,
        in_specs=spaces,
        out_specs=out_specs or [VMEM] * len(outs),
        scratch_shapes=list(scratch),
        input_output_aliases=aliases or {},
        name=name,
        compiler_params=pltpu.CompilerParams(vmem_limit_bytes=limit * 2**20),
        cost_estimate=pl.CostEstimate(flops=flops, bytes_accessed=size, transcendentals=0),
    )(*args)


def shape(dims, dtype=F32):
    return jax.ShapeDtypeStruct(tuple(dims), dtype)


def halves(value):
    high = value.astype(BF16)
    return high, (value - high.astype(F32)).astype(BF16)


def dot(left, right):
    return jnp.dot(left, right, preferred_element_type=F32)


def iota(dims, axis):
    return lax.broadcasted_iota(jnp.int32, dims, axis)


def one_hot(condition):
    return jnp.where(condition, 1.0, 0.0).astype(BF16)


IX, IY, IZ, SIDE = 0, 1, 2, 3


def place_vector(sizes):
    ix, iy, iz = (lax.axis_index(a) for a in MESH_AXES)
    nz = sizes["gz"]
    if nz == 2:
        sides = [jnp.where(iz == 0, 1, 0), jnp.ones((), jnp.int32)]
    else:
        sides = [jnp.ones((), jnp.int32), jnp.where(iz < nz - 1, 1, 0), jnp.zeros((), jnp.int32), jnp.where(iz > 0, 1, 0)]
    return jnp.stack([ix, iy, iz] + sides).astype(jnp.int32)


def swap_sides(messages, sizes):
    count = sizes["gz"]
    if count == 2:
        return [lax.ppermute(messages[0], "gz", [(0, 1), (1, 0)])]
    up = [(i, (i + 1) % count) for i in range(count)]
    down = [((i + 1) % count, i) for i in range(count)]
    return [lax.ppermute(messages[1], "gz", down), lax.ppermute(messages[0], "gz", up)]


def swap_ends(low, high, axis, sizes):
    count = sizes[axis]
    up = [(i, (i + 1) % count) for i in range(count)]
    down = [((i + 1) % count, i) for i in range(count)]
    return lax.ppermute(high, axis, up), lax.ppermute(low, axis, down)


def prepare_kernel(sides, place, axes, xv, yv, zv, y_row, z_row, fx, bx, fy, by, wz, bz, den, pad, wide, rows):
    ez = zv.shape[0]
    depth = wz.shape[0] // 4

    def stacked(value, out):
        high, low = halves(value[: LANES // 2])
        high, low = high.astype(F32), low.astype(F32)
        half = jnp.where(iota(high.shape, 1) < LANES // 2, high, pltpu.roll(high, LANES // 2, 1))
        out[0 : LANES // 2] = half.astype(BF16)
        out[LANES // 2 :] = low.astype(BF16)

    for vectors, forward, back in ((xv, fx, bx), (yv, fy, by)):
        pad[...] = jnp.zeros_like(pad)
        pad[0 : vectors.shape[0], 0 : vectors.shape[1]] = vectors[...]
        stacked(pad[...], back)
        stacked(pad[...].T, forward)

    wide[...] = jnp.zeros_like(wide)
    wide[0:ez, 0:ez] = zv[...]
    wide[SZ : SZ + ez, LANES : LANES + ez] = zv[...]
    middle = wide[OV : OV + depth]
    high, low = halves(middle)
    wz[0:depth] = high
    wz[depth : 2 * depth] = high
    wz[2 * depth : 3 * depth] = low
    rows[...] = jnp.zeros_like(rows)
    for side in range(sides):
        is_high = place[SIDE + 2 * side] > 0
        for k in range(OV):
            top, bottom = OV + depth + k, OV - 1 - k
            row = jnp.where(is_high, wide[top : top + 1], wide[bottom : bottom + 1])
            row_high, row_low = halves(row)
            at = 3 * SLOT * side + k
            rows[at : at + 1] = row_high.astype(F32)
            rows[at + SLOT : at + SLOT + 1] = row_high.astype(F32)
            rows[at + 2 * SLOT : at + 2 * SLOT + 1] = row_low.astype(F32)
    wz[3 * depth :] = rows[...].astype(BF16)

    rows[...] = jnp.zeros_like(rows)
    for side in range(sides):
        is_high = place[SIDE + 2 * side] > 0
        for k in range(RIM):
            top, bottom = OV + depth - 1 + k, OV - k
            rows[SLOT * side + k : SLOT * side + k + 1] = jnp.where(is_high, wide[top : top + 1], wide[bottom : bottom + 1])
    across = 2 * LANES
    for at, part in ((0, middle), (LANES, rows[...])):
        turned = jnp.concatenate([part[:, 0:LANES].T, part[:, LANES:].T], axis=0)
        high, low = halves(turned)
        bz[0:across, at : at + LANES] = high
        bz[across : 2 * across, at : at + LANES] = high
        bz[2 * across :, at : at + LANES] = low

    ey = yv.shape[0]
    diagonal = iota((ey, ey), 0) == iota((ey, ey), 1)
    y_column = jnp.sum(jnp.where(diagonal, y_row[...], 0.0), axis=1, keepdims=True)
    pad[...] = jnp.ones_like(pad)
    pad[0:1, 0:ez] = axes[2] * z_row[...]
    den[...] = axes[1] * y_column + pad[0:1]


def pack_x_kernel(right, scale, low, high):
    ext_x, ext_y, depth = right.shape
    for out, start, face in ((low, 0, 0), (high, ext_x - OV, ext_x - 1)):
        for t in range(OV):
            out[t * ext_y : (t + 1) * ext_y] = right[start + t]
        out[OV * ext_y :] = scale[face].astype(F32)


def pack_y_kernel(place, sizes, right, scale, x_low, x_high, low, high):
    ext_x, ext_y, depth = right.shape
    from_low = place[IX] > 0
    from_high = place[IX] < sizes["gx"] - 1
    for a in range(ext_x + 2 * OV):
        for out, start in ((low, 0), (high, ext_y - OV)):
            if a < OV:
                rows = jnp.where(from_low, x_low[a * ext_y + start : a * ext_y + start + OV], 0.0)
            elif a < ext_x + OV:
                rows = right[a - OV, start : start + OV]
            else:
                at = (a - OV - ext_x) * ext_y + start
                rows = jnp.where(from_high, x_high[at : at + OV], 0.0)
            out[a * OV : (a + 1) * OV] = rows
    base = (ext_x + 2 * OV) * OV
    for x in range(ext_x):
        low[base + x : base + x + 1] = scale[x, 0:16].astype(F32)[0:1]
        high[base + x : base + x + 1] = scale[x, ext_y - 16 : ext_y].astype(F32)[15:16]


def extend_kernel(sizes, sides, place, right, scale, x_low, x_high, y_low, y_high, ext, *messages):
    ext_x, ext_y, depth = right.shape
    wide_x, wide_y = ext_x + 2 * OV, ext_y + 2 * OV
    x_from_low, x_from_high = place[IX] > 0, place[IX] < sizes["gx"] - 1
    y_from_low, y_from_high = place[IY] > 0, place[IY] < sizes["gy"] - 1
    for a in range(wide_x):
        if a < OV:
            core = jnp.where(x_from_low, x_low[a * ext_y : (a + 1) * ext_y], 0.0)
        elif a < ext_x + OV:
            core = right[a - OV]
        else:
            at = (a - OV - ext_x) * ext_y
            core = jnp.where(x_from_high, x_high[at : at + ext_y], 0.0)
        ext[a * wide_y + OV : a * wide_y + OV + ext_y] = core
        ext[a * wide_y : a * wide_y + OV] = jnp.where(y_from_low, y_low[a * OV : (a + 1) * OV], 0.0)
        ext[a * wide_y + OV + ext_y : (a + 1) * wide_y] = jnp.where(y_from_high, y_high[a * OV : (a + 1) * OV], 0.0)
    lane = iota((depth, LANES), 1)
    cell = iota((depth, LANES), 0)
    slot = lax.rem(lane, SLOT)
    for side in range(sides):
        is_high = place[SIDE + 2 * side] > 0
        target = jnp.where(is_high, depth - 1 - slot, slot)
        face = jnp.where(is_high, depth - 1, 0)
        picks = jnp.where((target == cell) & (slot < OV), 1.0, 0.0)
        face_picks = jnp.where((cell == face) & (slot == OV), 1.0, 0.0)
        for group in range((wide_x + GROUP - 1) // GROUP):
            total = jnp.zeros((wide_y, LANES), F32)
            total_face = jnp.zeros((ext_y, LANES), F32)
            for q in range(GROUP):
                a = group * GROUP + q
                mine = lane // SLOT == q
                if a < wide_x:
                    high, low = halves(ext[a * wide_y : (a + 1) * wide_y])
                    pick = jnp.where(mine, picks, 0.0).astype(BF16)
                    total = total + dot(jnp.concatenate([high, low], axis=1), jnp.concatenate([pick, pick], axis=0))
                if a < ext_x:
                    total_face = total_face + dot(scale[a], jnp.where(mine, face_picks, 0.0).astype(BF16))
            messages[side][group * wide_y : (group + 1) * wide_y] = total
            messages[side][group * wide_y : group * wide_y + ext_y] += total_face


def solve_kernel(sides, place, axes, x_values, ext, *refs):
    received, refs = refs[:sides], refs[sides:]
    fx, bx, fy, by, wz, bz, den, local = refs[:8]
    messages, refs = refs[8 : 8 + sides], refs[8 + sides :]
    first_a, first_b, second_a, second_b = refs
    wide = x_values.shape[0]
    rows = ext.shape[0]
    wide_y = rows // wide
    batch = 8
    lane = iota((wide_y, LANES), 1)

    def along(matrix, pair):
        value = jnp.concatenate(pair, axis=1)
        fill = jnp.zeros((LANES // 2 - value.shape[0], value.shape[1]), F32)
        high, low = halves(jnp.concatenate([value, fill], axis=0))
        out = dot(matrix[...], jnp.concatenate([high, low], axis=0))
        return out[0 : value.shape[0]] + out[LANES // 2 : LANES // 2 + value.shape[0]]

    for start in range(0, wide, batch):
        block = pl.ds(start * wide_y, batch * wide_y)
        high, low = halves(ext[block])
        rims = []
        for a in range(start, start + batch):
            group, q = a // GROUP, a % GROUP
            piece = jnp.zeros((wide_y, LANES), F32)
            for side in range(sides):
                value = received[side][group * wide_y : (group + 1) * wide_y]
                value = jnp.where((lane // SLOT == q) & (place[SIDE + 2 * side + 1] > 0), value, 0.0)
                value_high, value_low = halves(value)
                value_high, value_low = value_high.astype(F32), value_low.astype(F32)
                at = LANES - SLOT * q + 3 * SLOT * side
                piece = piece + pltpu.roll(value_high, at % LANES, 1)
                piece = piece + pltpu.roll(value_low, (at + SLOT) % LANES, 1)
                piece = piece + pltpu.roll(value_high, (at + 2 * SLOT) % LANES, 1)
            rims.append(piece.astype(BF16))
        left = jnp.concatenate([high, low, high, jnp.concatenate(rims, axis=0)], axis=1)
        out = dot(left, wz[...])
        first_a[block] = out[:, 0:LANES]
        first_b[block] = out[:, LANES:]

    def strided(refs_pair, at, count, stride):
        return [ref[pl.ds(at, count, stride=stride), :] for ref in refs_pair]

    def x_forward(y):
        out = along(fx, strided((first_a, first_b), y, wide, wide_y))
        second_a[pl.ds(y * wide, wide)] = out[:, 0:LANES]
        second_b[pl.ds(y * wide, wide)] = out[:, LANES:]

    def y_both(i):
        out = along(fy, strided((second_a, second_b), i, wide_y, wide))
        inverse = 1.0 / (axes[0] * x_values[i] + den[...])
        out = along(by, [out[:, 0:LANES] * inverse, out[:, LANES:] * inverse])
        first_a[pl.ds(i * wide_y, wide_y)] = out[:, 0:LANES]
        first_b[pl.ds(i * wide_y, wide_y)] = out[:, LANES:]

    def x_back(y):
        out = along(bx, strided((first_a, first_b), y, wide, wide_y))
        second_a[pl.ds(y, wide, stride=wide_y), :] = out[:, 0:LANES]
        second_b[pl.ds(y, wide, stride=wide_y), :] = out[:, LANES:]

    for step, count in ((x_forward, wide_y), (y_both, wide), (x_back, wide_y)):

        def several(block, carry, step=step):
            for inner in range(8):
                step(block * 8 + inner)
            return carry

        lax.fori_loop(0, count // 8, several, 0)

    totals = [[jnp.zeros((wide_y, LANES), F32) for _ in range((wide + GROUP - 1) // GROUP)] for _ in range(sides)]
    for start in range(0, wide, batch):
        block = pl.ds(start * wide_y, batch * wide_y)
        high_a, low_a = halves(second_a[block])
        high_b, low_b = halves(second_b[block])
        out = dot(jnp.concatenate([high_a, high_b, low_a, low_b, high_a, high_b], axis=1), bz[...])
        local[block] = out[:, 0:LANES]
        for a in range(start, start + batch):
            group, q = a // GROUP, a % GROUP
            value = out[(a - start) * wide_y : (a - start + 1) * wide_y, LANES:]
            for side in range(sides):
                own = value if sides == 1 else jnp.where(lane // SLOT == side, value, 0.0)
                at = (SLOT * q + LANES - SLOT * side) % LANES
                totals[side][group] = totals[side][group] + (pltpu.roll(own, at, 1) if at else own)
    for side in range(sides):
        for group, total in enumerate(totals[side]):
            messages[side][group * wide_y : (group + 1) * wide_y] = total


def fold_z_kernel(sides, wide, place, local, *refs):
    own, received = refs[:sides], refs[sides : 2 * sides]
    out, refs = refs[2 * sides], refs[2 * sides + 1 :]
    faces, (low_end, high_end) = refs[:sides], refs[sides:]
    rows = local.shape[0]
    wide_y = rows // wide
    groups = (wide + GROUP - 1) // GROUP
    lane = iota((LANES, LANES), 0)
    cell = iota((LANES, LANES), 1)
    slot = lax.rem(lane, SLOT)
    wide_lane = iota((groups * wide_y, LANES), 1)
    pairs = []
    for side in range(sides):
        value = jnp.where(place[SIDE + 2 * side + 1] > 0, received[side][...], 0.0)
        both = value + pltpu.roll(own[side][...], LANES - 1, 1)
        inside = (lax.rem(wide_lane, SLOT) == 0) & (place[SIDE + 2 * side + 1] > 0)
        faces[side][...] = jnp.where(inside, both, 0.0)
        high, low = halves(value)
        pairs.append(jnp.concatenate([high, low], axis=1))
    for a in range(wide):
        group, q = a // GROUP, a % GROUP
        value = local[a * wide_y : (a + 1) * wide_y]
        for side in range(sides):
            is_high = place[SIDE + 2 * side] > 0
            target = jnp.where(is_high, LANES - slot, slot - 1)
            put = one_hot((lane // SLOT == q) & (slot >= 1) & (slot <= OV) & (cell == target))
            value = value + dot(pairs[side][group * wide_y : (group + 1) * wide_y], jnp.concatenate([put, put], axis=0))
        out[a * wide_y : (a + 1) * wide_y] = value
    ends = RIM * wide_y
    low_end[0:ends] = out[0:ends]
    high_end[0:ends] = out[rows - ends : rows]
    for side in range(sides):
        low_end[ends + side * wide_y : ends + (side + 1) * wide_y] = faces[side][0:wide_y]
        high_end[ends + side * wide_y : ends + (side + 1) * wide_y] = faces[side][(groups - 1) * wide_y :]


def fold_x_kernel(sizes, sides, wide, place, field, *refs):
    faces, refs = refs[:sides], refs[sides:]
    x_low, x_high, out = refs[:3]
    out_faces, (low_end, high_end) = refs[3 : 3 + sides], refs[3 + sides :]
    rows = field.shape[0]
    wide_y = rows // wide
    groups = (wide + GROUP - 1) // GROUP
    from_low, from_high = place[IX] > 0, place[IX] < sizes["gx"] - 1
    ends = RIM * wide_y
    low_at, high_at = (OV - 1) * wide_y, (wide - 2 * OV) * wide_y
    out[low_at : low_at + ends] = field[low_at : low_at + ends] + jnp.where(from_low, x_low[0:ends], 0.0)
    out[high_at : high_at + ends] = field[high_at : high_at + ends] + jnp.where(from_high, x_high[0:ends], 0.0)
    lane = iota((wide_y, LANES), 1)
    high_lane = (wide - 2 * OV) % GROUP * SLOT
    for side in range(sides):
        out_faces[side][...] = faces[side][...]
        part = slice(ends + side * wide_y, ends + (side + 1) * wide_y)
        inside = (lane >= (OV - 1) * SLOT) & (lane < 2 * OV * SLOT) & from_low
        out_faces[side][0:wide_y] += jnp.where(inside, x_low[part], 0.0)
        inside = (lane >= high_lane) & (lane < high_lane + RIM * SLOT) & from_high
        out_faces[side][(groups - 1) * wide_y :] += jnp.where(inside, x_high[part], 0.0)
    planes = wide - 2 * OV + 2
    for end, start in ((low_end, 0), (high_end, wide_y - RIM)):
        for p in range(planes):
            at = (p + OV - 1) * wide_y + start
            end[p * RIM : (p + 1) * RIM] = out[at : at + RIM]
        for side in range(sides):
            for group in range(groups):
                at = planes * RIM + (side * groups + group) * RIM
                end[at : at + RIM] = out_faces[side][group * wide_y + start : group * wide_y + start + RIM]


def operator_kernel(sizes, sides, wide, place, axes, field, *refs):
    faces, refs = refs[:sides], refs[sides:]
    y_low, y_high, right, scale, sx_low, sx_high, sy_low, sy_high = refs[:8]
    scale_faces, refs = refs[8 : 8 + sides], refs[8 + sides :]
    direction, applied, z_weight, wx, wy, sums, values, scales, edges = refs
    ext_x, ext_y, depth = right.shape
    wide_y = ext_y + 2 * OV
    groups = (wide + GROUP - 1) // GROUP
    planes = ext_x + 2
    core = slice(8, 8 + ext_y)
    inside = [
        (place[IX] > 0, place[IX] < sizes["gx"] - 1),
        (place[IY] > 0, place[IY] < sizes["gy"] - 1),
        (place[IZ] > 0, place[IZ] < sizes["gz"] - 1),
    ]
    for p in range(planes):
        at = (p + OV - 1) * wide_y
        values[p, 7 : 9 + ext_y] = field[at + OV - 1 : at + OV + ext_y + 1]
        values[p, 7 : 7 + RIM] += jnp.where(inside[1][0], y_low[p * RIM : (p + 1) * RIM], 0.0)
        values[p, 4 + ext_y : 4 + ext_y + RIM] += jnp.where(inside[1][1], y_high[p * RIM : (p + 1) * RIM], 0.0)
    for (axis_low, axis_high), low_at, high_at in (
        (inside[0], (0, slice(None)), (planes - 1, slice(None))),
        (inside[1], (slice(None), slice(7, 8)), (slice(None), slice(8 + ext_y, 9 + ext_y))),
    ):
        values[low_at] = jnp.where(axis_low, values[low_at], 0.0)
        values[high_at] = jnp.where(axis_high, values[high_at], 0.0)
    for side in range(sides):
        for group in range(groups):
            at = side * groups * wide_y + group * wide_y
            edges[at : at + wide_y] = faces[side][group * wide_y : (group + 1) * wide_y]
            row = (ext_x + 2) * RIM + (side * groups + group) * RIM
            edges[at + OV - 1 : at + OV - 1 + RIM] += jnp.where(inside[1][0], y_low[row : row + RIM], 0.0)
            edges[at + ext_y : at + ext_y + RIM] += jnp.where(inside[1][1], y_high[row : row + RIM], 0.0)
    x_rows, y_rows = OV * ext_y, wide * OV
    scales[0, core] = jnp.where(inside[0][0], sx_low[x_rows : x_rows + ext_y], 0.0)
    scales[planes - 1, core] = jnp.where(inside[0][1], sx_high[x_rows : x_rows + ext_y], 0.0)
    for x in range(ext_x):
        scales[x + 1, core] = scale[x].astype(F32)
        scales[x + 1, 7:8] = jnp.where(inside[1][0], sy_low[y_rows + x : y_rows + x + 1], 0.0)
        scales[x + 1, 8 + ext_y : 9 + ext_y] = jnp.where(inside[1][1], sy_high[y_rows + x : y_rows + x + 1], 0.0)

    hx, hy, hz = (0.5 * axes[d] for d in range(3))
    lane = iota((ext_y, depth), 1)
    row_lane = iota((LANES, depth), 0)
    row_cell = iota((LANES, depth), 1)
    zero = jnp.zeros((ext_y, depth), F32)
    sum_right, sum_product, sum_energy, sum_applied, sum_z = zero, zero, zero, zero, zero
    wx[0] = hx * (scales[1, core] + scales[0, core])
    wx[1] = hx * (scales[planes - 2, core] + scales[planes - 1, core])
    x_flux = wx[0] * (values[1, core] - values[0, core])
    for x in range(ext_x):
        mid, own = values[x + 1, core], scales[x + 1, core]
        next_flux = hx * (scales[x + 2, core] + own) * (values[x + 2, core] - mid)
        total = x_flux - next_flux
        x_flux = next_flux
        below, above = slice(7, 7 + ext_y), slice(9, 9 + ext_y)
        weight_below = hy * (own + scales[x + 1, below])
        weight_above = hy * (own + scales[x + 1, above])
        total = total + weight_below * (mid - values[x + 1, below]) + weight_above * (mid - values[x + 1, above])
        wy[0, x : x + 1] = weight_below[0:1]
        wy[1, x : x + 1] = weight_above[ext_y - 1 : ext_y]
        edge_value, edge_scale = zero, zero
        for side in range(sides):
            is_high, valid = place[SIDE + 2 * side] > 0, place[SIDE + 2 * side + 1] > 0
            target = jnp.where(is_high, depth - 1, 0)
            a = x + OV
            at = (side * groups + a // GROUP) * wide_y + OV
            high, low = halves(edges[at : at + ext_y])
            put = one_hot((row_lane == a % GROUP * SLOT) & (row_cell == target))
            edge_value = edge_value + dot(jnp.concatenate([high, low], axis=1), jnp.concatenate([put, put], axis=0))
            at = x // GROUP * wide_y
            face = jnp.where(valid, scale_faces[side][at : at + ext_y], 0.0).astype(BF16)
            put = one_hot((row_lane == x % GROUP * SLOT + OV) & (row_cell == target))
            edge_scale = edge_scale + dot(face, put)
        lower = jnp.where(lane == 0, edge_value, pltpu.roll(mid, 1, 1))
        lower_scale = jnp.where(lane == 0, edge_scale, pltpu.roll(own, 1, 1))
        flux = hz * (own + lower_scale) * (mid - lower)
        ends = (lane == 0) | (lane == depth - 1)
        end_weight = jnp.where(ends, hz * (own + edge_scale), 0.0)
        upper = jnp.where(lane == depth - 1, end_weight * (mid - edge_value), -pltpu.roll(flux, depth - 1, 1))
        total = total + flux + upper
        here = right[x]
        direction[x] = mid
        applied[x] = total
        z_weight[x] = end_weight
        sum_right = sum_right + here
        sum_product = sum_product + here * mid
        sum_energy = sum_energy + mid * total
        sum_applied = sum_applied + total
        sum_z = sum_z + end_weight

    def whole(value):
        return jnp.sum(jnp.sum(value, axis=0, keepdims=True), axis=1, keepdims=True)

    x_high_sum, y_high_sum = whole(wx[1]), whole(wy[1])
    z_high_sum = whole(jnp.where(lane == depth - 1, sum_z, 0.0))
    faces_sum = whole(wx[0]) + x_high_sum + whole(wy[0]) + y_high_sum + whole(sum_z)
    columns = [
        whole(sum_right),
        whole(sum_product),
        whole(sum_energy),
        whole(sum_applied),
        faces_sum,
        jnp.where(inside[0][1], x_high_sum, 0.0),
        jnp.where(inside[1][1], y_high_sum, 0.0),
        jnp.where(inside[2][1], z_high_sum, 0.0),
    ]
    at = iota((1, LANES), 1)
    row = jnp.zeros((1, LANES), F32)
    for number, value in enumerate(columns):
        row = jnp.where(at == number, value, row)
    sums[...] = jnp.broadcast_to(row, sums.shape)


def finish_kernel(sizes, place, sums, inverse, direction, applied, z_weight, wx, wy, right, solution, residual, held_s, held_r, sems):
    ext_x, ext_y, depth = right.shape
    nx, ny, nz = (sizes[a] for a in MESH_AXES)
    count, blocks = nx * ny * nz, nx * ny * nz // 2
    table = sums[...]
    part = [table[:, k : k + 1] for k in range(8)]
    member = iota((count, blocks), 0) // 2 == iota((count, blocks), 1)
    means = jnp.sum(jnp.where(member, part[0], 0.0), axis=0, keepdims=True) / (2.0 * ext_x * ext_y * depth)
    coarse = jnp.sum(inverse[...] * means, axis=1, keepdims=True)
    diagonal = iota((blocks, blocks), 0) == iota((blocks, blocks), 1)
    coarse_row = jnp.sum(jnp.where(diagonal, coarse, 0.0), axis=0, keepdims=True)
    level = jnp.sum(jnp.where(member, coarse_row, 0.0), axis=1, keepdims=True)

    def shifted(by):
        return jnp.concatenate([level[by:], level[:by]], axis=0)

    def whole(value):
        return jnp.sum(value, axis=0, keepdims=True)

    product = whole(part[1] + level * part[0])
    neighbours = part[5] * shifted(ny * nz) + part[6] * shifted(nz) + part[7] * shifted(1)
    curvature = whole(part[2] + 2.0 * level * part[3] + level * (level * part[4] - 2.0 * neighbours))
    step = product / curvature
    device = iota((count, 1), 0)
    mine = (place[IX] * ny + place[IY]) * nz + place[IZ]

    def level_at(number, inside):
        return whole(jnp.where((device == number) & inside, level, 0.0))

    own = level_at(mine, True)
    drops = []
    for axis, stride, size in ((IX, ny * nz, nx), (IY, nz, ny), (IZ, 1, nz)):
        drops.append(step * (own - level_at(mine - stride, place[axis] > 0)))
        drops.append(step * (own - level_at(mine + stride, place[axis] < size - 1)))
    z_drop = jnp.where(iota((1, depth), 1) < depth // 2, drops[4], drops[5])
    chunk = 12
    for x in range(ext_x):
        held_s[x] = step * (direction[x] + own)
        value = right[x] - step * applied[x] - z_drop * z_weight[x]
        if x == 0:
            value = value - drops[0] * wx[0]
        if x == ext_x - 1:
            value = value - drops[1] * wx[1]
        held_r[x] = value
        held_r[x, 0:1] = value[0:1] - drops[2] * wy[0, x : x + 1]
        held_r[x, ext_y - 1 : ext_y] = value[ext_y - 1 : ext_y] - drops[3] * wy[1, x : x + 1]
        if (x + 1) % chunk == 0:
            part_x = pl.ds(x + 1 - chunk, chunk)
            number = (x + 1) // chunk - 1
            pltpu.make_async_copy(held_s.at[part_x], solution.at[part_x], sems.at[0, number]).start()
            pltpu.make_async_copy(held_r.at[part_x], residual.at[part_x], sems.at[1, number]).start()
    for number in range(ext_x // chunk):
        part_x = pl.ds(number * chunk, chunk)
        pltpu.make_async_copy(held_s.at[part_x], solution.at[part_x], sems.at[0, number]).wait()
        pltpu.make_async_copy(held_r.at[part_x], residual.at[part_x], sems.at[1, number]).wait()


def body(sizes, right, scale, axes, xv, yv, zv, x_values, y_values, z_values, inverse):
    ext_x, ext_y, depth = right.shape
    wide_x, wide_y, ez = xv.shape[0], yv.shape[0], zv.shape[0]
    sides = 1 if sizes["gz"] == 2 else 2
    groups = (wide_x + GROUP - 1) // GROUP
    count = sizes["gx"] * sizes["gy"] * sizes["gz"]
    place = place_vector(sizes)
    bind = functools.partial

    x_message = shape([RIM * ext_y, depth])
    low, high = call(pack_x_kernel, "pack_x", [x_message] * 2, [right, scale], [VMEM] * 2)
    x_low, x_high = swap_ends(low, high, "gx", sizes)

    square = shape([LANES, LANES], BF16)
    mats = call(
        bind(prepare_kernel, sides),
        "prepare",
        [square] * 4 + [shape([4 * depth, 2 * LANES], BF16), shape([6 * LANES, 2 * LANES], BF16), shape([wide_y, LANES])],
        [place, axes, xv, yv, zv, y_values.reshape(1, -1), z_values.reshape(1, -1)],
        [SMEM] * 2 + [VMEM] * 5,
        [pltpu.VMEM((LANES, LANES), F32), pltpu.VMEM((depth + 2 * OV, 2 * LANES), F32), pltpu.VMEM((LANES, 2 * LANES), F32)],
    )

    y_message = shape([wide_x * OV + ext_x, depth])
    low, high = call(
        lambda place, *refs: pack_y_kernel(place, sizes, *refs),
        "pack_y",
        [y_message] * 2,
        [place, right, scale, x_low, x_high],
        [SMEM] + [VMEM] * 4,
    )
    y_low, y_high = swap_ends(low, high, "gy", sizes)

    rim_message = shape([groups * wide_y, LANES])
    field = shape([wide_x * wide_y, depth])
    ext, *rims = call(
        bind(extend_kernel, sizes, sides),
        "extend",
        [field] + [rim_message] * sides,
        [place, right, scale, x_low, x_high, y_low, y_high],
        [SMEM] + [VMEM] * 6,
    )
    rims = swap_sides(rims, sizes)

    tall = pltpu.VMEM((wide_x * wide_y, LANES), F32)
    local, *own_rims = call(
        bind(solve_kernel, sides),
        "solve",
        [field] + [rim_message] * sides,
        [place, axes, x_values, ext, *rims, *mats],
        [SMEM] * 3 + [VMEM] * (1 + sides + len(mats)),
        [tall] * 4,
        limit=20,
    )
    other_rims = swap_sides(own_rims, sizes)

    x_message = shape([(RIM + sides) * wide_y, depth])
    field_z, *refs = call(
        bind(fold_z_kernel, sides, wide_x),
        "fold_z",
        [field] + [rim_message] * sides + [x_message] * 2,
        [place, local, *own_rims, *other_rims],
        [SMEM] + [VMEM] * (1 + 2 * sides),
    )
    faces, (low, high) = refs[:sides], refs[sides:]
    xs_low, xs_high = swap_ends(low, high, "gx", sizes)

    y_message = shape([(ext_x + 2 + groups * sides) * RIM, depth])
    field_x, *refs = call(
        bind(fold_x_kernel, sizes, sides, wide_x),
        "fold_x",
        [field] + [rim_message] * sides + [y_message] * 2,
        [place, field_z, *faces, xs_low, xs_high],
        [SMEM] + [VMEM] * (3 + sides),
        aliases={1: 0},
    )
    faces, (low, high) = refs[:sides], refs[sides:]
    ys_low, ys_high = swap_ends(low, high, "gy", sizes)

    block = shape(right.shape)
    padded = pltpu.VMEM((ext_x + 2, ext_y + 16, depth), F32)
    direction, applied, z_weight, wx, wy, sums = call(
        bind(operator_kernel, sizes, sides, wide_x),
        "operator",
        [block] * 3 + [shape([2, ext_y, depth]), shape([2, ext_x, depth]), shape([count, LANES])],
        [place, axes, field_x, *faces, ys_low, ys_high, right, scale, x_low, x_high, y_low, y_high, *rims],
        [SMEM] * 2 + [VMEM] * (9 + 2 * sides),
        [padded, padded, pltpu.VMEM((sides * groups * wide_y, LANES), F32)],
        limit=12,
    )
    sums = lax.all_to_all(sums, MESH_AXES, 0, 0, tiled=True)

    held = pltpu.VMEM(right.shape, F32)
    return tuple(
        call(
            bind(finish_kernel, sizes),
            "finish",
            [block] * 2,
            [place, sums, inverse, direction, applied, z_weight, wx, wy, right],
            [SMEM] + [VMEM] * 8,
            [held, held, pltpu.SemaphoreType.DMA((2, ext_x // 12))],
            out_specs=[ANY] * 2,
        )
    )


def solution(mesh):
    sizes = dict(mesh.shape)
    in_specs = (P(*MESH_AXES), P(*MESH_AXES), P(), P(), P(), P(), P(), P(), P(), P())
    out_specs = (P(*MESH_AXES), P(*MESH_AXES))
    return jax.shard_map(functools.partial(body, sizes), mesh=mesh, in_specs=in_specs, out_specs=out_specs, check_vma=False)
```

time: 283 us -> 78.3 us (0.28); the launches traced: 278 us -> 78.1 us
  blocking collectives: 85 us -> 10.9 us
  local copies, waits for them, and re-layouts: 56.6 us -> 2.46 us
  starting transfers between devices: 57.5 us -> 15.3 us
  other arithmetic: 39.5 us -> 0 us
  matrix products: 23.7 us -> 0 us
  Pallas kernels: 0 us -> 22.9 us
  waiting for transfers between devices: 10.2 us -> 25.8 us
  between operations: 5.04 us -> 0.8 us
    psum x2 -> x0, blocking collectives: 85 us -> none  [the longest x1 43.6 us: body(): product = lax.psum(jnp.sum(residual * shifted), ('gx', 'gy', 'gz'))]
    ppermute x24 -> x10, starting transfers between devices: 57.5 us -> 15.3 us  [the longest x8 15 us: swap_ends(): return (lax.ppermute(high, axis, up), lax.ppermute(low, axis, down))]
    dot_general x7 -> x0, matrix products: 23.7 us -> none  [the longest x1 5.68 us: local_part(): first = jnp.einsum('abc,ai->ibc', extended, x_vectors, precision=exact_mode)]
    pallas_call x0 -> x9, Pallas kernels: none -> 22.9 us  [call(): pl.pallas_call(kernel, out_shape=outs, in_specs=spaces, out_specs=out_spe...]
    slice x19 -> x0, local copies, waits for them, and re-layouts: 22.1 us -> none  [the longest x12 14.8 us: padded_2(): lax.slice_in_dim(cells, cells.shape[dim] - width, cells.shape[dim], axis=...]
    ppermute x8 -> x0, local copies, waits for them, and re-layouts: 19.6 us -> none  [the longest x4 10.3 us: padded_2(): lax.ppermute(head, axis, [((i + 1) % count, i) for i in range(ends)])]
    ppermute x24 -> x10, waiting for transfers between devices: 10.2 us -> 25.8 us  [the longest x8 24.2 us: swap_ends(): return (lax.ppermute(high, axis, up), lax.ppermute(low, axis, down))]
    reduce_sum x2 -> x0, other arithmetic: 14.7 us -> none  [the longest x1 12.5 us: body(): curvature = lax.psum(jnp.sum(shifted * applied), ('gx', 'gy', 'gz'))]
  transfers between devices with their start and end apart: 24 -> 10, of which waited for: 4 -> 10; matrix products, arithmetic and copies ran while one was open for 24% -> 0% of each run, Pallas kernels for 0% -> 1%
where the time goes in v1:
time: 78.3 us; the launch traced here: 78.1 us
  waiting for transfers between devices  25.8 us (33%)
  Pallas kernels  22.9 us (29%)
  starting transfers between devices  15.3 us (20%)
  blocking collectives  10.9 us (14%)
  local copies, waits for them, and re-layouts  2.46 us (3%)
  between operations  0.8 us (1%)
    ppermute x8, waiting for transfers between devices, swap_ends(): return (lax.ppermute(high, axis, up), lax.ppermute(low, axis, down))  24.2 us
    pallas_call x9, Pallas kernels, call(): pl.pallas_call(kernel, out_shape=outs, in_specs=spaces, out_specs=out_spe...  22.9 us
    ppermute x8, starting transfers between devices, swap_ends(): return (lax.ppermute(high, axis, up), lax.ppermute(low, axis, down))  15 us
    all_to_all x1, blocking collectives, body(): sums = lax.all_to_all(sums, MESH_AXES, 0, 0, tiled=True)  10.9 us
    unnamed x24, local copies, waits for them, and re-layouts  2.38 us
  transfers between devices with their start and end apart: 10, of which 10 were waited for; matrix products, arithmetic and copies ran while one was open for 0% of the time, Pallas kernels for 1%

profile of v1, /device:TPU:0, one launch (start us, length us, event | category | flops | bytes accessed | tf_op | source)
XLA Modules:
  0.0 78.1 jit_solution(7782114171852785166)
XLA Ops:
  0.6 1.3 %copy-done = f32[48,48,128]{2,1,0:T(8,128)S(1)} copy-done((f32[48,48,128]{2,1,0:T(8,128)S(1)}, f32[48,48,128]{2,1,0:T(8,128)}, u32[]{:S(2)}) %copy-start) | copy-done | bytes 1179672
  1.9 1.1 %copy-done.2 = bf16[48,48,128]{2,1,0:T(8,128)(2,1)S(1)} copy-done((bf16[48,48,128]{2,1,0:T(8,128)(2,1)S(1)}, bf16[48,48,128]{2,1,0:T(8,128)(2,1)}, u32[]{:S(2)}) %copy-start.2) | copy-done | bytes 589848
  3.0 3.1 %collective-permute-start = (f32[240,128]{1,0:T(8,128)S(1)}, f32[240,128]{1,0:T(8,128)S(1)}, u32[]{:S(2)}, u32[]{:S(2)}) collective-permute-start(f32[240,128]{1,0:T(8,128)S(1)} %get-tuple-element.31), channel_id=1, source_target_pairs={{0,8},{8,16},{16,24},{24,0},{1,9},{9,17},{17,25},{25,1},{2,10},{10... | collective-permute-start | bytes 368648 | tf_op jit(solution)/shard_map/ppermute | solution.py:87
  6.1 2.1 %collective-permute-start.1 = (f32[240,128]{1,0:T(8,128)S(1)}, f32[240,128]{1,0:T(8,128)S(1)}, u32[]{:S(2)}, u32[]{:S(2)}) collective-permute-start(f32[240,128]{1,0:T(8,128)S(1)} %get-tuple-element.32), channel_id=1, source_target_pairs={{8,0},{16,8},{24,16},{0,24},{9,1},{17,9},{25,17},{1,25},{10,2},{18... | collective-permute-start | bytes 368648 | tf_op jit(solution)/shard_map/ppermute | solution.py:87
  8.2 0.1 stack.19.place
  8.2 4.0 %collective-permute-done.refs_2_.x_low.refs_5_ = f32[240,128]{1,0:T(8,128)S(1)} collective-permute-done((f32[240,128]{1,0:T(8,128)S(1)}, f32[240,128]{1,0:T(8,128)S(1)}, u32[]{:S(2)}, u32[]{:S(2)}) %collective-permute-start) | collective-permute-done | bytes 122912 | tf_op jit(solution)/shard_map/ppermute | solution.py:87
  12.2 1.2 %collective-permute-done.1.refs_3_.x_high.refs_6_ = f32[240,128]{1,0:T(8,128)S(1)} collective-permute-done((f32[240,128]{1,0:T(8,128)S(1)}, f32[240,128]{1,0:T(8,128)S(1)}, u32[]{:S(2)}, u32[]{:S(2)}) %collective-permute-start.1) | collective-permute-done | bytes 122912 | tf_op jit(solution)/shard_map/ppermute | solution.py:87
  13.5 0.6 pack_y.1
  14.2 1.5 %collective-permute-start.2 = (f32[272,128]{1,0:T(8,128)S(1)}, f32[272,128]{1,0:T(8,128)S(1)}, u32[]{:S(2)}, u32[]{:S(2)}) collective-permute-start(f32[272,128]{1,0:T(8,128)S(1)} %get-tuple-element.33), channel_id=1, source_target_pairs={{0,2},{2,4},{4,6},{6,0},{1,3},{3,5},{5,7},{7,1},{8,10},{10,12},{12... | collective-permute-start | bytes 417800 | tf_op jit(solution)/shard_map/ppermute | solution.py:87
  15.7 1.4 %collective-permute-start.3 = (f32[272,128]{1,0:T(8,128)S(1)}, f32[272,128]{1,0:T(8,128)S(1)}, u32[]{:S(2)}, u32[]{:S(2)}) collective-permute-start(f32[272,128]{1,0:T(8,128)S(1)} %get-tuple-element.34), channel_id=1, source_target_pairs={{2,0},{4,2},{6,4},{0,6},{3,1},{5,3},{7,5},{1,7},{10,8},{12,10},{14... | collective-permute-start | bytes 417800 | tf_op jit(solution)/shard_map/ppermute | solution.py:87
  17.2 4.4 %collective-permute-done.2.y_low.refs_7_ = f32[272,128]{1,0:T(8,128)S(1)} collective-permute-done((f32[272,128]{1,0:T(8,128)S(1)}, f32[272,128]{1,0:T(8,128)S(1)}, u32[]{:S(2)}, u32[]{:S(2)}) %collective-permute-start.2) | collective-permute-done | bytes 139296 | tf_op jit(solution)/shard_map/ppermute | solution.py:87
  21.6 1.5 %collective-permute-done.3.y_high.refs_8_ = f32[272,128]{1,0:T(8,128)S(1)} collective-permute-done((f32[272,128]{1,0:T(8,128)S(1)}, f32[272,128]{1,0:T(8,128)S(1)}, u32[]{:S(2)}, u32[]{:S(2)}) %collective-permute-start.3) | collective-permute-done | bytes 139296 | tf_op jit(solution)/shard_map/ppermute | solution.py:87
  23.1 1.6 %extend.1 = (f32[3136,128]{1,0:T(8,128)S(1)}, f32[224,128]{1,0:T(8,128)S(1)}) custom-call(s32[5]{0:T(128)S(1)} %stack.19.place, f32[48,48,128]{2,1,0:T(8,128)S(1)} %copy-done.1, bf16[48,48,128]{2,1,0:T(8,128)(2,1)S(1)} %copy-done.3, f32[240,128]{1,0:T(8,128)S(1)} %collective-permute-done.refs_2_.x_low.refs_5_, ...), custom_call_target="tpu_custom_call" | custom-call | bytes 4014100 | tf_op jit(solution)/shard_map/extend/pallas_call | solution.py:27
  24.7 0.1 collective-permute-start.4
  24.9 0.8 %prepare.1 = (bf16[128,128]{1,0:T(8,128)(2,1)S(1)}, bf16[128,128]{1,0:T(8,128)(2,1)S(1)}, bf16[128,128]{1,0:T(8,128)(2,1)S(1)}, bf16[128,128]{1,0:T(8,128)(2,1)S...) custom-call(s32[5]{0:T(128)S(1)} %stack.19.place, f32[3]{0:T(128)S(1)} %copy-done.8, ...), custom_call_target="tpu_custom_call" | custom-call | bytes 861472 | tf_op jit(solution)/shard_map/prepare/pallas_call | solution.py:27
  25.7 0.4 collective-permute-done.4.refs_0_.refs_9_
  26.1 11.4 %solve.1 = (f32[3136,128]{1,0:T(8,128)S(1)}, f32[224,128]{1,0:T(8,128)S(1)}) custom-call(s32[5]{0:T(128)S(1)} %stack.19.place, f32[3]{0:T(128)S(1)} %copy-done.8, f32[56]{0:T(128)S(1)} %copy-done.11, f32[3136,128]{1,0:T(8,128)S(1)} %get-tuple-element.35.ext, f32[224,128]{1,0:T(8,128)S(1)} %collective-permute-done.4.refs_0_.refs_9_, ...), custom_call_target="tpu_custom_call" | custom-call | bytes 4256000 | tf_op jit(solution)/shard_map/solve/pallas_call | solution.py:27
  37.6 0.2 collective-permute-start.5
  37.8 1.2 %collective-permute-done.5.refs_1_ = f32[224,128]{1,0:T(8,128)S(1)} collective-permute-done((f32[224,128]{1,0:T(8,128)S(1)}, f32[224,128]{1,0:T(8,128)S(1)}, u32[]{:S(2)}, u32[]{:S(2)}) %collective-permute-start.5) | collective-permute-done | bytes 114720 | tf_op jit(solution)/shard_map/ppermute | solution.py:77
  39.0 1.5 %fold_z.1 = (f32[3136,128]{1,0:T(8,128)S(1)}, f32[224,128]{1,0:T(8,128)S(1)}, f32[336,128]{1,0:T(8,128)S(1)}, f32[336,128]{1,0:T(8,128)S(1)}) custom-call(s32[5]{0:T(128)S(1)} %stack.19.place, f32[3136,128]{1,0:T(8,128)S(1)} %get-tuple-element.44.local, f32[224,128]{1,0:T(8,128)S(1)} %get-tuple-element.45.refs_0_, f32[224,128]{1,0:T(8,128)S(1)} %collective-permute-done.5.refs_1_), custom_call_target="tpu_custom_call" | custom-call | bytes 3899412 | tf_op jit(solution)/shard_map/fold_z/pallas_call | solution.py:27
  40.5 1.8 %collective-permute-start.6 = (f32[336,128]{1,0:T(8,128)S(1)}, f32[336,128]{1,0:T(8,128)S(1)}, u32[]{:S(2)}, u32[]{:S(2)}) collective-permute-start(f32[336,128]{1,0:T(8,128)S(1)} %get-tuple-element.48), channel_id=1, source_target_pairs={{0,8},{8,16},{16,24},{24,0},{1,9},{9,17},{17,25},{25,1},{2,10},{10... | collective-permute-start | bytes 516104 | tf_op jit(solution)/shard_map/ppermute | solution.py:87
  42.3 2.1 %collective-permute-start.7 = (f32[336,128]{1,0:T(8,128)S(1)}, f32[336,128]{1,0:T(8,128)S(1)}, u32[]{:S(2)}, u32[]{:S(2)}) collective-permute-start(f32[336,128]{1,0:T(8,128)S(1)} %get-tuple-element.49), channel_id=1, source_target_pairs={{8,0},{16,8},{24,16},{0,24},{9,1},{17,9},{25,17},{1,25},{10,2},{18... | collective-permute-start | bytes 516104 | tf_op jit(solution)/shard_map/ppermute | solution.py:87
  44.4 5.2 %collective-permute-done.6.refs_1_ = f32[336,128]{1,0:T(8,128)S(1)} collective-permute-done((f32[336,128]{1,0:T(8,128)S(1)}, f32[336,128]{1,0:T(8,128)S(1)}, u32[]{:S(2)}, u32[]{:S(2)}) %collective-permute-start.6) | collective-permute-done | bytes 172064 | tf_op jit(solution)/shard_map/ppermute | solution.py:87
  49.6 2.5 %collective-permute-done.7.refs_2_ = f32[336,128]{1,0:T(8,128)S(1)} collective-permute-done((f32[336,128]{1,0:T(8,128)S(1)}, f32[336,128]{1,0:T(8,128)S(1)}, u32[]{:S(2)}, u32[]{:S(2)}) %collective-permute-start.7) | collective-permute-done | bytes 172064 | tf_op jit(solution)/shard_map/ppermute | solution.py:87
  52.1 0.7 fold_x.1
  52.8 1.5 %collective-permute-start.8 = (f32[270,128]{1,0:T(8,128)S(1)}, f32[270,128]{1,0:T(8,128)S(1)}, u32[]{:S(2)}, u32[]{:S(2)}) collective-permute-start(f32[270,128]{1,0:T(8,128)S(1)} %get-tuple-element.52), channel_id=1, source_target_pairs={{0,2},{2,4},{4,6},{6,0},{1,3},{3,5},{5,7},{7,1},{8,10},{10,12},{12... | collective-permute-start | bytes 414728 | tf_op jit(solution)/shard_map/ppermute | solution.py:87
  54.3 1.4 %collective-permute-start.9 = (f32[270,128]{1,0:T(8,128)S(1)}, f32[270,128]{1,0:T(8,128)S(1)}, u32[]{:S(2)}, u32[]{:S(2)}) collective-permute-start(f32[270,128]{1,0:T(8,128)S(1)} %get-tuple-element.53), channel_id=1, source_target_pairs={{2,0},{4,2},{6,4},{0,6},{3,1},{5,3},{7,5},{1,7},{10,8},{12,10},{14... | collective-permute-start | bytes 414728 | tf_op jit(solution)/shard_map/ppermute | solution.py:87
  55.8 4.6 %collective-permute-done.8.refs_1_ = f32[270,128]{1,0:T(8,128)S(1)} collective-permute-done((f32[270,128]{1,0:T(8,128)S(1)}, f32[270,128]{1,0:T(8,128)S(1)}, u32[]{:S(2)}, u32[]{:S(2)}) %collective-permute-start.8) | collective-permute-done | bytes 138272 | tf_op jit(solution)/shard_map/ppermute | solution.py:87
  60.3 0.7 collective-permute-done.9.refs_2_
  61.0 3.3 %operator.1 = (f32[48,48,128]{2,1,0:T(8,128)S(1)}, f32[48,48,128]{2,1,0:T(8,128)S(1)}, f32[48,48,128]{2,1,0:T(8,128)S(1)}, f32[2,48,128]{2,1,0:T(8,128)S(1)}, f3...) custom-call(s32[5]{0:T(128)S(1)} %stack.19.place, f32[3]{0:T(128)S(1)} %copy-done.8, ...), custom_call_target="tpu_custom_call" | custom-call | bytes 8058912 | tf_op jit(solution)/shard_map/operator/pallas_call | solution.py:27
  64.3 10.9 %all_to_all.11 = f32[32,1,128]{2,1,0:T(1,128)S(1)} all-to-all(f32[32,1,128]{2,1,0:T(1,128)S(1)} %bitcast.11), channel_id=1, replica_groups=mesh['gx'=4,'gy'=4,'gz'=2] {'gx','gy','gz'}, dimensions={0} | all-to-all | bytes 32768 | tf_op jit(solution)/shard_map/all_to_all | solution.py:636
  75.2 2.9 %finish.1 = (f32[48,48,128]{2,1,0:T(8,128)}, f32[48,48,128]{2,1,0:T(8,128)}) custom-call(s32[5]{0:T(128)S(1)} %stack.19.place, f32[32,128]{1,0:T(8,128)S(1)} %bitcast.10, f32[16,16]{1,0:T(8,128)S(1)} %copy-done.7, f32[48,48,128]{2,1,0:T(8,128)S(1)} %get-tuple-element.55.direction, f32[48,48,128]{2,1,0:T(8,128)S(1)} %get-tuple-element.56.applied, ...), custom_call_target="tpu_custom_call" | custom-call | bytes 7193620 | tf_op jit(solution)/shard_map/finish/pallas_call | solution.py:27
  (23 shorter events, 0.1 us)
Async XLA Ops:
  0.6 1.3 %copy-start = (f32[48,48,128]{2,1,0:T(8,128)S(1)}, f32[48,48,128]{2,1,0:T(8,128)}, u32[]{:S(2)}) copy-start(f32[48,48,128]{2,1,0:T(8,128)} %right.5) | copy-start | bytes 3538948
  1.9 1.1 %copy-start.2 = (bf16[48,48,128]{2,1,0:T(8,128)(2,1)S(1)}, bf16[48,48,128]{2,1,0:T(8,128)(2,1)}, u32[]{:S(2)}) copy-start(bf16[48,48,128]{2,1,0:T(8,128)(2,1)} %refs_4_.1) | copy-start | bytes 1769476
  3.0 10.5 %copy-start.1 = (f32[48,48,128]{2,1,0:T(8,128)S(1)}, f32[48,48,128]{2,1,0:T(8,128)}, u32[]{:S(2)}) copy-start(f32[48,48,128]{2,1,0:T(8,128)} %right.5) | copy-start | bytes 3538948
  3.0 10.5 %copy-start.3 = (bf16[48,48,128]{2,1,0:T(8,128)(2,1)S(1)}, bf16[48,48,128]{2,1,0:T(8,128)(2,1)}, u32[]{:S(2)}) copy-start(bf16[48,48,128]{2,1,0:T(8,128)(2,1)} %refs_4_.1) | copy-start | bytes 1769476
  3.0 9.3 %collective-permute-start = (f32[240,128]{1,0:T(8,128)S(1)}, f32[240,128]{1,0:T(8,128)S(1)}, u32[]{:S(2)}, u32[]{:S(2)}) collective-permute-start(f32[240,128]{1,0:T(8,128)S(1)} %get-tuple-element.31), channel_id=1, source_target_pairs={{0,8},{8,16},{16,24},{24,0},{1,9},{9,17},{17,25},{25,1},{2,10},{10... | collective-permute-start | bytes 368648 | tf_op jit(solution)/shard_map/ppermute | solution.py:87
  6.1 7.4 %collective-permute-start.1 = (f32[240,128]{1,0:T(8,128)S(1)}, f32[240,128]{1,0:T(8,128)S(1)}, u32[]{:S(2)}, u32[]{:S(2)}) collective-permute-start(f32[240,128]{1,0:T(8,128)S(1)} %get-tuple-element.32), channel_id=1, source_target_pairs={{8,0},{16,8},{24,16},{0,24},{9,1},{17,9},{25,17},{1,25},{10,2},{18... | collective-permute-start | bytes 368648 | tf_op jit(solution)/shard_map/ppermute | solution.py:87
  14.1 10.7 %copy-start.4 = (f32[72,72]{1,0:T(8,128)S(1)}, f32[72,72]{1,0:T(8,128)}, u32[]{:S(2)}) copy-start(f32[72,72]{1,0:T(8,128)} %zv.1) | copy-start | bytes 62212
  14.1 10.7 %copy-start.5 = (f32[56,56]{1,0:T(8,128)S(1)}, f32[56,56]{1,0:T(8,128)}, u32[]{:S(2)}) copy-start(f32[56,56]{1,0:T(8,128)} %xv.1) | copy-start | bytes 37636
  14.1 10.7 %copy-start.6 = (f32[56,56]{1,0:T(8,128)S(1)}, f32[56,56]{1,0:T(8,128)}, u32[]{:S(2)}) copy-start(f32[56,56]{1,0:T(8,128)} %yv.1) | copy-start | bytes 37636
  14.1 10.7 %copy-start.8 = (f32[3]{0:T(128)S(1)}, f32[3]{0:T(128)}, u32[]{:S(2)}) copy-start(f32[3]{0:T(128)} %axes.5) | copy-start | bytes 40
  14.2 10.7 %copy-start.9 = (f32[56]{0:T(128)S(1)}, f32[56]{0:T(128)}, u32[]{:S(2)}) copy-start(f32[56]{0:T(128)} %param.17) | copy-start | bytes 676
  14.2 10.7 %copy-start.10 = (f32[72]{0:T(128)S(1)}, f32[72]{0:T(128)}, u32[]{:S(2)}) copy-start(f32[72]{0:T(128)} %param.18) | copy-start | bytes 868
  14.2 7.4 %collective-permute-start.2 = (f32[272,128]{1,0:T(8,128)S(1)}, f32[272,128]{1,0:T(8,128)S(1)}, u32[]{:S(2)}, u32[]{:S(2)}) collective-permute-start(f32[272,128]{1,0:T(8,128)S(1)} %get-tuple-element.33), channel_id=1, source_target_pairs={{0,2},{2,4},{4,6},{6,0},{1,3},{3,5},{5,7},{7,1},{8,10},{10,12},{12... | collective-permute-start | bytes 417800 | tf_op jit(solution)/shard_map/ppermute | solution.py:87
  15.7 10.4 %copy-start.11 = (f32[56]{0:T(128)S(1)}, f32[56]{0:T(128)}, u32[]{:S(2)}) copy-start(f32[56]{0:T(128)} %x_values.1) | copy-start | bytes 676
  15.7 7.4 %collective-permute-start.3 = (f32[272,128]{1,0:T(8,128)S(1)}, f32[272,128]{1,0:T(8,128)S(1)}, u32[]{:S(2)}, u32[]{:S(2)}) collective-permute-start(f32[272,128]{1,0:T(8,128)S(1)} %get-tuple-element.34), channel_id=1, source_target_pairs={{2,0},{4,2},{6,4},{0,6},{3,1},{5,3},{7,5},{1,7},{10,8},{12,10},{14... | collective-permute-start | bytes 417800 | tf_op jit(solution)/shard_map/ppermute | solution.py:87
  24.7 1.4 %collective-permute-start.4 = (f32[224,128]{1,0:T(8,128)S(1)}, f32[224,128]{1,0:T(8,128)S(1)}, u32[]{:S(2)}, u32[]{:S(2)}) collective-permute-start(f32[224,128]{1,0:T(8,128)S(1)} %get-tuple-element.36), channel_id=1, source_target_pairs={{0,1},{1,0},{2,3},{3,2},{4,5},{5,4},{6,7},{7,6},{8,9},{9,8},{10,11... | collective-permute-start | bytes 344072 | tf_op jit(solution)/shard_map/ppermute | solution.py:77
  37.6 1.4 %collective-permute-start.5 = (f32[224,128]{1,0:T(8,128)S(1)}, f32[224,128]{1,0:T(8,128)S(1)}, u32[]{:S(2)}, u32[]{:S(2)}) collective-permute-start(f32[224,128]{1,0:T(8,128)S(1)} %get-tuple-element.45.refs_0_), channel_id=1, source_target_pairs={{0,1},{1,0},{2,3},{3,2},{4,5},{5,4},{6,7},{7,6},{8,9},{9,8},{10,11... | collective-permute-start | bytes 344072 | tf_op jit(solution)/shard_map/ppermute | solution.py:77
  40.5 9.1 %collective-permute-start.6 = (f32[336,128]{1,0:T(8,128)S(1)}, f32[336,128]{1,0:T(8,128)S(1)}, u32[]{:S(2)}, u32[]{:S(2)}) collective-permute-start(f32[336,128]{1,0:T(8,128)S(1)} %get-tuple-element.48), channel_id=1, source_target_pairs={{0,8},{8,16},{16,24},{24,0},{1,9},{9,17},{17,25},{25,1},{2,10},{10... | collective-permute-start | bytes 516104 | tf_op jit(solution)/shard_map/ppermute | solution.py:87
  42.3 9.8 %collective-permute-start.7 = (f32[336,128]{1,0:T(8,128)S(1)}, f32[336,128]{1,0:T(8,128)S(1)}, u32[]{:S(2)}, u32[]{:S(2)}) collective-permute-start(f32[336,128]{1,0:T(8,128)S(1)} %get-tuple-element.49), channel_id=1, source_target_pairs={{8,0},{16,8},{24,16},{0,24},{9,1},{17,9},{25,17},{1,25},{10,2},{18... | collective-permute-start | bytes 516104 | tf_op jit(solution)/shard_map/ppermute | solution.py:87
  52.8 7.5 %collective-permute-start.8 = (f32[270,128]{1,0:T(8,128)S(1)}, f32[270,128]{1,0:T(8,128)S(1)}, u32[]{:S(2)}, u32[]{:S(2)}) collective-permute-start(f32[270,128]{1,0:T(8,128)S(1)} %get-tuple-element.52), channel_id=1, source_target_pairs={{0,2},{2,4},{4,6},{6,0},{1,3},{3,5},{5,7},{7,1},{8,10},{10,12},{12... | collective-permute-start | bytes 414728 | tf_op jit(solution)/shard_map/ppermute | solution.py:87
  54.3 6.7 %collective-permute-start.9 = (f32[270,128]{1,0:T(8,128)S(1)}, f32[270,128]{1,0:T(8,128)S(1)}, u32[]{:S(2)}, u32[]{:S(2)}) collective-permute-start(f32[270,128]{1,0:T(8,128)S(1)} %get-tuple-element.53), channel_id=1, source_target_pairs={{2,0},{4,2},{6,4},{0,6},{3,1},{5,3},{7,5},{1,7},{10,8},{12,10},{14... | collective-permute-start | bytes 414728 | tf_op jit(solution)/shard_map/ppermute | solution.py:87
  61.0 14.2 %copy-start.7 = (f32[16,16]{1,0:T(8,128)S(1)}, f32[16,16]{1,0:T(8,128)}, u32[]{:S(2)}) copy-start(f32[16,16]{1,0:T(8,128)} %inverse.1) | copy-start | bytes 3076

commit v2 on v1

v2 whole, which is shorter than its diff:
```python
import functools

import jax
import jax.numpy as jnp
from jax import lax
from jax.experimental import pallas as pl
from jax.experimental.pallas import tpu as pltpu
from jax.sharding import PartitionSpec as P

SZ = 64
OV = 4
RIM = OV + 1
LANES = 128
SLOT = 8
GROUP = LANES // SLOT
F32 = jnp.float32
BF16 = jnp.bfloat16
MESH_AXES = ("gx", "gy", "gz")

VMEM = pl.BlockSpec(memory_space=pltpu.VMEM)
ANY = pl.BlockSpec(memory_space=pl.ANY)
HBM = pl.BlockSpec(memory_space=pltpu.HBM)


def call(sizes, kernel, name, outs, args, spaces, scratch=(), limit=8, out_specs=None, aliases=None, flops=0):
    size = sum(o.size * o.dtype.itemsize for o in outs) + sum(a.size * a.dtype.itemsize for a in args)

    def placed(*refs):
        return kernel(place_values(sizes), *refs)

    return pl.pallas_call(
        placed,
        out_shape=outs,
        in_specs=spaces,
        out_specs=out_specs or [VMEM] * len(outs),
        scratch_shapes=list(scratch),
        input_output_aliases=aliases or {},
        name=name,
        compiler_params=pltpu.CompilerParams(vmem_limit_bytes=limit * 2**20),
        cost_estimate=pl.CostEstimate(flops=flops, bytes_accessed=size, transcendentals=0),
    )(*args)


def shape(dims, dtype=F32):
    return jax.ShapeDtypeStruct(tuple(dims), dtype)


def halves(value):
    high = value.astype(BF16)
    return high, (value - high.astype(F32)).astype(BF16)


def dot(left, right):
    return jnp.dot(left, right, preferred_element_type=F32)


def iota(dims, axis):
    return lax.broadcasted_iota(jnp.int32, dims, axis)


IX, IY, IZ, SIDE = 0, 1, 2, 3


def place_values(sizes):
    ix, iy, iz = (lax.axis_index(a) for a in MESH_AXES)
    nz = sizes["gz"]
    if nz == 2:
        sides = [1 - iz, 1]
    else:
        sides = [1, jnp.where(iz < nz - 1, 1, 0), 0, jnp.where(iz > 0, 1, 0)]
    return [ix, iy, iz] + sides


def swap_sides(messages, sizes):
    count = sizes["gz"]
    if count == 2:
        return [lax.ppermute(messages[0], "gz", [(0, 1), (1, 0)])]
    up = [(i, (i + 1) % count) for i in range(count)]
    down = [((i + 1) % count, i) for i in range(count)]
    return [lax.ppermute(messages[1], "gz", down), lax.ppermute(messages[0], "gz", up)]


def swap_ends(first, second, axis, sizes):
    count = sizes[axis]
    received = []
    for message, start in ((first, 0), (second, 1)):
        partner = list(range(count))
        for i in range(start, count - 1, 2):
            partner[i], partner[i + 1] = i + 1, i
        received.append(lax.ppermute(message, axis, list(enumerate(partner))))
    return received


def is_even(place, axis):
    return lax.rem(place[axis], 2) == 0


def from_ends(place, axis, sizes, first, second):
    even = is_even(place, axis)
    inside_low = place[axis] > 0
    inside_high = place[axis] < sizes[MESH_AXES[axis]] - 1

    def low(at):
        return jnp.where(inside_low, jnp.where(even, second[at], first[at]), 0.0)

    def high(at):
        return jnp.where(inside_high, jnp.where(even, first[at], second[at]), 0.0)

    return low, high


def prepare_kernel(sides, place, axes, xv, yv, zv, y_row, z_row, fx, bx, fy, by, wz, bz, den, pad, wide, rows):
    ez = zv.shape[0]
    depth = wz.shape[0] // 4

    def stacked(value, out):
        high, low = halves(value[: LANES // 2])
        high = high.astype(F32)
        twice = jnp.where(iota(high.shape, 1) < LANES // 2, high, pltpu.roll(high, LANES // 2, 1))
        out[:, 0:LANES] = twice.astype(BF16)
        out[:, LANES:] = low[:, 0 : LANES // 2]

    for vectors, forward, back in ((xv, fx, bx), (yv, fy, by)):
        pad[...] = jnp.zeros_like(pad)
        pad[0 : vectors.shape[0], 0 : vectors.shape[1]] = vectors[...]
        stacked(pad[...], back)
        stacked(pad[...].T, forward)

    wide[...] = jnp.zeros_like(wide)
    wide[0:ez, 0:ez] = zv[...]
    wide[SZ : SZ + ez, LANES : LANES + ez] = zv[...]
    middle = wide[OV : OV + depth]
    high, low = halves(middle)
    wz[0:depth] = high
    wz[depth : 2 * depth] = high
    wz[2 * depth : 3 * depth] = low
    rows[...] = jnp.zeros_like(rows)
    for side in range(sides):
        is_high = place[SIDE + 2 * side] > 0
        for k in range(OV):
            top, bottom = OV + depth + k, k
            row = jnp.where(is_high, wide[top : top + 1], wide[bottom : bottom + 1])
            row_high, row_low = halves(row)
            at = 3 * SLOT * side + k
            rows[at : at + 1] = row_high.astype(F32)
            rows[at + SLOT : at + SLOT + 1] = row_high.astype(F32)
            rows[at + 2 * SLOT : at + 2 * SLOT + 1] = row_low.astype(F32)
    wz[3 * depth :] = rows[...].astype(BF16)

    rows[...] = jnp.zeros_like(rows)
    for side in range(sides):
        is_high = place[SIDE + 2 * side] > 0
        for k in range(RIM):
            top, bottom = OV + depth - 1 + k, k
            rows[SLOT * side + k : SLOT * side + k + 1] = jnp.where(is_high, wide[top : top + 1], wide[bottom : bottom + 1])
    across = 2 * LANES
    for at, part in ((0, middle), (LANES, rows[...])):
        turned = jnp.concatenate([part[:, 0:LANES].T, part[:, LANES:].T], axis=0)
        high, low = halves(turned)
        bz[0:across, at : at + LANES] = high
        bz[across : 2 * across, at : at + LANES] = high
        bz[2 * across :, at : at + LANES] = low

    ey = yv.shape[0]
    diagonal = iota((ey, ey), 0) == iota((ey, ey), 1)
    y_column = jnp.sum(jnp.where(diagonal, y_row[...], 0.0), axis=1, keepdims=True)
    pad[...] = jnp.ones_like(pad)
    pad[0:1, 0:ez] = axes[:, 2:3] * z_row[...]
    den[...] = axes[:, 1:2] * y_column + pad[0:1]


def pack_x_kernel(place, right, scale, first, second, faces, sems):
    ext_x = right.shape[0]
    even = is_even(place, IX)
    copies = []
    for number, (out, high) in enumerate(((first, even), (second, jnp.logical_not(even)))):
        start = jnp.where(high, ext_x - OV, 0)
        face = jnp.where(high, ext_x - 1, 0)
        copies.append(pltpu.make_async_copy(right.at[pl.ds(start, OV)], out.at[pl.ds(0, OV)], sems.at[0, number]))
        copies.append(pltpu.make_async_copy(scale.at[face], faces.at[number], sems.at[1, number]))
    for copy in copies:
        copy.start()
    for copy in copies:
        copy.wait()
    for number, out in enumerate((first, second)):
        out[OV] = faces[number].astype(F32)


def pack_y_own_kernel(place, right, scale, first, second):
    ext_x, ext_y, depth = right.shape
    even = is_even(place, IY)
    base = (ext_x + 2 * OV) * OV
    for x in range(ext_x):
        low, high = right[x, 0:OV], right[x, ext_y - OV : ext_y]
        at = (x + OV) * OV
        first[at : at + OV] = jnp.where(even, high, low)
        second[at : at + OV] = jnp.where(even, low, high)
        low, high = scale[x, 0:16].astype(F32)[0:1], scale[x, ext_y - 16 : ext_y].astype(F32)[15:16]
        first[base + x : base + x + 1] = jnp.where(even, high, low)
        second[base + x : base + x + 1] = jnp.where(even, low, high)


def pack_y_rest_kernel(sizes, place, x_first, x_second, own_first, own_second, first, second):
    ext_y = x_first.shape[1]
    even = is_even(place, IY)
    x_low, x_high = from_ends(place, IX, sizes, x_first, x_second)
    last = (own_first.shape[0] - 2 * OV * OV) // (OV + 1) * OV
    for t in range(OV):
        for source, at in ((x_low, t * OV), (x_high, last + OV * OV + t * OV)):
            low, high = source((t, slice(0, OV))), source((t, slice(ext_y - OV, ext_y)))
            first[at : at + OV] = jnp.where(even, high, low)
            second[at : at + OV] = jnp.where(even, low, high)


def pack_rims(place, side, depth, wide_x, wide_y, ext, message, starts):
    lane = iota((8, LANES), 1)
    start = jnp.where(place[SIDE + 2 * side] > 0, depth - OV, 0)
    for row in starts:
        for group in range((wide_x + GROUP - 1) // GROUP):
            total = jnp.zeros((8, LANES), F32)
            for q in range(min(GROUP, wide_x - group * GROUP)):
                at = (group * GROUP + q) * wide_y + row
                moved = pltpu.roll(ext[at : at + 8], lax.rem(SLOT * q + depth - start, depth), 1)
                total = jnp.where((lane >= SLOT * q) & (lane < SLOT * q + OV), moved, total)
            message[group * wide_y + row : group * wide_y + row + 8] += total


def extend_own_kernel(sizes, sides, place, right, scale, x_first, x_second, ext, *messages):
    ext_x, ext_y, depth = right.shape
    wide_x, wide_y = ext_x + 2 * OV, ext_y + 2 * OV
    x_low, x_high = from_ends(place, IX, sizes, x_first, x_second)
    for a in range(wide_x):
        if a < OV:
            core = x_low(a)
        elif a < ext_x + OV:
            core = right[a - OV]
        else:
            core = x_high(a - OV - ext_x)
        ext[a * wide_y + OV : a * wide_y + OV + ext_y] = core
    lane = iota((ext_y, LANES), 1)
    for side in range(sides):
        face = jnp.where(place[SIDE + 2 * side] > 0, depth - 1, 0)
        messages[side][...] = jnp.zeros_like(messages[side])
        for group in range((ext_x + GROUP - 1) // GROUP):
            total = jnp.zeros((ext_y, LANES), F32)
            for q in range(min(GROUP, ext_x - group * GROUP)):
                at = SLOT * q + OV
                moved = pltpu.roll(scale[group * GROUP + q].astype(F32), lax.rem(at + depth - face, depth), 1)
                total = jnp.where(lane == at, moved, total)
            messages[side][group * wide_y : group * wide_y + ext_y] = total
        pack_rims(place, side, depth, wide_x, wide_y, ext, messages[side], range(8, wide_y - 8, 8))


def extend_rest_kernel(sizes, sides, wide_x, place, y_first, y_second, own_ext, *refs):
    refs = refs[sides:]
    ext, messages = refs[0], refs[1:]
    rows, depth = ext.shape
    wide_y = rows // wide_x
    y_low, y_high = from_ends(place, IY, sizes, y_first, y_second)
    for a in range(wide_x):
        part = slice(a * OV, (a + 1) * OV)
        ext[a * wide_y : a * wide_y + OV] = y_low(part)
        ext[(a + 1) * wide_y - OV : (a + 1) * wide_y] = y_high(part)
    for side in range(sides):
        pack_rims(place, side, depth, wide_x, wide_y, ext, messages[side], (0, wide_y - 8))


def solve_kernel(sides, place, axes, x_values, ext, *refs):
    received, refs = refs[:sides], refs[sides:]
    fx, bx, fy, by, wz, bz, den, local = refs[:8]
    messages, refs = refs[8 : 8 + sides], refs[8 + sides :]
    first_a, first_b, second_a, second_b = refs
    wide = x_values.shape[1]
    rows = ext.shape[0]
    wide_y = rows // wide
    batch = 8
    lane = iota((wide_y, LANES), 1)

    def along(matrix, pair):
        value = jnp.concatenate(pair, axis=1)
        fill = jnp.zeros((LANES // 2 - value.shape[0], value.shape[1]), F32)
        high, low = halves(jnp.concatenate([value, fill], axis=0))
        return dot(matrix[...], jnp.concatenate([high, low, high], axis=0))[0 : value.shape[0]]

    for start in range(0, wide, batch):
        block = pl.ds(start * wide_y, batch * wide_y)
        high, low = halves(ext[block])
        rims = []
        for a in range(start, start + batch):
            group, q = a // GROUP, a % GROUP
            piece = jnp.zeros((wide_y, LANES), F32)
            for side in range(sides):
                value = received[side][group * wide_y : (group + 1) * wide_y]
                value = jnp.where((lane // SLOT == q) & (place[SIDE + 2 * side + 1] > 0), value, 0.0)
                value_high, value_low = halves(value)
                value_high, value_low = value_high.astype(F32), value_low.astype(F32)
                at = LANES - SLOT * q + 3 * SLOT * side
                piece = piece + pltpu.roll(value_high, at % LANES, 1)
                piece = piece + pltpu.roll(value_low, (at + SLOT) % LANES, 1)
                piece = piece + pltpu.roll(value_high, (at + 2 * SLOT) % LANES, 1)
            rims.append(piece.astype(BF16))
        left = jnp.concatenate([high, low, high, jnp.concatenate(rims, axis=0)], axis=1)
        out = dot(left, wz[...])
        first_a[block] = out[:, 0:LANES]
        first_b[block] = out[:, LANES:]

    def strided(refs_pair, at, count, stride):
        return [ref[pl.ds(at, count, stride=stride), :] for ref in refs_pair]

    def x_forward(y):
        out = along(fx, strided((first_a, first_b), y, wide, wide_y))
        second_a[pl.ds(y * wide, wide)] = out[:, 0:LANES]
        second_b[pl.ds(y * wide, wide)] = out[:, LANES:]

    def y_both(i):
        out = along(fy, strided((second_a, second_b), i, wide_y, wide))
        inverse = 1.0 / (axes[:, 0:1] * x_values[:, i : i + 1] + den[...])
        out = along(by, [out[:, 0:LANES] * inverse, out[:, LANES:] * inverse])
        first_a[pl.ds(i * wide_y, wide_y)] = out[:, 0:LANES]
        first_b[pl.ds(i * wide_y, wide_y)] = out[:, LANES:]

    def x_back(y):
        out = along(bx, strided((first_a, first_b), y, wide, wide_y))
        second_a[pl.ds(y, wide, stride=wide_y), :] = out[:, 0:LANES]
        second_b[pl.ds(y, wide, stride=wide_y), :] = out[:, LANES:]

    for step, count in ((x_forward, wide_y), (y_both, wide), (x_back, wide_y)):
        for number in range(count):
            step(number)

    totals = [[jnp.zeros((wide_y, LANES), F32) for _ in range((wide + GROUP - 1) // GROUP)] for _ in range(sides)]
    for start in range(0, wide, batch):
        block = pl.ds(start * wide_y, batch * wide_y)
        high_a, low_a = halves(second_a[block])
        high_b, low_b = halves(second_b[block])
        out = dot(jnp.concatenate([high_a, high_b, low_a, low_b, high_a, high_b], axis=1), bz[...])
        local[block] = out[:, 0:LANES]
        for a in range(start, start + batch):
            group, q = a // GROUP, a % GROUP
            value = out[(a - start) * wide_y : (a - start + 1) * wide_y, LANES:]
            for side in range(sides):
                own = value if sides == 1 else jnp.where(lane // SLOT == side, value, 0.0)
                at = (SLOT * q + LANES - SLOT * side) % LANES
                totals[side][group] = totals[side][group] + (pltpu.roll(own, at, 1) if at else own)
    for side in range(sides):
        for group, total in enumerate(totals[side]):
            messages[side][group * wide_y : (group + 1) * wide_y] = total


def with_z_rims(place, sides, wide_y, local, received, a):
    lane = iota((wide_y, LANES), 1)
    group, q = a // GROUP, a % GROUP
    value = local[a * wide_y : (a + 1) * wide_y]
    for side in range(sides):
        is_high, valid = place[SIDE + 2 * side] > 0, place[SIDE + 2 * side + 1] > 0
        start = jnp.where(is_high, LANES - OV, 0)
        shift = lax.rem(jnp.where(is_high, LANES - OV, LANES - 1) + LANES - SLOT * q, LANES)
        moved = pltpu.roll(received[side][group * wide_y : (group + 1) * wide_y], shift, 1)
        value = value + jnp.where((lane >= start) & (lane < start + OV) & valid, moved, 0.0)
    return value


def pack_back_x_kernel(sides, wide, place, local, *refs):
    own, received = refs[:sides], refs[sides : 2 * sides]
    refs = refs[2 * sides :]
    faces, (first, second) = refs[:sides], refs[sides:]
    wide_y = local.shape[0] // wide
    groups = (wide + GROUP - 1) // GROUP
    even = is_even(place, IX)
    wide_lane = iota((groups * wide_y, LANES), 1)
    for side in range(sides):
        is_high, valid = place[SIDE + 2 * side] > 0, place[SIDE + 2 * side + 1] > 0
        other = pltpu.roll(received[side][...], jnp.where(is_high, LANES - OV, 0), 1)
        mine = pltpu.roll(own[side][...], jnp.where(is_high, LANES - 1, LANES - OV + 1), 1)
        faces[side][...] = jnp.where((lax.rem(wide_lane, SLOT) == 0) & valid, other + mine, 0.0)
        low, high = faces[side][0:wide_y], faces[side][(groups - 1) * wide_y :]
        at = (RIM + side) * wide_y
        first[at : at + wide_y] = jnp.where(even, high, low)
        second[at : at + wide_y] = jnp.where(even, low, high)
    for t in range(RIM):
        low = with_z_rims(place, sides, wide_y, local, received, t)
        high = with_z_rims(place, sides, wide_y, local, received, wide - RIM + t)
        first[t * wide_y : (t + 1) * wide_y] = jnp.where(even, high, low)
        second[t * wide_y : (t + 1) * wide_y] = jnp.where(even, low, high)


def fold_z_kernel(sides, wide, place, local, *refs):
    faces, received = refs[:sides], refs[sides : 2 * sides]
    out, first, second = refs[2 * sides :]
    wide_y = local.shape[0] // wide
    groups = (wide + GROUP - 1) // GROUP
    planes = wide - 2 * OV + 2
    even = is_even(place, IY)
    for a in range(wide):
        value = with_z_rims(place, sides, wide_y, local, received, a)
        out[a * wide_y : (a + 1) * wide_y] = value
        p = a - OV + 1
        if 0 <= p < planes:
            low, high = value[0:RIM], value[wide_y - RIM :]
            first[p * RIM : (p + 1) * RIM] = jnp.where(even, high, low)
            second[p * RIM : (p + 1) * RIM] = jnp.where(even, low, high)
    for side in range(sides):
        for group in range(groups):
            at = planes * RIM + (side * groups + group) * RIM
            low = faces[side][group * wide_y : group * wide_y + RIM]
            high = faces[side][(group + 1) * wide_y - RIM : (group + 1) * wide_y]
            first[at : at + RIM] = jnp.where(even, high, low)
            second[at : at + RIM] = jnp.where(even, low, high)


def x_received(sizes, wide, wide_y, place, x_first, x_second):
    low, high = from_ends(place, IX, sizes, x_first, x_second)
    high_lane = (wide - 2 * OV) % GROUP * SLOT

    def plane(a, rows):
        if OV - 1 <= a < OV - 1 + RIM:
            at, source = (a - OV + 1) * wide_y, low
        elif wide - 2 * OV <= a < wide - 2 * OV + RIM:
            at, source = (a - wide + 2 * OV) * wide_y, high
        else:
            return None
        return source(slice(at + rows.start, at + rows.stop))

    def faces(side, group, rows):
        lane = iota((rows.stop - rows.start, LANES), 1)
        at = (RIM + side) * wide_y
        rows = slice(at + rows.start, at + rows.stop)
        if group == 0:
            return jnp.where((lane >= (OV - 1) * SLOT) & (lane < 2 * OV * SLOT), low(rows), 0.0)
        if group == (wide + GROUP - 1) // GROUP - 1:
            return jnp.where((lane >= high_lane) & (lane < high_lane + RIM * SLOT), high(rows), 0.0)
        return None

    return plane, faces


def pack_back_y_kernel(sizes, sides, wide, wide_y, place, x_first, x_second, own_first, own_second, first, second):
    groups = (wide + GROUP - 1) // GROUP
    planes = wide - 2 * OV + 2
    even = is_even(place, IY)
    plane, faces = x_received(sizes, wide, wide_y, place, x_first, x_second)
    low_rows, high_rows = slice(0, RIM), slice(wide_y - RIM, wide_y)

    def add(at, low, high):
        first[at : at + RIM] += jnp.where(even, high, low)
        second[at : at + RIM] += jnp.where(even, low, high)

    for p in range(planes):
        low = plane(p + OV - 1, low_rows)
        if low is not None:
            add(p * RIM, low, plane(p + OV - 1, high_rows))
    for side in range(sides):
        for group in range(groups):
            low = faces(side, group, low_rows)
            if low is not None:
                add(planes * RIM + (side * groups + group) * RIM, low, faces(side, group, high_rows))


def weights_kernel(sizes, sides, place, axes, right, scale, x_first, x_second, y_first, y_second, *refs):
    scale_faces = refs[:sides]
    wx, wy, wz, z_weight, sums, scales = refs[sides:]
    ext_x, ext_y, depth = right.shape
    wide_y = ext_y + 2 * OV
    core = slice(8, 8 + ext_y)
    x_low, x_high = from_ends(place, IX, sizes, x_first, x_second)
    y_low, y_high = from_ends(place, IY, sizes, y_first, y_second)
    y_rows = (ext_x + 2 * OV) * OV
    scales[0, core] = x_low(OV)
    scales[ext_x + 1, core] = x_high(OV)
    for x in range(ext_x):
        scales[x + 1, core] = scale[x].astype(F32)
        part = slice(y_rows + x, y_rows + x + 1)
        scales[x + 1, 7:8] = y_low(part)
        scales[x + 1, 8 + ext_y : 9 + ext_y] = y_high(part)
    hx, hy, hz = (0.5 * axes[:, d : d + 1] for d in range(3))
    lane = iota((8, depth), 1)
    ends = (lane == 0) | (lane == depth - 1)
    zero = jnp.zeros((8, depth), F32)
    sum_right, sum_z = zero, zero
    for x in range(ext_x + 1):
        wx[x] = hx * (scales[x, core] + scales[x + 1, core])
    for x in range(ext_x):
        wy[x, 0 : ext_y + 1] = hy * (scales[x + 1, 7 : 8 + ext_y] + scales[x + 1, 8 : 9 + ext_y])
        for row in range(0, ext_y, 8):
            own = scales[x + 1, 8 + row : 16 + row]
            edge = zero
            for side in range(sides):
                is_high, valid = place[SIDE + 2 * side] > 0, place[SIDE + 2 * side + 1] > 0
                target = jnp.where(is_high, depth - 1, 0)
                at = x // GROUP * wide_y + row
                shift = lax.rem(target + depth - (x % GROUP * SLOT + OV), depth)
                edge = jnp.where((lane == target) & valid, pltpu.roll(scale_faces[side][at : at + 8], shift, 1), edge)
            wz[x, row : row + 8] = hz * (own + jnp.where(lane == 0, edge, pltpu.roll(own, 1, 1)))
            end_weight = jnp.where(ends, hz * (own + edge), 0.0)
            z_weight[x, row : row + 8] = end_weight
            sum_z = sum_z + end_weight
            sum_right = sum_right + right[x, row : row + 8]

    def whole(value):
        return jnp.sum(jnp.sum(value, axis=0, keepdims=True), axis=1, keepdims=True)

    def y_sum(row):
        total = jnp.zeros((1, depth), F32)
        for x in range(ext_x):
            total = total + wy[x, row : row + 1]
        return whole(total)

    x_high_sum, y_high_sum = whole(wx[ext_x]), y_sum(ext_y)
    z_high_sum = whole(jnp.where(lane == depth - 1, sum_z, 0.0))
    faces_sum = whole(wx[0]) + x_high_sum + y_sum(0) + y_high_sum + whole(sum_z)
    columns = {
        0: whole(sum_right),
        4: faces_sum,
        5: jnp.where(place[IX] < sizes["gx"] - 1, x_high_sum, 0.0),
        6: jnp.where(place[IY] < sizes["gy"] - 1, y_high_sum, 0.0),
        7: jnp.where(place[IZ] < sizes["gz"] - 1, z_high_sum, 0.0),
    }
    sums[...] = in_columns(columns, jnp.zeros((1, LANES), F32))


def in_columns(columns, row):
    at = iota((1, LANES), 1)
    for number, value in columns.items():
        row = jnp.where(at == number, value, row)
    return row


def operator_tile(place, sides, groups, values, edges, wx, wy, wz, z_weight, block, inner, row):
    depth = values.shape[2]
    ext_y = z_weight.shape[1]
    lane = iota((8, depth), 1)
    at = slice(8 + row, 16 + row)
    x = block * GROUP + inner
    mid = values[x + 1, at]
    total = wx[x, row : row + 8] * (mid - values[x, at]) + wx[x + 1, row : row + 8] * (mid - values[x + 2, at])
    total = total + wy[x, row : row + 8] * (mid - values[x + 1, 7 + row : 15 + row])
    total = total + wy[x, row + 1 : row + 9] * (mid - values[x + 1, 9 + row : 17 + row])
    edge = jnp.zeros((8, depth), F32)
    for side in range(sides):
        is_high, valid = place[SIDE + 2 * side] > 0, place[SIDE + 2 * side + 1] > 0
        target = jnp.where(is_high, depth - 1, 0)
        start = (side * groups + block + (inner + OV) // GROUP) * ext_y + row
        moved = edges[pl.ds(pl.multiple_of(start, 8), 8)]
        q = (inner + OV) % GROUP
        if q:
            moved = pltpu.roll(moved, depth - q * SLOT, 1)
        edge = jnp.where((lane == target) & valid, moved, edge)
    flux = wz[x, row : row + 8] * (mid - jnp.where(lane == 0, edge, pltpu.roll(mid, 1, 1)))
    above = z_weight[x, row : row + 8] * (mid - edge)
    total = total + flux + jnp.where(lane == depth - 1, above, -pltpu.roll(flux, depth - 1, 1))
    return mid, total


def operator_tiles(place, sides, groups, right, values, edges, weights, applied, sums, rows):
    def several(block, totals):
        product, energy, whole = totals
        for inner in range(GROUP):
            x = block * GROUP + inner
            for row in rows:
                mid, total = operator_tile(place, sides, groups, values, edges, *weights, block, inner, row)
                applied[x, row : row + 8] = total
                product = product + right[x, row : row + 8] * mid
                energy = energy + mid * total
                whole = whole + total
        return product, energy, whole

    totals = lax.fori_loop(0, right.shape[0] // GROUP, several, (jnp.zeros((8, values.shape[2]), F32),) * 3)
    for number, value in enumerate(totals):
        sums[number * 8 : (number + 1) * 8] = value


def to_face(place, side, value):
    return pltpu.roll(value, jnp.where(place[SIDE + 2 * side] > 0, LANES - 1, 0), 1)


def inner_kernel(sizes, sides, wide, place, right, field, x_first, x_second, *refs):
    faces, weights, refs = refs[:sides], refs[sides : sides + 4], refs[sides + 4 :]
    values, edges, applied, sums = refs
    ext_x, ext_y, depth = right.shape
    wide_y = ext_y + 2 * OV
    groups = (wide + GROUP - 1) // GROUP
    plane, face = x_received(sizes, wide, wide_y, place, x_first, x_second)
    inside_low, inside_high = place[IX] > 0, place[IX] < sizes["gx"] - 1
    rows = slice(OV - 1, wide_y - OV + 1)
    for p in range(ext_x + 2):
        a = p + OV - 1
        value = field[a * wide_y + rows.start : a * wide_y + rows.stop]
        more = plane(a, rows)
        if more is not None:
            value = value + more
        if p == 0:
            value = jnp.where(inside_low, value, 0.0)
        if p == ext_x + 1:
            value = jnp.where(inside_high, value, 0.0)
        values[p, 7 : 9 + ext_y] = value
    for side in range(sides):
        for group in range(groups):
            value = faces[side][group * wide_y : (group + 1) * wide_y]
            more = face(side, group, slice(0, wide_y))
            value = value if more is None else value + more
            at = (side * groups + group) * ext_y
            edges[at : at + ext_y] = to_face(place, side, value)[OV : OV + ext_y]
    operator_tiles(place, sides, groups, right, values, edges, weights, applied, sums, range(8, ext_y - 8, 8))


def outer_kernel(sizes, sides, wide, place, right, y_first, y_second, *refs):
    weights, fixed, refs = refs[:4], refs[4], refs[5:]
    inner_sums, refs = refs[3], refs[4:]
    values, edges, applied, out, sums = refs
    ext_x, ext_y, depth = right.shape
    wide_y = ext_y + 2 * OV
    groups = (wide + GROUP - 1) // GROUP
    low, high = from_ends(place, IY, sizes, y_first, y_second)
    inside_low, inside_high = place[IY] > 0, place[IY] < sizes["gy"] - 1
    for p in range(ext_x + 2):
        part = slice(p * RIM, (p + 1) * RIM)
        low_rows, high_rows = low(part), high(part)
        if p == 0 or p == ext_x + 1:
            inside = place[IX] > 0 if p == 0 else place[IX] < sizes["gx"] - 1
            low_rows, high_rows = (jnp.where(inside, rows, 0.0) for rows in (low_rows, high_rows))
        values[p, 7 : 7 + RIM] += low_rows
        values[p, 4 + ext_y : 4 + ext_y + RIM] += high_rows
        values[p, 7:8] = jnp.where(inside_low, values[p, 7:8], 0.0)
        values[p, 8 + ext_y : 9 + ext_y] = jnp.where(inside_high, values[p, 8 + ext_y : 9 + ext_y], 0.0)
    for number in range(sides * groups):
        at = (ext_x + 2 + number) * RIM
        start = number * ext_y
        side = number // groups
        edges[start : start + OV] += to_face(place, side, low(slice(at, at + RIM)))[1:]
        edges[start + ext_y - OV : start + ext_y] += to_face(place, side, high(slice(at, at + RIM)))[:OV]
    operator_tiles(place, sides, groups, right, values, edges, weights, applied, sums, (0, ext_y - 8))
    columns = {}
    for number in range(3):
        part = slice(number * 8, (number + 1) * 8)
        value = inner_sums[part] + sums[part]
        columns[number + 1] = jnp.sum(jnp.sum(value, axis=0, keepdims=True), axis=1, keepdims=True)
    out[...] = jnp.broadcast_to(in_columns(columns, fixed[...]), out.shape)


def finish_kernel(sizes, place, sums, inverse, values, applied, wx, wy, z_weight, right, solution, residual, held_s, held_r, sems):
    ext_x, ext_y, depth = right.shape
    nx, ny, nz = (sizes[a] for a in MESH_AXES)
    count, blocks = nx * ny * nz, nx * ny * nz // 2
    table = sums[...]
    part = [table[:, k : k + 1] for k in range(8)]
    member = iota((count, blocks), 0) // 2 == iota((count, blocks), 1)
    means = jnp.sum(jnp.where(member, part[0], 0.0), axis=0, keepdims=True) / (2.0 * ext_x * ext_y * depth)
    coarse = jnp.sum(inverse[...] * means, axis=1, keepdims=True)
    diagonal = iota((blocks, blocks), 0) == iota((blocks, blocks), 1)
    coarse_row = jnp.sum(jnp.where(diagonal, coarse, 0.0), axis=0, keepdims=True)
    level = jnp.sum(jnp.where(member, coarse_row, 0.0), axis=1, keepdims=True)

    def shifted(by):
        return jnp.concatenate([level[by:], level[:by]], axis=0)

    def whole(value):
        return jnp.sum(value, axis=0, keepdims=True)

    product = whole(part[1] + level * part[0])
    neighbours = part[5] * shifted(ny * nz) + part[6] * shifted(nz) + part[7] * shifted(1)
    curvature = whole(part[2] + 2.0 * level * part[3] + level * (level * part[4] - 2.0 * neighbours))
    step = product / curvature
    device = iota((count, 1), 0)
    mine = (place[IX] * ny + place[IY]) * nz + place[IZ]

    def level_at(number, inside):
        return whole(jnp.where((device == number) & inside, level, 0.0))

    own = level_at(mine, True)
    drops = []
    for axis, stride, size in ((IX, ny * nz, nx), (IY, nz, ny), (IZ, 1, nz)):
        drops.append(step * (own - level_at(mine - stride, place[axis] > 0)))
        drops.append(step * (own - level_at(mine + stride, place[axis] < size - 1)))
    z_drop = jnp.where(iota((1, depth), 1) < depth // 2, drops[4], drops[5])
    chunk = 12
    for x in range(ext_x):
        held_s[x] = step * (values[x + 1, 8 : 8 + ext_y] + own)
        value = right[x] - step * applied[x] - z_drop * z_weight[x]
        if x == 0:
            value = value - drops[0] * wx[0]
        if x == ext_x - 1:
            value = value - drops[1] * wx[ext_x]
        held_r[x] = value
        held_r[x, 0:1] = value[0:1] - drops[2] * wy[x, 0:1]
        held_r[x, ext_y - 1 : ext_y] = value[ext_y - 1 : ext_y] - drops[3] * wy[x, ext_y : ext_y + 1]
        if (x + 1) % chunk == 0:
            part_x = pl.ds(x + 1 - chunk, chunk)
            number = (x + 1) // chunk - 1
            pltpu.make_async_copy(held_s.at[part_x], solution.at[part_x], sems.at[0, number]).start()
            pltpu.make_async_copy(held_r.at[part_x], residual.at[part_x], sems.at[1, number]).start()
    for number in range(ext_x // chunk):
        part_x = pl.ds(number * chunk, chunk)
        pltpu.make_async_copy(held_s.at[part_x], solution.at[part_x], sems.at[0, number]).wait()
        pltpu.make_async_copy(held_r.at[part_x], residual.at[part_x], sems.at[1, number]).wait()


def body(sizes, right, scale, axes, xv, yv, zv, x_values, y_values, z_values, inverse):
    ext_x, ext_y, depth = right.shape
    wide_x, wide_y = xv.shape[0], yv.shape[0]
    sides = 1 if sizes["gz"] == 2 else 2
    groups = (wide_x + GROUP - 1) // GROUP
    count = sizes["gx"] * sizes["gy"] * sizes["gz"]
    bind = functools.partial
    run = bind(call, sizes)
    block = shape(right.shape)
    axes_row = axes.reshape(1, -1)
    beside = 2 * 10**9

    xs = run(
        pack_x_kernel,
        "pack_x",
        [shape([RIM, ext_y, depth])] * 2,
        [right, scale],
        [HBM] * 2,
        [pltpu.VMEM((2, ext_y, depth), BF16), pltpu.SemaphoreType.DMA((2, 2))],
        limit=60,
    )
    xs = swap_ends(*xs, "gx", sizes)

    thin = shape([LANES // 2, 3 * LANES // 2], BF16)
    mats = run(
        bind(prepare_kernel, sides),
        "prepare",
        [thin] * 4 + [shape([4 * depth, 2 * LANES], BF16), shape([6 * LANES, 2 * LANES], BF16), shape([wide_y, LANES])],
        [axes_row, xv, yv, zv, y_values.reshape(1, -1), z_values.reshape(1, -1)],
        [VMEM] * 6,
        [pltpu.VMEM((LANES, LANES), F32), pltpu.VMEM((depth + 2 * OV, 2 * LANES), F32), pltpu.VMEM((LANES, 2 * LANES), F32)],
        flops=beside,
    )
    y_message = [shape([wide_x * OV + ext_x, depth])] * 2
    ys = run(pack_y_own_kernel, "pack_y_own", y_message, [right, scale], [VMEM] * 2, flops=beside)
    ys, mats = lax.optimization_barrier((ys, mats))
    ys = run(
        bind(pack_y_rest_kernel, sizes),
        "pack_y_rest",
        y_message,
        [*xs, *ys],
        [VMEM] * 4,
        aliases={2: 0, 3: 1},
    )
    ys = swap_ends(*ys, "gy", sizes)

    rim_message = shape([groups * wide_y, LANES])
    field = shape([wide_x * wide_y, depth])
    ext, *rims = run(
        bind(extend_own_kernel, sizes, sides),
        "extend_own",
        [field] + [rim_message] * sides,
        [right, scale, *xs],
        [VMEM] * 4,
        flops=beside,
    )
    ext, *rims = run(
        bind(extend_rest_kernel, sizes, sides, wide_x),
        "extend_rest",
        [field] + [rim_message] * sides,
        [*ys, ext, *rims],
        [VMEM] * (3 + sides),
        aliases={2 + k: k for k in range(1 + sides)},
    )
    rims = swap_sides(rims, sizes)

    tall = pltpu.VMEM((wide_x * wide_y, LANES), F32)
    local, *own_rims = run(
        bind(solve_kernel, sides),
        "solve",
        [field] + [rim_message] * sides,
        [axes_row, x_values.reshape(1, -1), ext, *rims, *mats],
        [VMEM] * (3 + sides + len(mats)),
        [tall] * 4,
        limit=20,
    )
    other_rims = swap_sides(own_rims, sizes)

    *faces, low, high = run(
        bind(pack_back_x_kernel, sides, wide_x),
        "pack_back_x",
        [rim_message] * sides + [shape([(RIM + sides) * wide_y, depth])] * 2,
        [local, *own_rims, *other_rims],
        [VMEM] * (1 + 2 * sides),
    )
    back_xs = swap_ends(low, high, "gx", sizes)

    y_message = [shape([(ext_x + 2 + groups * sides) * RIM, depth])] * 2
    field_z, *back_ys = run(
        bind(fold_z_kernel, sides, wide_x),
        "fold_z",
        [field] + y_message,
        [local, *faces, *other_rims],
        [VMEM] * (1 + 2 * sides),
        flops=beside,
    )
    low, late_rims = lax.optimization_barrier((low, rims))
    scale_block = pltpu.VMEM((ext_x + 2, ext_y + 16, depth), F32)
    *weights, fixed = run(
        bind(weights_kernel, sizes, sides),
        "weights",
        [shape([ext_x + 1, ext_y, depth]), shape([ext_x, ext_y + 8, depth]), block, block, shape([1, LANES])],
        [axes_row, right, scale, *xs, *ys, *late_rims],
        [VMEM] * (7 + sides),
        [scale_block],
        flops=beside,
    )
    back_ys = run(
        bind(pack_back_y_kernel, sizes, sides, wide_x, wide_y),
        "pack_back_y",
        y_message,
        [*back_xs, *back_ys],
        [VMEM] * 4,
        aliases={2: 0, 3: 1},
    )
    back_ys = swap_ends(*back_ys, "gy", sizes)

    parts = [shape([ext_x + 2, ext_y + 16, depth]), shape([sides * groups * ext_y, LANES]), block]
    inner = run(
        bind(inner_kernel, sizes, sides, wide_x),
        "inner",
        parts + [shape([24, depth])],
        [right, field_z, *back_xs, *faces, *weights],
        [VMEM] * (8 + sides),
        flops=beside,
    )
    values, edges, applied, sums = run(
        bind(outer_kernel, sizes, sides, wide_x),
        "outer",
        parts + [shape([count, LANES])],
        [right, *back_ys, *weights, fixed, *inner],
        [VMEM] * 12,
        [pltpu.VMEM((24, depth), F32)],
        aliases={8: 0, 9: 1, 10: 2},
    )
    sums = lax.all_to_all(sums, MESH_AXES, 0, 0, tiled=True)

    held = pltpu.VMEM(right.shape, F32)
    wx, wy, _, z_weight = weights
    return tuple(
        run(
            bind(finish_kernel, sizes),
            "finish",
            [block] * 2,
            [sums, inverse, values, applied, wx, wy, z_weight, right],
            [VMEM] * 8,
            [held, held, pltpu.SemaphoreType.DMA((2, ext_x // 12))],
            out_specs=[ANY] * 2,
        )
    )


def solution(mesh):
    sizes = dict(mesh.shape)
    in_specs = (P(*MESH_AXES), P(*MESH_AXES), P(), P(), P(), P(), P(), P(), P(), P())
    out_specs = (P(*MESH_AXES), P(*MESH_AXES))
    return jax.shard_map(functools.partial(body, sizes), mesh=mesh, in_specs=in_specs, out_specs=out_specs, check_vma=False)
```

time: 78.3 us -> 63.3 us (0.81)
  waiting for transfers between devices: 25.8 us -> 9.12 us
  Pallas kernels: 22.9 us -> 17.4 us
  blocking collectives: 10.9 us -> 16.4 us
  starting transfers between devices: 15.3 us -> 19.2 us
  local copies, waits for them, and re-layouts: 2.46 us -> 0.05 us
    ppermute x8, waiting for transfers between devices: 24.2 us -> 6.63 us  [swap_ends(): received.append(lax.ppermute(message, axis, list(enumerate(partner))))]
    all_to_all x1, blocking collectives: 10.9 us -> 16.4 us  [body(): sums = lax.all_to_all(sums, MESH_AXES, 0, 0, tiled=True)]
    pallas_call x9 -> x14, Pallas kernels: 22.9 us -> 17.4 us  [call(): pl.pallas_call(placed, out_shape=outs, in_specs=spaces, out_specs=out_spe...]
    ppermute x8, starting transfers between devices: 15 us -> 18.9 us  [swap_ends(): received.append(lax.ppermute(message, axis, list(enumerate(partner))))]
    unnamed x24 -> x20, local copies, waits for them, and re-layouts: 2.38 us -> 0.05 us
    ppermute x2, waiting for transfers between devices: 1.56 us -> 2.5 us  [swap_sides(): return [lax.ppermute(messages[0], 'gz', [(0, 1), (1, 0)])]]
  transfers between devices with their start and end apart: 10 -> 10, of which waited for: 10 -> 6; matrix products, arithmetic and copies ran while one was open for 0% -> 0% of each run, Pallas kernels for 1% -> 7%
where the time goes in v2:
time: 63.3 us; the launch traced here: 63 us
  starting transfers between devices  19.2 us (30%)
  Pallas kernels  17.4 us (27%)
  blocking collectives  16.4 us (26%)
  waiting for transfers between devices  9.12 us (14%)
  between operations  0.83 us (1%)
    ppermute x8, starting transfers between devices, swap_ends(): received.append(lax.ppermute(message, axis, list(enumerate(partner))))  18.9 us
    pallas_call x14, Pallas kernels, call(): pl.pallas_call(placed, out_shape=outs, in_specs=spaces, out_specs=out_spe...  17.4 us
    all_to_all x1, blocking collectives, body(): sums = lax.all_to_all(sums, MESH_AXES, 0, 0, tiled=True)  16.4 us
    ppermute x8, waiting for transfers between devices, swap_ends(): received.append(lax.ppermute(message, axis, list(enumerate(partner))))  6.63 us
    ppermute x2, waiting for transfers between devices, swap_sides(): return [lax.ppermute(messages[0], 'gz', [(0, 1), (1, 0)])]  2.5 us
  transfers between devices with their start and end apart: 10, of which 6 were waited for; matrix products, arithmetic and copies ran while one was open for 0% of the time, Pallas kernels for 7%

profile of v2, /device:TPU:0, one launch (start us, length us, event | category | flops | bytes accessed | tf_op | source)
XLA Modules:
  0.0 63.0 jit_solution(894148631646547009)
XLA Ops:
  0.6 1.8 %pack_x.1 = (f32[5,48,128]{2,1,0:T(8,128)}, f32[5,48,128]{2,1,0:T(8,128)}) custom-call(f32[48,48,128]{2,1,0:T(8,128)} %refs_7_.1, bf16[48,48,128]{2,1,0:T(8,128)(2,1)} %refs_2_.3), custom_call_target="tpu_custom_call" | custom-call | bytes 2015232 | tf_op jit(solution)/shard_map/pack_x/pallas_call | solution.py:31
  2.5 3.1 %collective-permute-start = (f32[5,48,128]{2,1,0:T(8,128)}, f32[5,48,128]{2,1,0:T(8,128)S(1)}, u32[]{:S(2)}, u32[]{:S(2)}) collective-permute-start(f32[5,48,128]{2,1,0:T(8,128)} %get-tuple-element.51), channel_id=1, source_target_pairs={{0,8},{8,0},{16,24},{24,16},{1,9},{9,1},{17,25},{25,17},{2,10},{10... | collective-permute-start | bytes 368648 | tf_op jit(solution)/shard_map/ppermute | solution.py:90
  5.6 0.0 copy-start.8
  5.6 0.0 copy-start.9
  5.6 1.7 %collective-permute-start.1 = (f32[5,48,128]{2,1,0:T(8,128)}, f32[5,48,128]{2,1,0:T(8,128)S(1)}, u32[]{:S(2)}, u32[]{:S(2)}) collective-permute-start(f32[5,48,128]{2,1,0:T(8,128)} %get-tuple-element.52), channel_id=1, source_target_pairs={{0,0},{8,16},{16,8},{24,24},{1,1},{9,17},{17,9},{25,25},{2,2},{10,... | collective-permute-start | bytes 368648 | tf_op jit(solution)/shard_map/ppermute | solution.py:90
  7.3 0.1 pack_y_own.1
  7.4 0.3 prepare.1
  7.8 1.3 %collective-permute-done.refs_0_.refs_2_.refs_3_ = f32[5,48,128]{2,1,0:T(8,128)S(1)} collective-permute-done((f32[5,48,128]{2,1,0:T(8,128)}, f32[5,48,128]{2,1,0:T(8,128)S(1)}, u32[]{:S(2)}, u32[]{:S(2)}) %collective-permute-start) | collective-permute-done | bytes 122912 | tf_op jit(solution)/shard_map/ppermute | solution.py:90
  9.1 1.7 %collective-permute-start.2 = (f32[272,128]{1,0:T(8,128)S(1)}, f32[272,128]{1,0:T(8,128)S(1)}, u32[]{:S(2)}, u32[]{:S(2)}) collective-permute-start(f32[272,128]{1,0:T(8,128)S(1)} %get-tuple-element.64), channel_id=1, source_target_pairs={{0,2},{2,0},{4,6},{6,4},{1,3},{3,1},{5,7},{7,5},{8,10},{10,8},{12,... | collective-permute-start | bytes 417800 | tf_op jit(solution)/shard_map/ppermute | solution.py:90
  10.8 0.7 %collective-permute-start.3 = (f32[272,128]{1,0:T(8,128)S(1)}, f32[272,128]{1,0:T(8,128)S(1)}, u32[]{:S(2)}, u32[]{:S(2)}) collective-permute-start(f32[272,128]{1,0:T(8,128)S(1)} %get-tuple-element.65), channel_id=1, source_target_pairs={{0,0},{2,4},{4,2},{6,6},{1,1},{3,5},{5,3},{7,7},{8,8},{10,12},{12,... | collective-permute-start | bytes 417800 | tf_op jit(solution)/shard_map/ppermute | solution.py:90
  11.5 0.5 extend_own.1
  12.0 0.0 copy-start.3
  12.1 2.2 %collective-permute-done.2.refs_0_.refs_5_ = f32[272,128]{1,0:T(8,128)S(1)} collective-permute-done((f32[272,128]{1,0:T(8,128)S(1)}, f32[272,128]{1,0:T(8,128)S(1)}, u32[]{:S(2)}, u32[]{:S(2)}) %collective-permute-start.2) | collective-permute-done | bytes 139296 | tf_op jit(solution)/shard_map/ppermute | solution.py:90
  14.2 0.2 extend_rest.1
  14.5 0.1 collective-permute-start.4
  14.6 1.3 %collective-permute-done.4.refs_3_.refs_7_ = f32[224,128]{1,0:T(8,128)S(1)} collective-permute-done((f32[224,128]{1,0:T(8,128)S(1)}, f32[224,128]{1,0:T(8,128)S(1)}, u32[]{:S(2)}, u32[]{:S(2)}) %collective-permute-start.4) | collective-permute-done | bytes 114720 | tf_op jit(solution)/shard_map/ppermute | solution.py:77
  15.9 7.1 %solve.1 = (f32[3136,128]{1,0:T(8,128)S(1)}, f32[224,128]{1,0:T(8,128)S(1)}) custom-call(f32[1,3]{1,0:T(1,128)S(1)} %bitcast.12, f32[1,56]{1,0:T(1,128)S(1)} %bitcast.10, f32[3136,128]{1,0:T(8,128)S(1)} %get-tuple-element.68.refs_2_, f32[224,128]{1,0:T(8,128)S(1)} %collective-permute-done.4.refs_3_.refs_7_, bf16[64,192]{1,0:T(8,128)(2,1)S(1)} %get-tuple-element.70.refs_4_, ...), custom_call_target="tpu_custom_call" | custom-call | bytes 4223212 | tf_op jit(solution)/shard_map/solve/pallas_call | solution.py:31
  23.0 0.2 collective-permute-start.5
  23.2 1.2 %collective-permute-done.5.refs_2_ = f32[224,128]{1,0:T(8,128)S(1)} collective-permute-done((f32[224,128]{1,0:T(8,128)S(1)}, f32[224,128]{1,0:T(8,128)S(1)}, u32[]{:S(2)}, u32[]{:S(2)}) %collective-permute-start.5) | collective-permute-done | bytes 114720 | tf_op jit(solution)/shard_map/ppermute | solution.py:77
  24.4 0.2 pack_back_x.1
  24.6 5.0 %collective-permute-start.6 = (f32[336,128]{1,0:T(8,128)S(1)}, f32[336,128]{1,0:T(8,128)S(1)}, u32[]{:S(2)}, u32[]{:S(2)}) collective-permute-start(f32[336,128]{1,0:T(8,128)S(1)} %get-tuple-element.79), channel_id=1, source_target_pairs={{0,8},{8,0},{16,24},{24,16},{1,9},{9,1},{17,25},{25,17},{2,10},{10... | collective-permute-start | bytes 516104 | tf_op jit(solution)/shard_map/ppermute | solution.py:90
  29.6 0.7 %collective-permute-start.7 = (f32[336,128]{1,0:T(8,128)S(1)}, f32[336,128]{1,0:T(8,128)S(1)}, u32[]{:S(2)}, u32[]{:S(2)}) collective-permute-start(f32[336,128]{1,0:T(8,128)S(1)} %get-tuple-element.80), channel_id=1, source_target_pairs={{0,0},{8,16},{16,8},{24,24},{1,1},{9,17},{17,9},{25,25},{2,2},{10,... | collective-permute-start | bytes 516104 | tf_op jit(solution)/shard_map/ppermute | solution.py:90
  30.3 0.5 fold_z.1
  30.8 1.2 %weights.1 = (f32[49,48,128]{2,1,0:T(8,128)S(1)}, f32[48,56,128]{2,1,0:T(8,128)S(1)}, f32[48,48,128]{2,1,0:T(8,128)S(1)}, f32[48,48,128]{2,1,0:T(8,128)S(1)}, f32[1,128]{1,0:T(1,128)S(1)}) custom-call(f32[1,3]{1,0:T(1,128)S(1)} %bitcast.13, f32[48,48,128]{2,1,0:T(8,128)S(1)} %copy-done, bf16[48,48,128]{2,1,0:T(8,128)(2,1)S(1)} %copy-done.1, ...), custom_call_target="tpu_custom_call" | custom-call | flops 2000000000 | bytes 7348748 | tf_op jit(solution)/shard_map/weights/pallas_call | solution.py:31
  32.0 2.3 %collective-permute-done.6.refs_0_.refs_2_ = f32[336,128]{1,0:T(8,128)S(1)} collective-permute-done((f32[336,128]{1,0:T(8,128)S(1)}, f32[336,128]{1,0:T(8,128)S(1)}, u32[]{:S(2)}, u32[]{:S(2)}) %collective-permute-start.6) | collective-permute-done | bytes 172064 | tf_op jit(solution)/shard_map/ppermute | solution.py:90
  34.3 5.5 %collective-permute-start.8 = (f32[270,128]{1,0:T(8,128)S(1)}, f32[270,128]{1,0:T(8,128)S(1)}, u32[]{:S(2)}, u32[]{:S(2)}) collective-permute-start(f32[270,128]{1,0:T(8,128)S(1)} %get-tuple-element.84), channel_id=1, source_target_pairs={{0,2},{2,0},{4,6},{6,4},{1,3},{3,1},{5,7},{7,5},{8,10},{10,8},{12,... | collective-permute-start | bytes 414728 | tf_op jit(solution)/shard_map/ppermute | solution.py:90
  39.8 0.7 %collective-permute-start.9 = (f32[270,128]{1,0:T(8,128)S(1)}, f32[270,128]{1,0:T(8,128)S(1)}, u32[]{:S(2)}, u32[]{:S(2)}) collective-permute-start(f32[270,128]{1,0:T(8,128)S(1)} %get-tuple-element.85), channel_id=1, source_target_pairs={{0,0},{2,4},{4,2},{6,6},{1,1},{3,5},{5,3},{7,7},{8,8},{10,12},{12,... | collective-permute-start | bytes 414728 | tf_op jit(solution)/shard_map/ppermute | solution.py:90
  40.5 2.0 %inner.1 = (f32[50,64,128]{2,1,0:T(8,128)S(1)}, f32[192,128]{1,0:T(8,128)S(1)}, f32[48,48,128]{2,1,0:T(8,128)S(1)}, f32[24,128]{1,0:T(8,128)S(1)}) custom-call(f32[48,48,128]{2,1,0:T(8,128)S(1)} %copy-done, f32[3136,128]{1,0:T(8,128)S(1)} %get-tuple-element.92.refs_1_, f32[336,128]{1,0:T(8,128)S(1)} %collective-permute-done.6.refs_0_.refs_2_, ...), custom_call_target="tpu_custom_call" | custom-call | flops 2000000000 | bytes 11112448 | tf_op jit(solution)/shard_map/inner/pallas_call | solution.py:31
  42.5 0.8 %collective-permute-done.8.refs_1_ = f32[270,128]{1,0:T(8,128)S(1)} collective-permute-done((f32[270,128]{1,0:T(8,128)S(1)}, f32[270,128]{1,0:T(8,128)S(1)}, u32[]{:S(2)}, u32[]{:S(2)}) %collective-permute-start.8) | collective-permute-done | bytes 138272 | tf_op jit(solution)/shard_map/ppermute | solution.py:90
  43.3 1.0 %outer.1 = (f32[50,64,128]{2,1,0:T(8,128)S(1)}, f32[192,128]{1,0:T(8,128)S(1)}, f32[48,48,128]{2,1,0:T(8,128)S(1)}, f32[32,128]{1,0:T(8,128)S(1)}) custom-call(f32[48,48,128]{2,1,0:T(8,128)S(1)} %copy-done, f32[270,128]{1,0:T(8,128)S(1)} %collective-permute-done.8.refs_1_, ...), custom_call_target="tpu_custom_call", output_to_operand_aliasing={{0}: (8, {}), {1}: (9, {}), {2}: (10, {})} | custom-call | bytes 12257792 | tf_op jit(solution)/shard_map/outer/pallas_call | solution.py:31
  44.3 16.4 %all_to_all.11 = f32[32,1,128]{2,1,0:T(1,128)S(1)} all-to-all(f32[32,1,128]{2,1,0:T(1,128)S(1)} %bitcast.9), channel_id=1, replica_groups=mesh['gx'=4,'gy'=4,'gz'=2] {'gx','gy','gz'}, dimensions={0} | all-to-all | bytes 32768 | tf_op jit(solution)/shard_map/all_to_all | solution.py:832
  60.7 2.3 %finish.1 = (f32[48,48,128]{2,1,0:T(8,128)}, f32[48,48,128]{2,1,0:T(8,128)}) custom-call(f32[32,128]{1,0:T(8,128)S(1)} %bitcast.8, f32[16,16]{1,0:T(8,128)S(1)} %copy-done.2, f32[50,64,128]{2,1,0:T(8,128)S(1)} %get-tuple-element.98.refs_2_, f32[48,48,128]{2,1,0:T(8,128)S(1)} %get-tuple-element.99.refs_3_, ...), custom_call_target="tpu_custom_call" | custom-call | bytes 10134528 | tf_op jit(solution)/shard_map/finish/pallas_call | solution.py:31
  (23 shorter events, 0.1 us)
Async XLA Ops:
  0.6 6.7 %copy-start = (f32[48,48,128]{2,1,0:T(8,128)S(1)}, f32[48,48,128]{2,1,0:T(8,128)}, u32[]{:S(2)}) copy-start(f32[48,48,128]{2,1,0:T(8,128)} %refs_7_.1) | copy-start | bytes 3538948
  0.6 6.7 %copy-start.1 = (bf16[48,48,128]{2,1,0:T(8,128)(2,1)S(1)}, bf16[48,48,128]{2,1,0:T(8,128)(2,1)}, u32[]{:S(2)}) copy-start(bf16[48,48,128]{2,1,0:T(8,128)(2,1)} %refs_2_.3) | copy-start | bytes 1769476
  2.5 6.6 %collective-permute-start = (f32[5,48,128]{2,1,0:T(8,128)}, f32[5,48,128]{2,1,0:T(8,128)S(1)}, u32[]{:S(2)}, u32[]{:S(2)}) collective-permute-start(f32[5,48,128]{2,1,0:T(8,128)} %get-tuple-element.51), channel_id=1, source_target_pairs={{0,8},{8,0},{16,24},{24,16},{1,9},{9,1},{17,25},{25,17},{2,10},{10... | collective-permute-start | bytes 368648 | tf_op jit(solution)/shard_map/ppermute | solution.py:90
  5.6 1.8 %copy-start.4 = (f32[3]{0:T(128)S(1)}, f32[3]{0:T(128)}, u32[]{:S(2)}) copy-start(f32[3]{0:T(128)} %param.12) | copy-start | bytes 40
  5.6 1.8 %copy-start.5 = (f32[72,72]{1,0:T(8,128)S(1)}, f32[72,72]{1,0:T(8,128)}, u32[]{:S(2)}) copy-start(f32[72,72]{1,0:T(8,128)} %refs_3_.1) | copy-start | bytes 62212
  5.6 1.8 %copy-start.6 = (f32[56,56]{1,0:T(8,128)S(1)}, f32[56,56]{1,0:T(8,128)}, u32[]{:S(2)}) copy-start(f32[56,56]{1,0:T(8,128)} %refs_1_.8) | copy-start | bytes 37636
  5.6 1.8 %copy-start.7 = (f32[56,56]{1,0:T(8,128)S(1)}, f32[56,56]{1,0:T(8,128)}, u32[]{:S(2)}) copy-start(f32[56,56]{1,0:T(8,128)} %refs_2_.2) | copy-start | bytes 37636
  5.6 1.8 %copy-start.8 = (f32[56]{0:T(128)S(1)}, f32[56]{0:T(128)}, u32[]{:S(2)}) copy-start(f32[56]{0:T(128)} %param.17) | copy-start | bytes 676
  5.6 1.8 %copy-start.9 = (f32[72]{0:T(128)S(1)}, f32[72]{0:T(128)}, u32[]{:S(2)}) copy-start(f32[72]{0:T(128)} %param.18) | copy-start | bytes 868
  5.6 3.5 %collective-permute-start.1 = (f32[5,48,128]{2,1,0:T(8,128)}, f32[5,48,128]{2,1,0:T(8,128)S(1)}, u32[]{:S(2)}, u32[]{:S(2)}) collective-permute-start(f32[5,48,128]{2,1,0:T(8,128)} %get-tuple-element.52), channel_id=1, source_target_pairs={{0,0},{8,16},{16,8},{24,24},{1,1},{9,17},{17,9},{25,25},{2,2},{10,... | collective-permute-start | bytes 368648 | tf_op jit(solution)/shard_map/ppermute | solution.py:90
  9.1 5.1 %collective-permute-start.2 = (f32[272,128]{1,0:T(8,128)S(1)}, f32[272,128]{1,0:T(8,128)S(1)}, u32[]{:S(2)}, u32[]{:S(2)}) collective-permute-start(f32[272,128]{1,0:T(8,128)S(1)} %get-tuple-element.64), channel_id=1, source_target_pairs={{0,2},{2,0},{4,6},{6,4},{1,3},{3,1},{5,7},{7,5},{8,10},{10,8},{12,... | collective-permute-start | bytes 417800 | tf_op jit(solution)/shard_map/ppermute | solution.py:90
  10.8 3.4 %collective-permute-start.3 = (f32[272,128]{1,0:T(8,128)S(1)}, f32[272,128]{1,0:T(8,128)S(1)}, u32[]{:S(2)}, u32[]{:S(2)}) collective-permute-start(f32[272,128]{1,0:T(8,128)S(1)} %get-tuple-element.65), channel_id=1, source_target_pairs={{0,0},{2,4},{4,2},{6,6},{1,1},{3,5},{5,3},{7,7},{8,8},{10,12},{12,... | collective-permute-start | bytes 417800 | tf_op jit(solution)/shard_map/ppermute | solution.py:90
  12.0 3.8 %copy-start.3 = (f32[56]{0:T(128)S(1)}, f32[56]{0:T(128)}, u32[]{:S(2)}) copy-start(f32[56]{0:T(128)} %param.16) | copy-start | bytes 676
  14.5 1.4 %collective-permute-start.4 = (f32[224,128]{1,0:T(8,128)S(1)}, f32[224,128]{1,0:T(8,128)S(1)}, u32[]{:S(2)}, u32[]{:S(2)}) collective-permute-start(f32[224,128]{1,0:T(8,128)S(1)} %get-tuple-element.69), channel_id=1, source_target_pairs={{0,1},{1,0},{2,3},{3,2},{4,5},{5,4},{6,7},{7,6},{8,9},{9,8},{10,11... | collective-permute-start | bytes 344072 | tf_op jit(solution)/shard_map/ppermute | solution.py:77
  23.0 1.4 %collective-permute-start.5 = (f32[224,128]{1,0:T(8,128)S(1)}, f32[224,128]{1,0:T(8,128)S(1)}, u32[]{:S(2)}, u32[]{:S(2)}) collective-permute-start(f32[224,128]{1,0:T(8,128)S(1)} %get-tuple-element.78.refs_1_), channel_id=1, source_target_pairs={{0,1},{1,0},{2,3},{3,2},{4,5},{5,4},{6,7},{7,6},{8,9},{9,8},{10,11... | collective-permute-start | bytes 344072 | tf_op jit(solution)/shard_map/ppermute | solution.py:77
  24.6 9.7 %collective-permute-start.6 = (f32[336,128]{1,0:T(8,128)S(1)}, f32[336,128]{1,0:T(8,128)S(1)}, u32[]{:S(2)}, u32[]{:S(2)}) collective-permute-start(f32[336,128]{1,0:T(8,128)S(1)} %get-tuple-element.79), channel_id=1, source_target_pairs={{0,8},{8,0},{16,24},{24,16},{1,9},{9,1},{17,25},{25,17},{2,10},{10... | collective-permute-start | bytes 516104 | tf_op jit(solution)/shard_map/ppermute | solution.py:90
  29.6 2.4 %collective-permute-start.7 = (f32[336,128]{1,0:T(8,128)S(1)}, f32[336,128]{1,0:T(8,128)S(1)}, u32[]{:S(2)}, u32[]{:S(2)}) collective-permute-start(f32[336,128]{1,0:T(8,128)S(1)} %get-tuple-element.80), channel_id=1, source_target_pairs={{0,0},{8,16},{16,8},{24,24},{1,1},{9,17},{17,9},{25,25},{2,2},{10,... | collective-permute-start | bytes 516104 | tf_op jit(solution)/shard_map/ppermute | solution.py:90
  34.3 9.0 %collective-permute-start.8 = (f32[270,128]{1,0:T(8,128)S(1)}, f32[270,128]{1,0:T(8,128)S(1)}, u32[]{:S(2)}, u32[]{:S(2)}) collective-permute-start(f32[270,128]{1,0:T(8,128)S(1)} %get-tuple-element.84), channel_id=1, source_target_pairs={{0,2},{2,0},{4,6},{6,4},{1,3},{3,1},{5,7},{7,5},{8,10},{10,8},{12,... | collective-permute-start | bytes 414728 | tf_op jit(solution)/shard_map/ppermute | solution.py:90
  39.8 3.5 %collective-permute-start.9 = (f32[270,128]{1,0:T(8,128)S(1)}, f32[270,128]{1,0:T(8,128)S(1)}, u32[]{:S(2)}, u32[]{:S(2)}) collective-permute-start(f32[270,128]{1,0:T(8,128)S(1)} %get-tuple-element.85), channel_id=1, source_target_pairs={{0,0},{2,4},{4,2},{6,6},{1,1},{3,5},{5,3},{7,7},{8,8},{10,12},{12,... | collective-permute-start | bytes 414728 | tf_op jit(solution)/shard_map/ppermute | solution.py:90
  43.3 17.4 %copy-start.2 = (f32[16,16]{1,0:T(8,128)S(1)}, f32[16,16]{1,0:T(8,128)}, u32[]{:S(2)}) copy-start(f32[16,16]{1,0:T(8,128)} %refs_1_.11) | copy-start | bytes 3076

commit v3 on v2

v3 whole, which is shorter than its diff:
```python
import functools

import jax
import jax.numpy as jnp
from jax import lax
from jax.experimental import pallas as pl
from jax.experimental.pallas import tpu as pltpu
from jax.sharding import PartitionSpec as P

SZ = 64
OV = 4
RIM = OV + 1
LANES = 128
SLOT = 8
GROUP = LANES // SLOT
F32 = jnp.float32
BF16 = jnp.bfloat16
MESH_AXES = ("gx", "gy", "gz")

VMEM = pl.BlockSpec(memory_space=pltpu.VMEM)
ANY = pl.BlockSpec(memory_space=pl.ANY)
HBM = pl.BlockSpec(memory_space=pltpu.HBM)


def call(sizes, kernel, name, outs, args, spaces, scratch=(), limit=8, out_specs=None, aliases=None, flops=0):
    size = sum(o.size * o.dtype.itemsize for o in outs) + sum(a.size * a.dtype.itemsize for a in args)

    def placed(*refs):
        return kernel(place_values(sizes), *refs)

    return pl.pallas_call(
        placed,
        out_shape=outs,
        in_specs=spaces,
        out_specs=out_specs or [VMEM] * len(outs),
        scratch_shapes=list(scratch),
        input_output_aliases=aliases or {},
        name=name,
        compiler_params=pltpu.CompilerParams(vmem_limit_bytes=limit * 2**20),
        cost_estimate=pl.CostEstimate(flops=flops, bytes_accessed=size, transcendentals=0),
    )(*args)


def shape(dims, dtype=F32):
    return jax.ShapeDtypeStruct(tuple(dims), dtype)


def halves(value):
    high = value.astype(BF16)
    return high, (value - high.astype(F32)).astype(BF16)


def dot(left, right):
    return jnp.dot(left, right, preferred_element_type=F32)


def iota(dims, axis):
    return lax.broadcasted_iota(jnp.int32, dims, axis)


IX, IY, IZ, SIDE = 0, 1, 2, 3


def place_values(sizes):
    ix, iy, iz = (lax.axis_index(a) for a in MESH_AXES)
    nz = sizes["gz"]
    if nz == 2:
        sides = [1 - iz, 1]
    else:
        sides = [1, jnp.where(iz < nz - 1, 1, 0), 0, jnp.where(iz > 0, 1, 0)]
    return [ix, iy, iz] + sides


def swap_sides(messages, sizes):
    count = sizes["gz"]
    if count == 2:
        return [lax.ppermute(messages[0], "gz", [(0, 1), (1, 0)])]
    up = [(i, (i + 1) % count) for i in range(count)]
    down = [((i + 1) % count, i) for i in range(count)]
    return [lax.ppermute(messages[1], "gz", down), lax.ppermute(messages[0], "gz", up)]


def swap_ends(first, second, axis, sizes):
    count = sizes[axis]
    received = []
    for message, start in ((first, 0), (second, 1)):
        partner = list(range(count))
        for i in range(start, count - 1, 2):
            partner[i], partner[i + 1] = i + 1, i
        received.append(lax.ppermute(message, axis, list(enumerate(partner))))
    return received


def is_even(place, axis):
    return lax.rem(place[axis], 2) == 0


def from_ends(place, axis, sizes, first, second):
    even = is_even(place, axis)
    inside_low = place[axis] > 0
    inside_high = place[axis] < sizes[MESH_AXES[axis]] - 1

    def low(at):
        return jnp.where(inside_low, jnp.where(even, second[at], first[at]), 0.0)

    def high(at):
        return jnp.where(inside_high, jnp.where(even, first[at], second[at]), 0.0)

    return low, high


def prepare_kernel(sides, cells, place, axes, xv, yv, zv, y_row, z_row, inverse, fx, bx, fy, by, wz, bz, den, spread, pad, wide, rows):
    ez = zv.shape[0]
    depth = wz.shape[0] // 4

    def stacked(value, out):
        size = out.shape[1] // 3
        high, low = (part.astype(F32) for part in halves(value[: LANES // 2]))
        spread = jnp.concatenate([high, jnp.zeros_like(high)], axis=1)
        wide_low = jnp.concatenate([low, jnp.zeros_like(low)], axis=1)
        out[...] = (spread + pltpu.roll(spread, size, 1) + pltpu.roll(wide_low, 2 * size, 1)).astype(BF16)[:, : 3 * size]

    for vectors, forward, back in ((xv, fx, bx), (yv, fy, by)):
        size = vectors.shape[0]
        pad[...] = jnp.zeros_like(pad)
        pad[0:size, 0:size] = vectors[...]
        stacked(pad[...], back)
        if vectors is yv:
            pad[0 : size - OV, 0:size] = vectors[OV:size]
            pad[size - OV : size, 0:size] = vectors[0:OV]
        stacked(pad[...].T, forward)

    wide[...] = jnp.zeros_like(wide)
    wide[0:ez, 0:ez] = zv[...]
    wide[SZ : SZ + ez, LANES : LANES + ez] = zv[...]
    middle = wide[OV : OV + depth]
    high, low = halves(middle)
    wz[0:depth] = high
    wz[depth : 2 * depth] = high
    wz[2 * depth : 3 * depth] = low
    rows[...] = jnp.zeros_like(rows)
    for side in range(sides):
        is_high = place[SIDE + 2 * side] > 0
        for k in range(OV):
            top, bottom = OV + depth + k, k
            row = jnp.where(is_high, wide[top : top + 1], wide[bottom : bottom + 1])
            row_high, row_low = halves(row)
            at = 3 * SLOT * side + k
            rows[at : at + 1] = row_high.astype(F32)
            rows[at + SLOT : at + SLOT + 1] = row_high.astype(F32)
            rows[at + 2 * SLOT : at + 2 * SLOT + 1] = row_low.astype(F32)
    wz[3 * depth :] = rows[...].astype(BF16)

    rows[...] = jnp.zeros_like(rows)
    for side in range(sides):
        is_high = place[SIDE + 2 * side] > 0
        for k in range(RIM):
            top, bottom = OV + depth - 1 + k, k
            rows[SLOT * side + k : SLOT * side + k + 1] = jnp.where(is_high, wide[top : top + 1], wide[bottom : bottom + 1])
    across = 2 * LANES
    for at, part in ((0, middle), (LANES, rows[...])):
        turned = jnp.concatenate([part[:, 0:LANES].T, part[:, LANES:].T], axis=0)
        high, low = halves(turned)
        bz[0:across, at : at + LANES] = high
        bz[across : 2 * across, at : at + LANES] = high
        bz[2 * across :, at : at + LANES] = low

    ey = yv.shape[0]
    diagonal = iota((ey, ey), 0) == iota((ey, ey), 1)
    y_column = jnp.sum(jnp.where(diagonal, y_row[...], 0.0), axis=1, keepdims=True)
    pad[...] = jnp.ones_like(pad)
    pad[0:1, 0:ez] = axes[:, 2:3] * z_row[...]
    den[...] = axes[:, 1:2] * y_column + pad[0:1]
    count, blocks = spread.shape[0], inverse.shape[0]
    member = jnp.where(iota((count, blocks), 0) // 2 == iota((count, blocks), 1), 1.0, 0.0)
    from_block = jnp.where(iota((blocks, count), 0) == iota((blocks, count), 1) // 2, 1.0, 0.0)
    exact = functools.partial(jnp.dot, preferred_element_type=F32, precision=lax.Precision.HIGHEST)
    spread[...] = exact(exact(member, inverse[...]), from_block) / cells


def pack_y_own_kernel(place, right, scale, first, second):
    ext_x, ext_y, depth = right.shape
    even = is_even(place, IY)
    base = (ext_x + 2 * OV) * OV
    for x in range(ext_x):
        low, high = right[x, 0:OV], right[x, ext_y - OV : ext_y]
        at = (x + OV) * OV
        first[at : at + OV] = jnp.where(even, high, low)
        second[at : at + OV] = jnp.where(even, low, high)
        low, high = scale[x, 0:16].astype(F32)[0:1], scale[x, ext_y - 16 : ext_y].astype(F32)[15:16]
        first[base + x : base + x + 1] = jnp.where(even, high, low)
        second[base + x : base + x + 1] = jnp.where(even, low, high)


def pack_y_rest_kernel(sizes, sides, wide_x, place, x_first, x_second, *refs):
    rims, (first, second) = refs[:sides], refs[sides + 2 :]
    ext_y = x_first.shape[1]
    even = is_even(place, IY)
    x_low, x_high = from_ends(place, IX, sizes, x_first, x_second)
    last = (wide_x - 2 * OV) * OV
    groups = (wide_x + GROUP - 1) // GROUP
    for side in range(sides):
        for group in range(groups):
            start = group * ext_y
            low, high = rims[side][start : start + OV], rims[side][start + ext_y - OV : start + ext_y]
            at = wide_x * OV + wide_x - 2 * OV + (side * groups + group) * OV
            first[at : at + OV] = jnp.where(even, high, low)
            second[at : at + OV] = jnp.where(even, low, high)
    for t in range(OV):
        for source, at in ((x_low, t * OV), (x_high, last + OV * OV + t * OV)):
            low, high = source((t, slice(0, OV))), source((t, slice(ext_y - OV, ext_y)))
            first[at : at + OV] = jnp.where(even, high, low)
            second[at : at + OV] = jnp.where(even, low, high)


def pack_z_kernel(planes, faces, sides, place, *refs):
    if faces:
        right, scale, *messages = refs
        sources = {a + OV: right.at[a] for a in range(right.shape[0])}
        ext_x, ext_y, depth = right.shape
    else:
        x_first, x_second, *messages = refs
        messages = messages[sides:]
        low, high = from_ends(place, IX, planes, x_first, x_second)
        ext_y, depth = x_first.shape[1:]
        ext_x = messages[0].shape[0] // ext_y * GROUP - 2 * OV
        ext_x = ext_x // GROUP * GROUP
        sources = {}
    lane = iota((ext_y, LANES), 1)
    for side in range(sides):
        is_high = place[SIDE + 2 * side] > 0
        start, face = jnp.where(is_high, depth - OV, 0), jnp.where(is_high, depth - 1, 0)
        for group in range(messages[side].shape[0] // ext_y):
            at = slice(group * ext_y, (group + 1) * ext_y)
            total = jnp.zeros((ext_y, LANES), F32) if faces else messages[side][at]
            for q in range(GROUP):
                a = group * GROUP + q
                if faces and a in sources:
                    cells = sources[a][...]
                elif not faces and a < OV:
                    cells = low(a)
                elif not faces and ext_x + OV <= a < ext_x + 2 * OV:
                    cells = high(a - OV - ext_x)
                else:
                    cells = None
                if cells is not None:
                    moved = pltpu.roll(cells, lax.rem(SLOT * q + depth - start, depth), 1)
                    total = jnp.where((lane >= SLOT * q) & (lane < SLOT * q + OV), moved, total)
                if faces and a < ext_x:
                    moved = pltpu.roll(scale[a].astype(F32), lax.rem(SLOT * q + OV + depth - face, depth), 1)
                    total = jnp.where(lane == SLOT * q + OV, moved, total)
            messages[side][at] = total


def rim_columns(place, sides, values, q):
    lane = iota(values[0].shape, 1)
    piece = jnp.zeros(values[0].shape, F32)
    for side in range(sides):
        value = jnp.where((lane // SLOT == q) & (place[SIDE + 2 * side + 1] > 0), values[side], 0.0)
        high = value.astype(BF16).astype(F32)
        at = LANES - SLOT * q + 3 * SLOT * side
        for number, part in enumerate((high, value - high, high)):
            shift = (at + number * SLOT) % LANES
            piece = piece + (pltpu.roll(part, shift, 1) if shift else part)
    return piece.astype(BF16)


def z_forward(cells, rims, wz):
    high, low = halves(cells)
    return dot(jnp.concatenate([high, low, high, rims], axis=1), wz[...])


def along(matrix, pair):
    value = jnp.concatenate(pair, axis=1)
    high = value.astype(BF16).astype(F32)
    stack = jnp.concatenate([high, value - high, high], axis=0).astype(BF16)
    return dot(matrix[...], stack)[0 : value.shape[0]]


def strided(pair, at, count, stride):
    return [ref[pl.ds(at, count, stride=stride), :] for ref in pair]


def solve_own_kernel(sizes, sides, place, right, x_first, x_second, *refs):
    received, (fx, wz, out_a, out_b, first_a, first_b) = refs[:sides], refs[sides:]
    ext_x, ext_y, depth = right.shape
    wide = ext_x + 2 * OV
    low, high = from_ends(place, IX, sizes, x_first, x_second)
    batch = 8
    for start in range(0, wide, batch):
        cells, rims = [], []
        for a in range(start, start + batch):
            if a < OV:
                cells.append(low(a))
            elif a < ext_x + OV:
                cells.append(right[a - OV])
            else:
                cells.append(high(a - OV - ext_x))
            at = slice(a // GROUP * ext_y, (a // GROUP + 1) * ext_y)
            rims.append(rim_columns(place, sides, [ref[at] for ref in received], a % GROUP))
        out = z_forward(jnp.concatenate(cells, axis=0), jnp.concatenate(rims, axis=0), wz)
        block = pl.ds(start * ext_y, batch * ext_y)
        first_a[block] = out[:, 0:LANES]
        first_b[block] = out[:, LANES:]
    for y in range(ext_y):
        out = along(fx, strided((first_a, first_b), y, wide, ext_y))
        out_a[y * wide : (y + 1) * wide] = out[:, 0:LANES]
        out_b[y * wide : (y + 1) * wide] = out[:, LANES:]


def solve_rest_kernel(sizes, sides, place, axes, x_values, scale, y_first, y_second, own_a, own_b, *refs):
    fx, bx, fy, by, wz, bz, den, back_a, back_b, first, second = refs[:11]
    edge_a, edge_b, halo_a, halo_b, mode_a, mode_b = refs[11:]
    wide = x_values.shape[1]
    rows = back_a.shape[0]
    wide_y = rows // wide
    ext_y = wide_y - 2 * OV
    groups = (wide + GROUP - 1) // GROUP
    low, high = from_ends(place, IY, sizes, y_first, y_second)
    both = []
    for side in range(sides):
        values = []
        for group in range(groups):
            at = wide * OV + wide - 2 * OV + (side * groups + group) * OV
            values.append(jnp.concatenate([high(slice(at, at + OV)), low(slice(at, at + OV))], axis=0))
        both.append(values)
    cells, rims = [], []
    for a in range(wide):
        part = slice(a * OV, (a + 1) * OV)
        cells.append(jnp.concatenate([high(part), low(part)], axis=0))
        rims.append(rim_columns(place, sides, [values[a // GROUP] for values in both], a % GROUP))
    out = z_forward(jnp.concatenate(cells, axis=0), jnp.concatenate(rims, axis=0), wz)
    edge_a[...] = out[:, 0:LANES]
    edge_b[...] = out[:, LANES:]
    for t in range(2 * OV):
        out = along(fx, strided((edge_a, edge_b), t, wide, 2 * OV))
        halo_a[t * wide : (t + 1) * wide] = out[:, 0:LANES]
        halo_b[t * wide : (t + 1) * wide] = out[:, LANES:]
    for i in range(wide):
        pair = []
        for inside, outside in ((own_a, halo_a), (own_b, halo_b)):
            parts = strided((inside,), i, ext_y, wide) + strided((outside,), i, 2 * OV, wide)
            pair.append(jnp.concatenate(parts, axis=0))
        out = along(fy, pair)
        inverse = 1.0 / (axes[:, 0:1] * x_values[:, i : i + 1] + den[...])
        out = along(by, [out[:, 0:LANES] * inverse, out[:, LANES:] * inverse])
        mode_a[pl.ds(i * wide_y, wide_y)] = out[:, 0:LANES]
        mode_b[pl.ds(i * wide_y, wide_y)] = out[:, LANES:]
    for y in range(wide_y):
        out = along(bx, strided((mode_a, mode_b), y, wide, wide_y))
        back_a[pl.ds(y, wide, stride=wide_y), :] = out[:, 0:LANES]
        back_b[pl.ds(y, wide, stride=wide_y), :] = out[:, LANES:]
    even = is_even(place, IX)
    ends = RIM * wide_y
    low, low_rims = z_back(sides, wide_y, back_a, back_b, bz, 0, RIM)
    high, high_rims = z_back(sides, wide_y, back_a, back_b, bz, wide - RIM, RIM)
    first[0:ends] = jnp.where(even, high, low)
    second[0:ends] = jnp.where(even, low, high)
    for side in range(sides):
        low = sum(low_rims[side].values())
        high = sum(high_rims[side].values())
        at = ends + side * wide_y
        first[at : at + wide_y] = jnp.where(even, high, low)
        second[at : at + wide_y] = jnp.where(even, low, high)
    low, high = scale[0].astype(F32), scale[scale.shape[0] - 1].astype(F32)
    at = ends + sides * wide_y
    first[at : at + ext_y] = jnp.where(even, high, low)
    second[at : at + ext_y] = jnp.where(even, low, high)


def z_back(sides, wide_y, back_a, back_b, bz, start, count):
    lane = iota((wide_y, LANES), 1)
    block = pl.ds(start * wide_y, count * wide_y)
    high_a, low_a = halves(back_a[block])
    high_b, low_b = halves(back_b[block])
    out = dot(jnp.concatenate([high_a, high_b, low_a, low_b, high_a, high_b], axis=1), bz[...])
    rims = [{} for _ in range(sides)]
    for a in range(start, start + count):
        group, q = a // GROUP, a % GROUP
        value = out[(a - start) * wide_y : (a - start + 1) * wide_y, LANES:]
        for side in range(sides):
            own = value if sides == 1 else jnp.where(lane // SLOT == side, value, 0.0)
            at = (SLOT * q + LANES - SLOT * side) % LANES
            moved = pltpu.roll(own, at, 1) if at else own
            rims[side][group] = rims[side][group] + moved if group in rims[side] else moved
    return out[:, 0:LANES], rims


def solve_tail_kernel(sides, wide, place, back_a, back_b, bz, local, *rims):
    wide_y = back_a.shape[0] // wide
    for side in range(sides):
        rims[side][...] = jnp.zeros_like(rims[side])
    count = 10
    for start in range(OV - 1, wide - OV + 1, count):
        out, more = z_back(sides, wide_y, back_a, back_b, bz, start, count)
        at = start - OV + 1
        local[at * wide_y : (at + count) * wide_y] = out
        for side in range(sides):
            for group, value in more[side].items():
                rims[side][group * wide_y : (group + 1) * wide_y] += value


def placed_rims(place, sides, received, a, rows):
    total = None
    for side in range(sides):
        is_high, valid = place[SIDE + 2 * side] > 0, place[SIDE + 2 * side + 1] > 0
        start = jnp.where(is_high, LANES - OV, 0)
        shift = lax.rem(jnp.where(is_high, LANES - OV, LANES - 1) + LANES - SLOT * (a % GROUP), LANES)
        value = received[side][rows]
        lane = iota(value.shape, 1)
        value = jnp.where((lane >= start) & (lane < start + OV) & valid, pltpu.roll(value, shift, 1), 0.0)
        total = value if total is None else total + value
    return total


def pack_back_z_kernel(sizes, sides, wide, wide_y, place, x_first, x_second, *refs):
    own, out = refs[:sides], refs[sides:]
    _, faces = x_received(sizes, wide, wide_y, place, x_first, x_second)
    for side in range(sides):
        for group in range((wide + GROUP - 1) // GROUP):
            part = slice(group * wide_y, (group + 1) * wide_y)
            more = faces(side, group, slice(0, wide_y))
            out[side][part] = own[side][part] if more is None else own[side][part] + more


def fold_x_kernel(sizes, wide, wide_y, place, x_first, x_second, local, out):
    plane, _ = x_received(sizes, wide, wide_y, place, x_first, x_second)
    for p in range(wide - 2 * OV + 2):
        part = slice(p * wide_y, (p + 1) * wide_y)
        more = plane(p + OV - 1, slice(0, wide_y))
        out[part] = local[part] if more is None else local[part] + more


def pack_back_y_kernel(sides, wide, wide_y, place, field, *refs):
    own, received = refs[:sides], refs[sides : 2 * sides]
    faces, (first, second) = refs[2 * sides : 3 * sides], refs[3 * sides :]
    groups = (wide + GROUP - 1) // GROUP
    planes = wide - 2 * OV + 2
    even = is_even(place, IY)

    def put(at, low, high):
        first[at : at + RIM] = jnp.where(even, high, low)
        second[at : at + RIM] = jnp.where(even, low, high)

    lane = iota((groups * wide_y, LANES), 1)
    for side in range(sides):
        is_high, valid = place[SIDE + 2 * side] > 0, place[SIDE + 2 * side + 1] > 0
        other = pltpu.roll(received[side][...], jnp.where(is_high, LANES - OV, 0), 1)
        mine = pltpu.roll(own[side][...], jnp.where(is_high, LANES - 1, LANES - OV + 1), 1)
        faces[side][...] = jnp.where((lax.rem(lane, SLOT) == 0) & valid, other + mine, 0.0)
        for group in range(groups):
            low = faces[side][group * wide_y : group * wide_y + 8]
            high = faces[side][(group + 1) * wide_y - 8 : (group + 1) * wide_y]
            put(planes * RIM + (side * groups + group) * RIM, low[0:RIM], high[8 - RIM :])
    for p in range(planes):
        a = p + OV - 1
        ends = []
        for start in (0, wide_y - 8):
            at = a // GROUP * wide_y + start
            value = placed_rims(place, sides, received, a, slice(at, at + 8))
            ends.append(field[p * wide_y + start : p * wide_y + start + 8] + value)
        put(p * RIM, ends[0][0:RIM], ends[1][8 - RIM :])


def x_received(sizes, wide, wide_y, place, x_first, x_second):
    low, high = from_ends(place, IX, sizes, x_first, x_second)
    high_lane = (wide - 2 * OV) % GROUP * SLOT

    def plane(a, rows):
        if OV - 1 <= a < OV - 1 + RIM:
            at, source = (a - OV + 1) * wide_y, low
        elif wide - 2 * OV <= a < wide - 2 * OV + RIM:
            at, source = (a - wide + 2 * OV) * wide_y, high
        else:
            return None
        return source(slice(at + rows.start, at + rows.stop))

    def faces(side, group, rows):
        lane = iota((rows.stop - rows.start, LANES), 1)
        at = (RIM + side) * wide_y
        rows = slice(at + rows.start, at + rows.stop)
        if group == 0:
            return jnp.where((lane >= (OV - 1) * SLOT) & (lane < 2 * OV * SLOT), low(rows), 0.0)
        if group == (wide + GROUP - 1) // GROUP - 1:
            return jnp.where((lane >= high_lane) & (lane < high_lane + RIM * SLOT), high(rows), 0.0)
        return None

    return plane, faces


def weights_kernel(sizes, sides, place, axes, right, scale, x_first, x_second, y_first, y_second, *refs):
    scale_faces = refs[:sides]
    wx, wy, wz, z_weight, sums, scales = refs[sides:]
    ext_x, ext_y, depth = right.shape
    core = slice(8, 8 + ext_y)
    x_low, x_high = from_ends(place, IX, sizes, x_first, x_second)
    y_low, y_high = from_ends(place, IY, sizes, y_first, y_second)
    y_rows = (ext_x + 2 * OV) * OV
    x_rows = slice(x_first.shape[0] - ext_y, x_first.shape[0])
    scales[0, core] = x_low(x_rows)
    scales[ext_x + 1, core] = x_high(x_rows)
    for x in range(ext_x):
        scales[x + 1, core] = scale[x].astype(F32)
        part = slice(y_rows + x, y_rows + x + 1)
        scales[x + 1, 7:8] = y_low(part)
        scales[x + 1, 8 + ext_y : 9 + ext_y] = y_high(part)
    hx, hy, hz = (0.5 * axes[:, d : d + 1] for d in range(3))
    lane = iota((8, depth), 1)
    ends = (lane == 0) | (lane == depth - 1)
    zero = jnp.zeros((8, depth), F32)
    sum_right, sum_z = zero, zero
    for x in range(ext_x + 1):
        wx[x] = hx * (scales[x, core] + scales[x + 1, core])
    for x in range(ext_x):
        wy[x, 0 : ext_y + 1] = hy * (scales[x + 1, 7 : 8 + ext_y] + scales[x + 1, 8 : 9 + ext_y])
        for row in range(0, ext_y, 8):
            own = scales[x + 1, 8 + row : 16 + row]
            edge = zero
            for side in range(sides):
                is_high, valid = place[SIDE + 2 * side] > 0, place[SIDE + 2 * side + 1] > 0
                target = jnp.where(is_high, depth - 1, 0)
                at = x // GROUP * ext_y + row
                shift = lax.rem(target + depth - (x % GROUP * SLOT + OV), depth)
                edge = jnp.where((lane == target) & valid, pltpu.roll(scale_faces[side][at : at + 8], shift, 1), edge)
            wz[x, row : row + 8] = hz * (own + jnp.where(lane == 0, edge, pltpu.roll(own, 1, 1)))
            end_weight = jnp.where(ends, hz * (own + edge), 0.0)
            z_weight[x, row : row + 8] = end_weight
            sum_z = sum_z + end_weight
            sum_right = sum_right + right[x, row : row + 8]

    def whole(value):
        return jnp.sum(jnp.sum(value, axis=0, keepdims=True), axis=1, keepdims=True)

    def y_sum(row):
        total = jnp.zeros((1, depth), F32)
        for x in range(ext_x):
            total = total + wy[x, row : row + 1]
        return whole(total)

    x_high_sum, y_high_sum = whole(wx[ext_x]), y_sum(ext_y)
    z_high_sum = whole(jnp.where(lane == depth - 1, sum_z, 0.0))
    faces_sum = whole(wx[0]) + x_high_sum + y_sum(0) + y_high_sum + whole(sum_z)
    columns = {
        0: whole(sum_right),
        4: faces_sum,
        5: jnp.where(place[IX] < sizes["gx"] - 1, x_high_sum, 0.0),
        6: jnp.where(place[IY] < sizes["gy"] - 1, y_high_sum, 0.0),
        7: jnp.where(place[IZ] < sizes["gz"] - 1, z_high_sum, 0.0),
    }
    sums[...] = in_columns(columns, jnp.zeros((1, LANES), F32))


def in_columns(columns, row):
    at = iota((1, LANES), 1)
    for number, value in columns.items():
        row = jnp.where(at == number, value, row)
    return row


def operator_tile(place, sides, groups, values, edges, wx, wy, wz, z_weight, block, inner, row):
    depth = values.shape[2]
    ext_y = z_weight.shape[1]
    lane = iota((8, depth), 1)
    at = slice(8 + row, 16 + row)
    x = block * GROUP + inner
    mid = values[x + 1, at]
    total = wx[x, row : row + 8] * (mid - values[x, at]) + wx[x + 1, row : row + 8] * (mid - values[x + 2, at])
    total = total + wy[x, row : row + 8] * (mid - values[x + 1, 7 + row : 15 + row])
    total = total + wy[x, row + 1 : row + 9] * (mid - values[x + 1, 9 + row : 17 + row])
    edge = jnp.zeros((8, depth), F32)
    for side in range(sides):
        is_high, valid = place[SIDE + 2 * side] > 0, place[SIDE + 2 * side + 1] > 0
        target = jnp.where(is_high, depth - 1, 0)
        start = (side * groups + block + (inner + OV) // GROUP) * ext_y + row
        moved = edges[pl.ds(pl.multiple_of(start, 8), 8)]
        q = (inner + OV) % GROUP
        if q:
            moved = pltpu.roll(moved, depth - q * SLOT, 1)
        edge = jnp.where((lane == target) & valid, moved, edge)
    flux = wz[x, row : row + 8] * (mid - jnp.where(lane == 0, edge, pltpu.roll(mid, 1, 1)))
    above = z_weight[x, row : row + 8] * (mid - edge)
    total = total + flux + jnp.where(lane == depth - 1, above, -pltpu.roll(flux, depth - 1, 1))
    return mid, total


def operator_tiles(place, sides, groups, right, values, edges, weights, applied, sums, rows):
    def several(block, totals):
        product, energy, whole = totals
        for inner in range(GROUP):
            x = block * GROUP + inner
            for row in rows:
                mid, total = operator_tile(place, sides, groups, values, edges, *weights, block, inner, row)
                applied[x, row : row + 8] = total
                product = product + right[x, row : row + 8] * mid
                energy = energy + mid * total
                whole = whole + total
        return product, energy, whole

    totals = lax.fori_loop(0, right.shape[0] // GROUP, several, (jnp.zeros((8, values.shape[2]), F32),) * 3)
    for number, value in enumerate(totals):
        sums[number * 8 : (number + 1) * 8] = value


def to_face(place, side, value):
    return pltpu.roll(value, jnp.where(place[SIDE + 2 * side] > 0, LANES - 1, 0), 1)


def inner_kernel(sizes, sides, wide, place, right, field, *refs):
    received, faces, weights = refs[:sides], refs[sides : 2 * sides], refs[2 * sides : 2 * sides + 4]
    values, edges, applied, sums = refs[2 * sides + 4 :]
    ext_x, ext_y, depth = right.shape
    wide_y = ext_y + 2 * OV
    groups = (wide + GROUP - 1) // GROUP
    inside_low, inside_high = place[IX] > 0, place[IX] < sizes["gx"] - 1
    for p in range(ext_x + 2):
        a = p + OV - 1
        at = a // GROUP * wide_y
        value = placed_rims(place, sides, received, a, slice(at, at + wide_y))
        value = value + field[p * wide_y : (p + 1) * wide_y]
        if p == 0:
            value = jnp.where(inside_low, value, 0.0)
        if p == ext_x + 1:
            value = jnp.where(inside_high, value, 0.0)
        values[p, 8 - OV : 8 - OV + wide_y] = value
    for side in range(sides):
        for group in range(groups):
            value = faces[side][group * wide_y : (group + 1) * wide_y]
            at = (side * groups + group) * ext_y
            edges[at : at + ext_y] = to_face(place, side, value)[OV : OV + ext_y]
    operator_tiles(place, sides, groups, right, values, edges, weights, applied, sums, range(8, ext_y - 8, 8))


def outer_kernel(sizes, sides, wide, place, right, y_first, y_second, *refs):
    weights, fixed, refs = refs[:4], refs[4], refs[5:]
    inner_sums, refs = refs[3], refs[4:]
    values, edges, applied, out, sums = refs
    ext_x, ext_y, depth = right.shape
    wide_y = ext_y + 2 * OV
    groups = (wide + GROUP - 1) // GROUP
    low, high = from_ends(place, IY, sizes, y_first, y_second)
    inside_low, inside_high = place[IY] > 0, place[IY] < sizes["gy"] - 1
    for p in range(ext_x + 2):
        part = slice(p * RIM, (p + 1) * RIM)
        low_rows, high_rows = low(part), high(part)
        if p == 0 or p == ext_x + 1:
            inside = place[IX] > 0 if p == 0 else place[IX] < sizes["gx"] - 1
            low_rows, high_rows = (jnp.where(inside, rows, 0.0) for rows in (low_rows, high_rows))
        values[p, 7 : 7 + RIM] += low_rows
        values[p, 4 + ext_y : 4 + ext_y + RIM] += high_rows
        values[p, 7:8] = jnp.where(inside_low, values[p, 7:8], 0.0)
        values[p, 8 + ext_y : 9 + ext_y] = jnp.where(inside_high, values[p, 8 + ext_y : 9 + ext_y], 0.0)
    for number in range(sides * groups):
        at = (ext_x + 2 + number) * RIM
        start = number * ext_y
        side = number // groups
        edges[start : start + OV] += to_face(place, side, low(slice(at, at + RIM)))[1:]
        edges[start + ext_y - OV : start + ext_y] += to_face(place, side, high(slice(at, at + RIM)))[:OV]
    operator_tiles(place, sides, groups, right, values, edges, weights, applied, sums, (0, ext_y - 8))
    columns = {}
    for number in range(3):
        part = slice(number * 8, (number + 1) * 8)
        value = inner_sums[part] + sums[part]
        columns[number + 1] = jnp.sum(jnp.sum(value, axis=0, keepdims=True), axis=1, keepdims=True)
    out[...] = jnp.broadcast_to(in_columns(columns, fixed[...]), out.shape)


def finish_kernel(sizes, place, sums, spread, values, applied, wx, wy, z_weight, right, solution, residual, held_s, held_r, sems):
    ext_x, ext_y, depth = right.shape
    nx, ny, nz = (sizes[a] for a in MESH_AXES)
    count = nx * ny * nz
    table = sums[...]
    part = [table[:, k : k + 1] for k in range(8)]
    from_device = iota((count, count), 0) == iota((count, count), 1)
    sums_row = jnp.sum(jnp.where(from_device, part[0], 0.0), axis=0, keepdims=True)
    level = jnp.sum(spread[...] * sums_row, axis=1, keepdims=True)

    def shifted(by):
        return jnp.concatenate([level[by:], level[:by]], axis=0)

    def whole(value):
        return jnp.sum(value, axis=0, keepdims=True)

    product = whole(part[1] + level * part[0])
    neighbours = part[5] * shifted(ny * nz) + part[6] * shifted(nz) + part[7] * shifted(1)
    curvature = whole(part[2] + 2.0 * level * part[3] + level * (level * part[4] - 2.0 * neighbours))
    step = product / curvature
    device = iota((count, 1), 0)
    mine = (place[IX] * ny + place[IY]) * nz + place[IZ]

    def level_at(number, inside):
        return whole(jnp.where((device == number) & inside, level, 0.0))

    own = level_at(mine, True)
    drops = []
    for axis, stride, size in ((IX, ny * nz, nx), (IY, nz, ny), (IZ, 1, nz)):
        drops.append(step * (own - level_at(mine - stride, place[axis] > 0)))
        drops.append(step * (own - level_at(mine + stride, place[axis] < size - 1)))
    z_drop = jnp.where(iota((1, depth), 1) < depth // 2, drops[4], drops[5])
    chunk = 12
    for x in range(ext_x):
        held_s[x] = step * (values[x + 1, 8 : 8 + ext_y] + own)
        value = right[x] - step * applied[x] - z_drop * z_weight[x]
        if x == 0:
            value = value - drops[0] * wx[0]
        if x == ext_x - 1:
            value = value - drops[1] * wx[ext_x]
        held_r[x] = value
        held_r[x, 0:1] = value[0:1] - drops[2] * wy[x, 0:1]
        held_r[x, ext_y - 1 : ext_y] = value[ext_y - 1 : ext_y] - drops[3] * wy[x, ext_y : ext_y + 1]
        if (x + 1) % chunk == 0:
            part_x = pl.ds(x + 1 - chunk, chunk)
            number = (x + 1) // chunk - 1
            pltpu.make_async_copy(held_s.at[part_x], solution.at[part_x], sems.at[0, number]).start()
            pltpu.make_async_copy(held_r.at[part_x], residual.at[part_x], sems.at[1, number]).start()
    for number in range(ext_x // chunk):
        part_x = pl.ds(number * chunk, chunk)
        pltpu.make_async_copy(held_s.at[part_x], solution.at[part_x], sems.at[0, number]).wait()
        pltpu.make_async_copy(held_r.at[part_x], residual.at[part_x], sems.at[1, number]).wait()


def body(sizes, right, scale, axes, xv, yv, zv, x_values, y_values, z_values, inverse):
    ext_x, ext_y, depth = right.shape
    wide_x, wide_y = xv.shape[0], yv.shape[0]
    sides = 1 if sizes["gz"] == 2 else 2
    groups = (wide_x + GROUP - 1) // GROUP
    count = sizes["gx"] * sizes["gy"] * sizes["gz"]
    bind = functools.partial
    run = bind(call, sizes)
    block = shape(right.shape)
    axes_row = axes.reshape(1, -1)
    beside = 2 * 10**9

    up = lax.rem(lax.axis_index("gx"), 2) == 0
    starts = jnp.where(up, ext_x - OV, 0), jnp.where(up, 0, ext_x - OV)
    xs = [lax.dynamic_slice_in_dim(right, start, OV, 0) for start in starts]
    xs = swap_ends(*xs, "gx", sizes)

    thin = [shape([LANES // 2, 3 * size], BF16) for size in (wide_x, wide_x, wide_y, wide_y)]
    mats = run(
        bind(prepare_kernel, sides, 2.0 * ext_x * ext_y * depth),
        "prepare",
        thin + [shape([4 * depth, 2 * LANES], BF16), shape([6 * LANES, 2 * LANES], BF16), shape([wide_y, LANES]), shape([count, count])],
        [axes_row, xv, yv, zv, y_values.reshape(1, -1), z_values.reshape(1, -1), inverse],
        [VMEM] * 7,
        [pltpu.VMEM((LANES, LANES), F32), pltpu.VMEM((depth + 2 * OV, 2 * LANES), F32), pltpu.VMEM((LANES, 2 * LANES), F32)],
        flops=beside,
    )
    rim_message = [shape([groups * ext_y, LANES])] * sides
    rims = run(
        bind(pack_z_kernel, None, True, sides),
        "pack_z_own",
        rim_message,
        [right, scale],
        [VMEM] * 2,
        flops=beside,
    )
    y_message = [shape([wide_x * OV + ext_x + sides * groups * OV, depth])] * 2
    ys = run(pack_y_own_kernel, "pack_y_own", y_message, [right, scale], [VMEM] * 2, flops=beside)
    rims, ys, mats = lax.optimization_barrier((rims, ys, mats))
    *mats, spread = mats
    rims = run(
        bind(pack_z_kernel, sizes, False, sides),
        "pack_z_rest",
        rim_message,
        [*xs, *rims],
        [VMEM] * (2 + sides),
        aliases={2 + k: k for k in range(sides)},
    )
    rims = swap_sides(rims, sizes)

    ys = run(
        bind(pack_y_rest_kernel, sizes, sides, wide_x),
        "pack_y_rest",
        y_message,
        [*xs, *rims, *ys],
        [VMEM] * (4 + sides),
        aliases={2 + sides: 0, 3 + sides: 1},
    )
    ys = swap_ends(*ys, "gy", sizes)

    fx, _, _, _, wz, _, _ = mats
    tall = pltpu.VMEM((wide_x * wide_y, LANES), F32)
    core = pltpu.VMEM((wide_x * ext_y, LANES), F32)
    owns = run(
        bind(solve_own_kernel, sizes, sides),
        "solve_own",
        [shape([wide_x * ext_y, LANES])] * 2,
        [right, *xs, *rims, fx, wz],
        [VMEM] * (5 + sides),
        [core] * 2,
        limit=16,
        flops=2 * beside,
    )
    field = shape([wide_x * wide_y, depth])
    rim_message = shape([groups * wide_y, LANES])
    edge = pltpu.VMEM((wide_x * 2 * OV, LANES), F32)
    *back, low, high = run(
        bind(solve_rest_kernel, sizes, sides),
        "solve_rest",
        [field] * 2 + [shape([(RIM + sides) * wide_y + ext_y, depth])] * 2,
        [axes_row, x_values.reshape(1, -1), scale, *ys, *owns, *mats],
        [VMEM] * (7 + len(mats)),
        [edge] * 4 + [tall] * 2,
        limit=20,
    )
    back_xs = swap_ends(low, high, "gx", sizes)

    planes = ext_x + 2
    field = shape([planes * wide_y, depth])
    local, *own_rims = run(
        bind(solve_tail_kernel, sides, wide_x),
        "solve_tail",
        [field] + [rim_message] * sides,
        [*back, mats[5]],
        [VMEM] * 3,
        flops=beside,
    )
    own_rims = run(
        bind(pack_back_z_kernel, sizes, sides, wide_x, wide_y),
        "pack_back_z",
        [rim_message] * sides,
        [*back_xs, *own_rims],
        [VMEM] * (2 + sides),
    )
    late_rims, own_rims = lax.optimization_barrier((rims, own_rims))
    other_rims = swap_sides(own_rims, sizes)
    field_x = run(
        bind(fold_x_kernel, sizes, wide_x, wide_y),
        "fold_x",
        [field],
        [*back_xs, local],
        [VMEM] * 3,
        flops=beside,
    )[0]
    scale_block = pltpu.VMEM((planes, ext_y + 16, depth), F32)
    *weights, fixed = run(
        bind(weights_kernel, sizes, sides),
        "weights",
        [shape([ext_x + 1, ext_y, depth]), shape([ext_x, ext_y + 8, depth]), block, block, shape([1, LANES])],
        [axes_row, right, scale, *back_xs, *ys, *late_rims],
        [VMEM] * (7 + sides),
        [scale_block],
        flops=beside,
    )
    *faces, low, high = run(
        bind(pack_back_y_kernel, sides, wide_x, wide_y),
        "pack_back_y",
        [rim_message] * sides + [shape([(planes + groups * sides) * RIM, depth])] * 2,
        [field_x, *own_rims, *other_rims],
        [VMEM] * (1 + 2 * sides),
    )
    back_ys = swap_ends(low, high, "gy", sizes)

    parts = [shape([planes, ext_y + 16, depth]), shape([sides * groups * ext_y, LANES]), block]
    inner = run(
        bind(inner_kernel, sizes, sides, wide_x),
        "inner",
        parts + [shape([24, depth])],
        [right, field_x, *other_rims, *faces, *weights],
        [VMEM] * (6 + 2 * sides),
        flops=beside,
    )
    values, edges, applied, sums = run(
        bind(outer_kernel, sizes, sides, wide_x),
        "outer",
        parts + [shape([count, LANES])],
        [right, *back_ys, *weights, fixed, *inner],
        [VMEM] * 12,
        [pltpu.VMEM((24, depth), F32)],
        aliases={8: 0, 9: 1, 10: 2},
    )
    sums = lax.all_to_all(sums, MESH_AXES, 0, 0, tiled=True)

    held = pltpu.VMEM(right.shape, F32)
    wx, wy, _, z_weight = weights
    return tuple(
        run(
            bind(finish_kernel, sizes),
            "finish",
            [block] * 2,
            [sums, spread, values, applied, wx, wy, z_weight, right],
            [VMEM] * 8,
            [held, held, pltpu.SemaphoreType.DMA((2, ext_x // 12))],
            out_specs=[ANY] * 2,
        )
    )


def solution(mesh):
    sizes = dict(mesh.shape)
    in_specs = (P(*MESH_AXES), P(*MESH_AXES), P(), P(), P(), P(), P(), P(), P(), P())
    out_specs = (P(*MESH_AXES), P(*MESH_AXES))
    return jax.shard_map(functools.partial(body, sizes), mesh=mesh, in_specs=in_specs, out_specs=out_specs, check_vma=False)
```

time: 63.3 us -> 60.4 us (0.954)
  local copies, waits for them, and re-layouts: 0.05 us -> 3.97 us
  starting transfers between devices: 19.2 us -> 16.6 us
  waiting for transfers between devices: 9.12 us -> 7.52 us
  blocking collectives: 16.4 us -> 14.8 us
  Pallas kernels: 17.4 us -> 16.2 us
    unnamed x20 -> x24, local copies, waits for them, and re-layouts: 0.05 us -> 3.01 us
    ppermute x8, starting transfers between devices: 18.9 us -> 16.5 us  [swap_ends(): received.append(lax.ppermute(message, axis, list(enumerate(partner))))]
    all_to_all x1, blocking collectives: 16.4 us -> 14.8 us  [body(): sums = lax.all_to_all(sums, MESH_AXES, 0, 0, tiled=True)]
    ppermute x2, waiting for transfers between devices: 2.5 us -> 1.29 us  [swap_sides(): return [lax.ppermute(messages[0], 'gz', [(0, 1), (1, 0)])]]
    pallas_call x14 -> x15, Pallas kernels: 17.4 us -> 16.2 us  [call(): pl.pallas_call(placed, out_shape=outs, in_specs=spaces, out_specs=out_spe...]
    dynamic_slice x0 -> x1, local copies, waits for them, and re-layouts: none -> 0.96 us  [body(): xs = [lax.dynamic_slice_in_dim(right, start, OV, 0) for start in starts]]
  transfers between devices with their start and end apart: 10 -> 10, of which waited for: 6 -> 4; matrix products, arithmetic and copies ran while one was open for 0% -> 0% of each run, Pallas kernels for 7% -> 14%
where the time goes in v3:
time: 60.4 us; the launch traced here: 60 us
  starting transfers between devices  16.6 us (27%)
  Pallas kernels  16.2 us (27%)
  blocking collectives  14.8 us (25%)
  waiting for transfers between devices  7.52 us (12%)
  local copies, waits for them, and re-layouts  3.97 us (7%)
  between operations  0.87 us (1%)
    ppermute x8, starting transfers between devices, swap_ends(): received.append(lax.ppermute(message, axis, list(enumerate(partner))))  16.5 us
    pallas_call x15, Pallas kernels, call(): pl.pallas_call(placed, out_shape=outs, in_specs=spaces, out_specs=out_spe...  16.2 us
    all_to_all x1, blocking collectives, body(): sums = lax.all_to_all(sums, MESH_AXES, 0, 0, tiled=True)  14.8 us
    ppermute x8, waiting for transfers between devices, swap_ends(): received.append(lax.ppermute(message, axis, list(enumerate(partner))))  6.23 us
    unnamed x24, local copies, waits for them, and re-layouts  3.01 us
    ppermute x2, waiting for transfers between devices, swap_sides(): return [lax.ppermute(messages[0], 'gz', [(0, 1), (1, 0)])]  1.29 us
  transfers between devices with their start and end apart: 10, of which 4 were waited for; matrix products, arithmetic and copies ran while one was open for 0% of the time, Pallas kernels for 14%

profile of v3, /device:TPU:0, one launch (start us, length us, event | category | flops | bytes accessed | tf_op | source)
XLA Modules:
  0.0 60.0 jit_solution(3434808014251778228)
XLA Ops:
  0.6 1.0 %constant_dynamic-slice_fusion = (f32[4,48,128]{2,1,0:T(8,128)S(1)}, f32[4,48,128]{2,1,0:T(8,128)S(1)}) fusion(f32[48,48,128]{2,1,0:T(8,128)} %refs_7_.1, s32[]{:T(128)S(6)} %select_n.10, s32[]{:T(128)S(6)} %select_n.9), kind=kLoop, calls=%fused_computation | loop fusion | bytes 393224 | tf_op jit(solution)/shard_map/dynamic_slice | solution.py:735
  1.6 0.7 %collective-permute-start.1 = (f32[4,48,128]{2,1,0:T(8,128)S(1)}, f32[4,48,128]{2,1,0:T(8,128)S(1)}, u32[]{:S(2)}, u32[]{:S(2)}) collective-permute-start(f32[4,48,128]{2,1,0:T(8,128)S(1)} %get-tuple-element.98), channel_id=1, source_target_pairs={{0,0},{8,16},{16,8},{24,24},{1,1},{9,17},{17,9},{25,25},{2,2},{10,... | collective-permute-start | bytes 294920 | tf_op jit(solution)/shard_map/ppermute | solution.py:90
  2.3 5.9 %collective-permute-start = (f32[4,48,128]{2,1,0:T(8,128)S(1)}, f32[4,48,128]{2,1,0:T(8,128)S(1)}, u32[]{:S(2)}, u32[]{:S(2)}) collective-permute-start(f32[4,48,128]{2,1,0:T(8,128)S(1)} %get-tuple-element.99), channel_id=1, source_target_pairs={{0,8},{8,0},{16,24},{24,16},{1,9},{9,1},{17,25},{25,17},{2,10},{10... | collective-permute-start | bytes 294920 | tf_op jit(solution)/shard_map/ppermute | solution.py:90
  8.2 1.3 %copy-done = f32[48,48,128]{2,1,0:T(8,128)S(1)} copy-done((f32[48,48,128]{2,1,0:T(8,128)S(1)}, f32[48,48,128]{2,1,0:T(8,128)}, u32[]{:S(2)}) %copy-start) | copy-done | bytes 1179672
  9.5 1.1 %copy-done.2 = bf16[48,48,128]{2,1,0:T(8,128)(2,1)S(1)} copy-done((bf16[48,48,128]{2,1,0:T(8,128)(2,1)S(1)}, bf16[48,48,128]{2,1,0:T(8,128)(2,1)}, u32[]{:S(2)}) %copy-start.2) | copy-done | bytes 589848
  10.5 0.5 pack_z_own.1.refs_2_
  11.1 0.1 pack_y_own.1
  11.2 0.5 copy-done.5
  11.7 0.1 copy-done.6
  11.9 0.4 prepare.1
  12.3 0.1 pack_z_rest.1
  12.5 1.3 %collective-permute-done.2.refs_2_.refs_3_.refs_7_ = f32[192,128]{1,0:T(8,128)S(1)} collective-permute-done((f32[192,128]{1,0:T(8,128)S(1)}, f32[192,128]{1,0:T(8,128)S(1)}, u32[]{:S(2)}, u32[]{:S(2)}) %collective-permute-start.2) | collective-permute-done | bytes 98336 | tf_op jit(solution)/shard_map/ppermute | solution.py:77
  13.8 1.6 %collective-permute-start.3 = (f32[288,128]{1,0:T(8,128)S(1)}, f32[288,128]{1,0:T(8,128)S(1)}, u32[]{:S(2)}, u32[]{:S(2)}) collective-permute-start(f32[288,128]{1,0:T(8,128)S(1)} %get-tuple-element.63), channel_id=1, source_target_pairs={{0,2},{2,0},{4,6},{6,4},{1,3},{3,1},{5,7},{7,5},{8,10},{10,8},{12,... | collective-permute-start | bytes 442376 | tf_op jit(solution)/shard_map/ppermute | solution.py:90
  15.4 0.8 %collective-permute-start.4 = (f32[288,128]{1,0:T(8,128)S(1)}, f32[288,128]{1,0:T(8,128)S(1)}, u32[]{:S(2)}, u32[]{:S(2)}) collective-permute-start(f32[288,128]{1,0:T(8,128)S(1)} %get-tuple-element.64), channel_id=1, source_target_pairs={{0,0},{2,4},{4,2},{6,6},{1,1},{3,5},{5,3},{7,7},{8,8},{10,12},{12,... | collective-permute-start | bytes 442376 | tf_op jit(solution)/shard_map/ppermute | solution.py:90
  16.2 2.4 %solve_own.1 = (f32[2688,128]{1,0:T(8,128)S(1)}, f32[2688,128]{1,0:T(8,128)S(1)}) custom-call(f32[48,48,128]{2,1,0:T(8,128)S(1)} %copy-done.1, f32[4,48,128]{2,1,0:T(8,128)S(1)} %collective-permute-done.refs_0_.refs_1_, f32[4,48,128]{2,1,0:T(8,128)S(1)} %collective-permute-done.1.refs_1_.refs_2_, ...), custom_call_target="tpu_custom_call" | custom-call | flops 4000000000 | bytes 4510720 | tf_op jit(solution)/shard_map/solve_own/pallas_call | solution.py:31
  18.6 1.2 %collective-permute-done.3.refs_3_.refs_5_ = f32[288,128]{1,0:T(8,128)S(1)} collective-permute-done((f32[288,128]{1,0:T(8,128)S(1)}, f32[288,128]{1,0:T(8,128)S(1)}, u32[]{:S(2)}, u32[]{:S(2)}) %collective-permute-start.3) | collective-permute-done | bytes 147488 | tf_op jit(solution)/shard_map/ppermute | solution.py:90
  19.8 4.2 %solve_rest.1 = (f32[3136,128]{1,0:T(8,128)S(1)}, f32[3136,128]{1,0:T(8,128)S(1)}, f32[384,128]{1,0:T(8,128)S(1)}, f32[384,128]{1,0:T(8,128)S(1)}) custom-call(f32[1,3]{1,0:T(1,128)S(1)} %bitcast.12, f32[1,56]{1,0:T(1,128)S(1)} %bitcast.10, bf16[48,48,128]{2,1,0:T(8,128)(2,1)S(1)} %copy-done.3, f32[288,128]{1,0:T(8,128)S(1)} %collective-permute-done.3.refs_3_.refs_5_, ...), custom_call_target="tpu_custom_call" | custom-call | bytes 8012012 | tf_op jit(solution)/shard_map/solve_rest/pallas_call | solution.py:31
  24.0 0.6 collective-permute-start.5
  24.5 0.7 %collective-permute-start.6 = (f32[384,128]{1,0:T(8,128)S(1)}, f32[384,128]{1,0:T(8,128)S(1)}, u32[]{:S(2)}, u32[]{:S(2)}) collective-permute-start(f32[384,128]{1,0:T(8,128)S(1)} %get-tuple-element.75), channel_id=1, source_target_pairs={{0,0},{8,16},{16,8},{24,24},{1,1},{9,17},{17,9},{25,25},{2,2},{10,... | collective-permute-start | bytes 589832 | tf_op jit(solution)/shard_map/ppermute | solution.py:90
  25.2 1.4 %solve_tail.1 = (f32[2800,128]{1,0:T(8,128)S(1)}, f32[224,128]{1,0:T(8,128)S(1)}) custom-call(f32[3136,128]{1,0:T(8,128)S(1)} %get-tuple-element.76.refs_0_, f32[3136,128]{1,0:T(8,128)S(1)} %get-tuple-element.77.refs_1_, bf16[768,256]{1,0:T(8,128)(2,1)S(1)} %get-tuple-element.72.refs_12_.refs_2_), custom_call_target="tpu_custom_call" | custom-call | flops 2000000000 | bytes 5152768 | tf_op jit(solution)/shard_map/solve_tail/pallas_call | solution.py:31
  26.6 3.6 %collective-permute-done.5.refs_0_.refs_3_ = f32[384,128]{1,0:T(8,128)S(1)} collective-permute-done((f32[384,128]{1,0:T(8,128)S(1)}, f32[384,128]{1,0:T(8,128)S(1)}, u32[]{:S(2)}, u32[]{:S(2)}) %collective-permute-start.5) | collective-permute-done | bytes 196640 | tf_op jit(solution)/shard_map/ppermute | solution.py:90
  30.2 0.1 collective-permute-start.7
  30.3 0.1 fold_x.1.refs_0_.refs_1_
  30.4 1.2 %weights.1 = (f32[49,48,128]{2,1,0:T(8,128)S(1)}, f32[48,56,128]{2,1,0:T(8,128)S(1)}, f32[48,48,128]{2,1,0:T(8,128)S(1)}, f32[48,48,128]{2,1,0:T(8,128)S(1)}, f32[1,128]{1,0:T(1,128)S(1)}) custom-call(f32[1,3]{1,0:T(1,128)S(1)} %bitcast.13, f32[48,48,128]{2,1,0:T(8,128)S(1)} %copy-done.1, bf16[48,48,128]{2,1,0:T(8,128)(2,1)S(1)} %copy-done.3, ...), custom_call_target="tpu_custom_call" | custom-call | flops 2000000000 | bytes 7496204 | tf_op jit(solution)/shard_map/weights/pallas_call | solution.py:31
  31.6 0.2 pack_back_y.1
  31.9 5.7 %collective-permute-start.8 = (f32[270,128]{1,0:T(8,128)S(1)}, f32[270,128]{1,0:T(8,128)S(1)}, u32[]{:S(2)}, u32[]{:S(2)}) collective-permute-start(f32[270,128]{1,0:T(8,128)S(1)} %get-tuple-element.81), channel_id=1, source_target_pairs={{0,2},{2,0},{4,6},{6,4},{1,3},{3,1},{5,7},{7,5},{8,10},{10,8},{12,... | collective-permute-start | bytes 414728 | tf_op jit(solution)/shard_map/ppermute | solution.py:90
  37.5 0.7 %collective-permute-start.9 = (f32[270,128]{1,0:T(8,128)S(1)}, f32[270,128]{1,0:T(8,128)S(1)}, u32[]{:S(2)}, u32[]{:S(2)}) collective-permute-start(f32[270,128]{1,0:T(8,128)S(1)} %get-tuple-element.82), channel_id=1, source_target_pairs={{0,0},{2,4},{4,2},{6,6},{1,1},{3,5},{5,3},{7,7},{8,8},{10,12},{12,... | collective-permute-start | bytes 414728 | tf_op jit(solution)/shard_map/ppermute | solution.py:90
  38.2 2.4 %inner.1 = (f32[50,64,128]{2,1,0:T(8,128)S(1)}, f32[192,128]{1,0:T(8,128)S(1)}, f32[48,48,128]{2,1,0:T(8,128)S(1)}, f32[24,128]{1,0:T(8,128)S(1)}) custom-call(f32[48,48,128]{2,1,0:T(8,128)S(1)} %copy-done.1, f32[2800,128]{1,0:T(8,128)S(1)} %fold_x.1.refs_0_.refs_1_, f32[224,128]{1,0:T(8,128)S(1)} %collective-permute-done.7.refs_2_, ...), custom_call_target="tpu_custom_call" | custom-call | flops 2000000000 | bytes 10711040 | tf_op jit(solution)/shard_map/inner/pallas_call | solution.py:31
  40.6 1.4 %collective-permute-done.8.refs_1_ = f32[270,128]{1,0:T(8,128)S(1)} collective-permute-done((f32[270,128]{1,0:T(8,128)S(1)}, f32[270,128]{1,0:T(8,128)S(1)}, u32[]{:S(2)}, u32[]{:S(2)}) %collective-permute-start.8) | collective-permute-done | bytes 138272 | tf_op jit(solution)/shard_map/ppermute | solution.py:90
  42.0 1.0 %outer.1 = (f32[50,64,128]{2,1,0:T(8,128)S(1)}, f32[192,128]{1,0:T(8,128)S(1)}, f32[48,48,128]{2,1,0:T(8,128)S(1)}, f32[32,128]{1,0:T(8,128)S(1)}) custom-call(f32[48,48,128]{2,1,0:T(8,128)S(1)} %copy-done.1, f32[270,128]{1,0:T(8,128)S(1)} %collective-permute-done.8.refs_1_, ...), custom_call_target="tpu_custom_call", output_to_operand_aliasing={{0}: (8, {}), {1}: (9, {}), {2}: (10, {})} | custom-call | bytes 12257792 | tf_op jit(solution)/shard_map/outer/pallas_call | solution.py:31
  43.0 14.8 %all_to_all.11 = f32[32,1,128]{2,1,0:T(1,128)S(1)} all-to-all(f32[32,1,128]{2,1,0:T(1,128)S(1)} %bitcast.9), channel_id=1, replica_groups=mesh['gx'=4,'gy'=4,'gz'=2] {'gx','gy','gz'}, dimensions={0} | all-to-all | bytes 32768 | tf_op jit(solution)/shard_map/all_to_all | solution.py:872
  57.8 2.3 %finish.1 = (f32[48,48,128]{2,1,0:T(8,128)}, f32[48,48,128]{2,1,0:T(8,128)}) custom-call(f32[32,128]{1,0:T(8,128)S(1)} %bitcast.8, f32[32,32]{1,0:T(8,128)S(1)} %get-tuple-element.95.refs_1_, f32[50,64,128]{2,1,0:T(8,128)S(1)} %get-tuple-element.96.refs_2_, f32[48,48,128]{2,1,0:T(8,128)S(1)} %get-tuple-element.97.refs_3_, ...), custom_call_target="tpu_custom_call" | custom-call | bytes 10137600 | tf_op jit(solution)/shard_map/finish/pallas_call | solution.py:31
  (29 shorter events, 0.2 us)
Async XLA Ops:
  1.6 10.7 %collective-permute-start.1 = (f32[4,48,128]{2,1,0:T(8,128)S(1)}, f32[4,48,128]{2,1,0:T(8,128)S(1)}, u32[]{:S(2)}, u32[]{:S(2)}) collective-permute-start(f32[4,48,128]{2,1,0:T(8,128)S(1)} %get-tuple-element.98), channel_id=1, source_target_pairs={{0,0},{8,16},{16,8},{24,24},{1,1},{9,17},{17,9},{25,25},{2,2},{10,... | collective-permute-start | bytes 294920 | tf_op jit(solution)/shard_map/ppermute | solution.py:90
  2.3 10.0 %collective-permute-start = (f32[4,48,128]{2,1,0:T(8,128)S(1)}, f32[4,48,128]{2,1,0:T(8,128)S(1)}, u32[]{:S(2)}, u32[]{:S(2)}) collective-permute-start(f32[4,48,128]{2,1,0:T(8,128)S(1)} %get-tuple-element.99), channel_id=1, source_target_pairs={{0,8},{8,0},{16,24},{24,16},{1,9},{9,1},{17,25},{25,17},{2,10},{10... | collective-permute-start | bytes 294920 | tf_op jit(solution)/shard_map/ppermute | solution.py:90
  8.2 1.3 %copy-start = (f32[48,48,128]{2,1,0:T(8,128)S(1)}, f32[48,48,128]{2,1,0:T(8,128)}, u32[]{:S(2)}) copy-start(f32[48,48,128]{2,1,0:T(8,128)} %refs_7_.1) | copy-start | bytes 3538948
  9.5 1.1 %copy-start.2 = (bf16[48,48,128]{2,1,0:T(8,128)(2,1)S(1)}, bf16[48,48,128]{2,1,0:T(8,128)(2,1)}, u32[]{:S(2)}) copy-start(bf16[48,48,128]{2,1,0:T(8,128)(2,1)} %refs_2_.5) | copy-start | bytes 1769476
  11.1 0.7 %copy-start.5 = (f32[3]{0:T(128)S(1)}, f32[3]{0:T(128)}, u32[]{:S(2)}) copy-start(f32[3]{0:T(128)} %param.12) | copy-start | bytes 40
  11.1 0.8 %copy-start.6 = (f32[72,72]{1,0:T(8,128)S(1)}, f32[72,72]{1,0:T(8,128)}, u32[]{:S(2)}) copy-start(f32[72,72]{1,0:T(8,128)} %refs_3_.1) | copy-start | bytes 62212
  11.1 0.8 %copy-start.7 = (f32[56,56]{1,0:T(8,128)S(1)}, f32[56,56]{1,0:T(8,128)}, u32[]{:S(2)}) copy-start(f32[56,56]{1,0:T(8,128)} %refs_1_.6) | copy-start | bytes 37636
  11.1 0.8 %copy-start.8 = (f32[56,56]{1,0:T(8,128)S(1)}, f32[56,56]{1,0:T(8,128)}, u32[]{:S(2)}) copy-start(f32[56,56]{1,0:T(8,128)} %refs_2_.3) | copy-start | bytes 37636
  11.1 0.8 %copy-start.9 = (f32[16,16]{1,0:T(8,128)S(1)}, f32[16,16]{1,0:T(8,128)}, u32[]{:S(2)}) copy-start(f32[16,16]{1,0:T(8,128)} %refs_6_.1) | copy-start | bytes 3076
  11.1 0.7 %copy-start.10 = (f32[56]{0:T(128)S(1)}, f32[56]{0:T(128)}, u32[]{:S(2)}) copy-start(f32[56]{0:T(128)} %param.17) | copy-start | bytes 676
  11.1 0.7 %copy-start.11 = (f32[72]{0:T(128)S(1)}, f32[72]{0:T(128)}, u32[]{:S(2)}) copy-start(f32[72]{0:T(128)} %param.18) | copy-start | bytes 868
  11.9 4.3 %copy-start.1 = (f32[48,48,128]{2,1,0:T(8,128)S(1)}, f32[48,48,128]{2,1,0:T(8,128)}, u32[]{:S(2)}) copy-start(f32[48,48,128]{2,1,0:T(8,128)} %refs_7_.1) | copy-start | bytes 3538948
  12.4 1.4 %collective-permute-start.2 = (f32[192,128]{1,0:T(8,128)S(1)}, f32[192,128]{1,0:T(8,128)S(1)}, u32[]{:S(2)}, u32[]{:S(2)}) collective-permute-start(f32[192,128]{1,0:T(8,128)S(1)} %pack_z_rest.1), channel_id=1, source_target_pairs={{0,1},{1,0},{2,3},{3,2},{4,5},{5,4},{6,7},{7,6},{8,9},{9,8},{10,11... | collective-permute-start | bytes 294920 | tf_op jit(solution)/shard_map/ppermute | solution.py:77
  13.8 6.0 %collective-permute-start.3 = (f32[288,128]{1,0:T(8,128)S(1)}, f32[288,128]{1,0:T(8,128)S(1)}, u32[]{:S(2)}, u32[]{:S(2)}) collective-permute-start(f32[288,128]{1,0:T(8,128)S(1)} %get-tuple-element.63), channel_id=1, source_target_pairs={{0,2},{2,0},{4,6},{6,4},{1,3},{3,1},{5,7},{7,5},{8,10},{10,8},{12,... | collective-permute-start | bytes 442376 | tf_op jit(solution)/shard_map/ppermute | solution.py:90
  15.4 4.4 %copy-start.3 = (bf16[48,48,128]{2,1,0:T(8,128)(2,1)S(1)}, bf16[48,48,128]{2,1,0:T(8,128)(2,1)}, u32[]{:S(2)}) copy-start(bf16[48,48,128]{2,1,0:T(8,128)(2,1)} %refs_2_.5) | copy-start | bytes 1769476
  15.4 4.4 %copy-start.4 = (f32[56]{0:T(128)S(1)}, f32[56]{0:T(128)}, u32[]{:S(2)}) copy-start(f32[56]{0:T(128)} %param.16) | copy-start | bytes 676
  15.4 4.4 %collective-permute-start.4 = (f32[288,128]{1,0:T(8,128)S(1)}, f32[288,128]{1,0:T(8,128)S(1)}, u32[]{:S(2)}, u32[]{:S(2)}) collective-permute-start(f32[288,128]{1,0:T(8,128)S(1)} %get-tuple-element.64), channel_id=1, source_target_pairs={{0,0},{2,4},{4,2},{6,6},{1,1},{3,5},{5,3},{7,7},{8,8},{10,12},{12,... | collective-permute-start | bytes 442376 | tf_op jit(solution)/shard_map/ppermute | solution.py:90
  24.0 6.2 %collective-permute-start.5 = (f32[384,128]{1,0:T(8,128)S(1)}, f32[384,128]{1,0:T(8,128)S(1)}, u32[]{:S(2)}, u32[]{:S(2)}) collective-permute-start(f32[384,128]{1,0:T(8,128)S(1)} %get-tuple-element.74), channel_id=1, source_target_pairs={{0,8},{8,0},{16,24},{24,16},{1,9},{9,1},{17,25},{25,17},{2,10},{10... | collective-permute-start | bytes 589832 | tf_op jit(solution)/shard_map/ppermute | solution.py:90
  24.5 5.6 %collective-permute-start.6 = (f32[384,128]{1,0:T(8,128)S(1)}, f32[384,128]{1,0:T(8,128)S(1)}, u32[]{:S(2)}, u32[]{:S(2)}) collective-permute-start(f32[384,128]{1,0:T(8,128)S(1)} %get-tuple-element.75), channel_id=1, source_target_pairs={{0,0},{8,16},{16,8},{24,24},{1,1},{9,17},{17,9},{25,25},{2,2},{10,... | collective-permute-start | bytes 589832 | tf_op jit(solution)/shard_map/ppermute | solution.py:90
  30.2 1.4 %collective-permute-start.7 = (f32[224,128]{1,0:T(8,128)S(1)}, f32[224,128]{1,0:T(8,128)S(1)}, u32[]{:S(2)}, u32[]{:S(2)}) collective-permute-start(f32[224,128]{1,0:T(8,128)S(1)} %pack_back_z.1.refs_1_), channel_id=1, source_target_pairs={{0,1},{1,0},{2,3},{3,2},{4,5},{5,4},{6,7},{7,6},{8,9},{9,8},{10,11... | collective-permute-start | bytes 344072 | tf_op jit(solution)/shard_map/ppermute | solution.py:77
  31.9 10.1 %collective-permute-start.8 = (f32[270,128]{1,0:T(8,128)S(1)}, f32[270,128]{1,0:T(8,128)S(1)}, u32[]{:S(2)}, u32[]{:S(2)}) collective-permute-start(f32[270,128]{1,0:T(8,128)S(1)} %get-tuple-element.81), channel_id=1, source_target_pairs={{0,2},{2,0},{4,6},{6,4},{1,3},{3,1},{5,7},{7,5},{8,10},{10,8},{12,... | collective-permute-start | bytes 414728 | tf_op jit(solution)/shard_map/ppermute | solution.py:90
  37.5 4.4 %collective-permute-start.9 = (f32[270,128]{1,0:T(8,128)S(1)}, f32[270,128]{1,0:T(8,128)S(1)}, u32[]{:S(2)}, u32[]{:S(2)}) collective-permute-start(f32[270,128]{1,0:T(8,128)S(1)} %get-tuple-element.82), channel_id=1, source_target_pairs={{0,0},{2,4},{4,2},{6,6},{1,1},{3,5},{5,3},{7,7},{8,8},{10,12},{12,... | collective-permute-start | bytes 414728 | tf_op jit(solution)/shard_map/ppermute | solution.py:90

commit v4 on v3

--- a/solution.py
+++ b/solution.py
@@ -735,16 +735,6 @@
     xs = [lax.dynamic_slice_in_dim(right, start, OV, 0) for start in starts]
     xs = swap_ends(*xs, "gx", sizes)
 
-    thin = [shape([LANES // 2, 3 * size], BF16) for size in (wide_x, wide_x, wide_y, wide_y)]
-    mats = run(
-        bind(prepare_kernel, sides, 2.0 * ext_x * ext_y * depth),
-        "prepare",
-        thin + [shape([4 * depth, 2 * LANES], BF16), shape([6 * LANES, 2 * LANES], BF16), shape([wide_y, LANES]), shape([count, count])],
-        [axes_row, xv, yv, zv, y_values.reshape(1, -1), z_values.reshape(1, -1), inverse],
-        [VMEM] * 7,
-        [pltpu.VMEM((LANES, LANES), F32), pltpu.VMEM((depth + 2 * OV, 2 * LANES), F32), pltpu.VMEM((LANES, 2 * LANES), F32)],
-        flops=beside,
-    )
     rim_message = [shape([groups * ext_y, LANES])] * sides
     rims = run(
         bind(pack_z_kernel, None, True, sides),
@@ -756,8 +746,7 @@
     )
     y_message = [shape([wide_x * OV + ext_x + sides * groups * OV, depth])] * 2
     ys = run(pack_y_own_kernel, "pack_y_own", y_message, [right, scale], [VMEM] * 2, flops=beside)
-    rims, ys, mats = lax.optimization_barrier((rims, ys, mats))
-    *mats, spread = mats
+    rims, ys = lax.optimization_barrier((rims, ys))
     rims = run(
         bind(pack_z_kernel, sizes, False, sides),
         "pack_z_rest",
@@ -766,7 +755,18 @@
         [VMEM] * (2 + sides),
         aliases={2 + k: k for k in range(sides)},
     )
+    rims, late_zv = lax.optimization_barrier((rims, zv))
     rims = swap_sides(rims, sizes)
+    thin = [shape([LANES // 2, 3 * size], BF16) for size in (wide_x, wide_x, wide_y, wide_y)]
+    *mats, spread = run(
+        bind(prepare_kernel, sides, 2.0 * ext_x * ext_y * depth),
+        "prepare",
+        thin + [shape([4 * depth, 2 * LANES], BF16), shape([6 * LANES, 2 * LANES], BF16), shape([wide_y, LANES]), shape([count, count])],
+        [axes_row, xv, yv, late_zv, y_values.reshape(1, -1), z_values.reshape(1, -1), inverse],
+        [VMEM] * 7,
+        [pltpu.VMEM((LANES, LANES), F32), pltpu.VMEM((depth + 2 * OV, 2 * LANES), F32), pltpu.VMEM((LANES, 2 * LANES), F32)],
+        flops=beside,
+    )
 
     ys = run(
         bind(pack_y_rest_kernel, sizes, sides, wide_x),

time: 60.4 us -> 59.3 us (0.982)
  waiting for transfers between devices: 7.52 us -> 5.84 us
  starting transfers between devices: 16.6 us -> 17.5 us
    ppermute x8, starting transfers between devices: 16.5 us -> 17.4 us  [swap_ends(): received.append(lax.ppermute(message, axis, list(enumerate(partner))))]
    ppermute x8, waiting for transfers between devices: 6.23 us -> 5.37 us  [swap_ends(): received.append(lax.ppermute(message, axis, list(enumerate(partner))))]
    ppermute x2, waiting for transfers between devices: 1.29 us -> 0.47 us  [swap_sides(): return [lax.ppermute(messages[0], 'gz', [(0, 1), (1, 0)])]]
where the time goes in v4:
time: 59.3 us; the launch traced here: 58.9 us
  starting transfers between devices  17.5 us (30%)
  Pallas kernels  16.2 us (27%)
  blocking collectives  14.7 us (25%)
  waiting for transfers between devices  5.84 us (10%)
  local copies, waits for them, and re-layouts  3.74 us (6%)
  between operations  0.89 us (2%)
    ppermute x8, starting transfers between devices, swap_ends(): received.append(lax.ppermute(message, axis, list(enumerate(partner))))  17.4 us
    pallas_call x15, Pallas kernels, call(): pl.pallas_call(placed, out_shape=outs, in_specs=spaces, out_specs=out_spe...  16.2 us
    all_to_all x1, blocking collectives, body(): sums = lax.all_to_all(sums, MESH_AXES, 0, 0, tiled=True)  14.7 us
    ppermute x8, waiting for transfers between devices, swap_ends(): received.append(lax.ppermute(message, axis, list(enumerate(partner))))  5.37 us
    unnamed x24, local copies, waits for them, and re-layouts  2.78 us
  transfers between devices with their start and end apart: 10, of which 4 were waited for; matrix products, arithmetic and copies ran while one was open for 0% of the time, Pallas kernels for 14%

profile of v4, /device:TPU:0, one launch (start us, length us, event | category | flops | bytes accessed | tf_op | source)
XLA Modules:
  0.0 58.9 jit_solution(13338022389567936592)
XLA Ops:
  0.6 1.0 %constant_dynamic-slice_fusion = (f32[4,48,128]{2,1,0:T(8,128)S(1)}, f32[4,48,128]{2,1,0:T(8,128)S(1)}) fusion(f32[48,48,128]{2,1,0:T(8,128)} %refs_7_.1, s32[]{:T(128)S(6)} %select_n.10, s32[]{:T(128)S(6)} %select_n.9), kind=kLoop, calls=%fused_computation | loop fusion | bytes 393224 | tf_op jit(solution)/shard_map/dynamic_slice | solution.py:735
  1.6 0.7 %collective-permute-start.1 = (f32[4,48,128]{2,1,0:T(8,128)S(1)}, f32[4,48,128]{2,1,0:T(8,128)S(1)}, u32[]{:S(2)}, u32[]{:S(2)}) collective-permute-start(f32[4,48,128]{2,1,0:T(8,128)S(1)} %get-tuple-element.86), channel_id=1, source_target_pairs={{0,0},{8,16},{16,8},{24,24},{1,1},{9,17},{17,9},{25,25},{2,2},{10,... | collective-permute-start | bytes 294920 | tf_op jit(solution)/shard_map/ppermute | solution.py:90
  2.3 5.9 %collective-permute-start = (f32[4,48,128]{2,1,0:T(8,128)S(1)}, f32[4,48,128]{2,1,0:T(8,128)S(1)}, u32[]{:S(2)}, u32[]{:S(2)}) collective-permute-start(f32[4,48,128]{2,1,0:T(8,128)S(1)} %get-tuple-element.87), channel_id=1, source_target_pairs={{0,8},{8,0},{16,24},{24,16},{1,9},{9,1},{17,25},{25,17},{2,10},{10... | collective-permute-start | bytes 294920 | tf_op jit(solution)/shard_map/ppermute | solution.py:90
  8.2 1.3 %copy-done = f32[48,48,128]{2,1,0:T(8,128)S(1)} copy-done((f32[48,48,128]{2,1,0:T(8,128)S(1)}, f32[48,48,128]{2,1,0:T(8,128)}, u32[]{:S(2)}) %copy-start) | copy-done | bytes 1179672
  9.5 1.1 %copy-done.2 = bf16[48,48,128]{2,1,0:T(8,128)(2,1)S(1)} copy-done((bf16[48,48,128]{2,1,0:T(8,128)(2,1)S(1)}, bf16[48,48,128]{2,1,0:T(8,128)(2,1)}, u32[]{:S(2)}) %copy-start.2) | copy-done | bytes 589848
  10.5 0.5 pack_z_own.1.refs_2_
  11.1 0.1 pack_y_own.1
  11.2 0.1 pack_z_rest.1
  11.4 0.1 collective-permute-start.2
  11.5 0.3 copy-done.5
  11.7 0.1 copy-done.6
  11.9 0.4 prepare.1
  12.3 0.5 collective-permute-done.2.refs_2_.refs_3_.refs_7_
  12.8 1.6 %collective-permute-start.3 = (f32[288,128]{1,0:T(8,128)S(1)}, f32[288,128]{1,0:T(8,128)S(1)}, u32[]{:S(2)}, u32[]{:S(2)}) collective-permute-start(f32[288,128]{1,0:T(8,128)S(1)} %get-tuple-element.50), channel_id=1, source_target_pairs={{0,2},{2,0},{4,6},{6,4},{1,3},{3,1},{5,7},{7,5},{8,10},{10,8},{12,... | collective-permute-start | bytes 442376 | tf_op jit(solution)/shard_map/ppermute | solution.py:90
  14.3 0.7 %collective-permute-start.4 = (f32[288,128]{1,0:T(8,128)S(1)}, f32[288,128]{1,0:T(8,128)S(1)}, u32[]{:S(2)}, u32[]{:S(2)}) collective-permute-start(f32[288,128]{1,0:T(8,128)S(1)} %get-tuple-element.51), channel_id=1, source_target_pairs={{0,0},{2,4},{4,2},{6,6},{1,1},{3,5},{5,3},{7,7},{8,8},{10,12},{12,... | collective-permute-start | bytes 442376 | tf_op jit(solution)/shard_map/ppermute | solution.py:90
  15.0 2.4 %solve_own.1 = (f32[2688,128]{1,0:T(8,128)S(1)}, f32[2688,128]{1,0:T(8,128)S(1)}) custom-call(f32[48,48,128]{2,1,0:T(8,128)S(1)} %copy-done.1, f32[4,48,128]{2,1,0:T(8,128)S(1)} %collective-permute-done.refs_0_.refs_1_, f32[4,48,128]{2,1,0:T(8,128)S(1)} %collective-permute-done.1.refs_1_.refs_2_, ...), custom_call_target="tpu_custom_call" | custom-call | flops 4000000000 | bytes 4510720 | tf_op jit(solution)/shard_map/solve_own/pallas_call | solution.py:31
  17.4 1.4 %collective-permute-done.3.refs_3_.refs_5_ = f32[288,128]{1,0:T(8,128)S(1)} collective-permute-done((f32[288,128]{1,0:T(8,128)S(1)}, f32[288,128]{1,0:T(8,128)S(1)}, u32[]{:S(2)}, u32[]{:S(2)}) %collective-permute-start.3) | collective-permute-done | bytes 147488 | tf_op jit(solution)/shard_map/ppermute | solution.py:90
  18.8 4.2 %solve_rest.1 = (f32[3136,128]{1,0:T(8,128)S(1)}, f32[3136,128]{1,0:T(8,128)S(1)}, f32[384,128]{1,0:T(8,128)S(1)}, f32[384,128]{1,0:T(8,128)S(1)}) custom-call(f32[1,3]{1,0:T(1,128)S(1)} %bitcast.12, f32[1,56]{1,0:T(1,128)S(1)} %bitcast.10, bf16[48,48,128]{2,1,0:T(8,128)(2,1)S(1)} %copy-done.3, f32[288,128]{1,0:T(8,128)S(1)} %collective-permute-done.3.refs_3_.refs_5_, ...), custom_call_target="tpu_custom_call" | custom-call | bytes 8012012 | tf_op jit(solution)/shard_map/solve_rest/pallas_call | solution.py:31
  22.9 1.6 %collective-permute-start.5 = (f32[384,128]{1,0:T(8,128)S(1)}, f32[384,128]{1,0:T(8,128)S(1)}, u32[]{:S(2)}, u32[]{:S(2)}) collective-permute-start(f32[384,128]{1,0:T(8,128)S(1)} %get-tuple-element.62), channel_id=1, source_target_pairs={{0,8},{8,0},{16,24},{24,16},{1,9},{9,1},{17,25},{25,17},{2,10},{10... | collective-permute-start | bytes 589832 | tf_op jit(solution)/shard_map/ppermute | solution.py:90
  24.5 0.7 %collective-permute-start.6 = (f32[384,128]{1,0:T(8,128)S(1)}, f32[384,128]{1,0:T(8,128)S(1)}, u32[]{:S(2)}, u32[]{:S(2)}) collective-permute-start(f32[384,128]{1,0:T(8,128)S(1)} %get-tuple-element.63), channel_id=1, source_target_pairs={{0,0},{8,16},{16,8},{24,24},{1,1},{9,17},{17,9},{25,25},{2,2},{10,... | collective-permute-start | bytes 589832 | tf_op jit(solution)/shard_map/ppermute | solution.py:90
  25.2 1.4 %solve_tail.1 = (f32[2800,128]{1,0:T(8,128)S(1)}, f32[224,128]{1,0:T(8,128)S(1)}) custom-call(f32[3136,128]{1,0:T(8,128)S(1)} %get-tuple-element.64.refs_0_, f32[3136,128]{1,0:T(8,128)S(1)} %get-tuple-element.65.refs_1_, bf16[768,256]{1,0:T(8,128)(2,1)S(1)} %get-tuple-element.60.refs_12_.refs_2_), custom_call_target="tpu_custom_call" | custom-call | flops 2000000000 | bytes 5152768 | tf_op jit(solution)/shard_map/solve_tail/pallas_call | solution.py:31
  26.6 2.5 %collective-permute-done.5.refs_0_.refs_3_ = f32[384,128]{1,0:T(8,128)S(1)} collective-permute-done((f32[384,128]{1,0:T(8,128)S(1)}, f32[384,128]{1,0:T(8,128)S(1)}, u32[]{:S(2)}, u32[]{:S(2)}) %collective-permute-start.5) | collective-permute-done | bytes 196640 | tf_op jit(solution)/shard_map/ppermute | solution.py:90
  29.2 0.1 fold_x.1.refs_0_.refs_1_
  29.4 1.2 %weights.1 = (f32[49,48,128]{2,1,0:T(8,128)S(1)}, f32[48,56,128]{2,1,0:T(8,128)S(1)}, f32[48,48,128]{2,1,0:T(8,128)S(1)}, f32[48,48,128]{2,1,0:T(8,128)S(1)}, f32[1,128]{1,0:T(1,128)S(1)}) custom-call(f32[1,3]{1,0:T(1,128)S(1)} %bitcast.13, f32[48,48,128]{2,1,0:T(8,128)S(1)} %copy-done.1, bf16[48,48,128]{2,1,0:T(8,128)(2,1)S(1)} %copy-done.3, ...), custom_call_target="tpu_custom_call" | custom-call | flops 2000000000 | bytes 7496204 | tf_op jit(solution)/shard_map/weights/pallas_call | solution.py:31
  30.6 0.2 pack_back_y.1
  30.8 5.7 %collective-permute-start.8 = (f32[270,128]{1,0:T(8,128)S(1)}, f32[270,128]{1,0:T(8,128)S(1)}, u32[]{:S(2)}, u32[]{:S(2)}) collective-permute-start(f32[270,128]{1,0:T(8,128)S(1)} %get-tuple-element.69), channel_id=1, source_target_pairs={{0,2},{2,0},{4,6},{6,4},{1,3},{3,1},{5,7},{7,5},{8,10},{10,8},{12,... | collective-permute-start | bytes 414728 | tf_op jit(solution)/shard_map/ppermute | solution.py:90
  36.5 0.7 %collective-permute-start.9 = (f32[270,128]{1,0:T(8,128)S(1)}, f32[270,128]{1,0:T(8,128)S(1)}, u32[]{:S(2)}, u32[]{:S(2)}) collective-permute-start(f32[270,128]{1,0:T(8,128)S(1)} %get-tuple-element.70), channel_id=1, source_target_pairs={{0,0},{2,4},{4,2},{6,6},{1,1},{3,5},{5,3},{7,7},{8,8},{10,12},{12,... | collective-permute-start | bytes 414728 | tf_op jit(solution)/shard_map/ppermute | solution.py:90
  37.2 2.4 %inner.1 = (f32[50,64,128]{2,1,0:T(8,128)S(1)}, f32[192,128]{1,0:T(8,128)S(1)}, f32[48,48,128]{2,1,0:T(8,128)S(1)}, f32[24,128]{1,0:T(8,128)S(1)}) custom-call(f32[48,48,128]{2,1,0:T(8,128)S(1)} %copy-done.1, f32[2800,128]{1,0:T(8,128)S(1)} %fold_x.1.refs_0_.refs_1_, f32[224,128]{1,0:T(8,128)S(1)} %collective-permute-done.7.refs_2_, ...), custom_call_target="tpu_custom_call" | custom-call | flops 2000000000 | bytes 10711040 | tf_op jit(solution)/shard_map/inner/pallas_call | solution.py:31
  39.5 1.5 %collective-permute-done.8.refs_1_ = f32[270,128]{1,0:T(8,128)S(1)} collective-permute-done((f32[270,128]{1,0:T(8,128)S(1)}, f32[270,128]{1,0:T(8,128)S(1)}, u32[]{:S(2)}, u32[]{:S(2)}) %collective-permute-start.8) | collective-permute-done | bytes 138272 | tf_op jit(solution)/shard_map/ppermute | solution.py:90
  41.0 1.0 %outer.1 = (f32[50,64,128]{2,1,0:T(8,128)S(1)}, f32[192,128]{1,0:T(8,128)S(1)}, f32[48,48,128]{2,1,0:T(8,128)S(1)}, f32[32,128]{1,0:T(8,128)S(1)}) custom-call(f32[48,48,128]{2,1,0:T(8,128)S(1)} %copy-done.1, f32[270,128]{1,0:T(8,128)S(1)} %collective-permute-done.8.refs_1_, ...), custom_call_target="tpu_custom_call", output_to_operand_aliasing={{0}: (8, {}), {1}: (9, {}), {2}: (10, {})} | custom-call | bytes 12257792 | tf_op jit(solution)/shard_map/outer/pallas_call | solution.py:31
  42.0 14.7 %all_to_all.11 = f32[32,1,128]{2,1,0:T(1,128)S(1)} all-to-all(f32[32,1,128]{2,1,0:T(1,128)S(1)} %bitcast.9), channel_id=1, replica_groups=mesh['gx'=4,'gy'=4,'gz'=2] {'gx','gy','gz'}, dimensions={0} | all-to-all | bytes 32768 | tf_op jit(solution)/shard_map/all_to_all | solution.py:872
  56.7 2.3 %finish.1 = (f32[48,48,128]{2,1,0:T(8,128)}, f32[48,48,128]{2,1,0:T(8,128)}) custom-call(f32[32,128]{1,0:T(8,128)S(1)} %bitcast.8, f32[32,32]{1,0:T(8,128)S(1)} %get-tuple-element.83.refs_1_, f32[50,64,128]{2,1,0:T(8,128)S(1)} %get-tuple-element.84.refs_2_, f32[48,48,128]{2,1,0:T(8,128)S(1)} %get-tuple-element.85.refs_3_, ...), custom_call_target="tpu_custom_call" | custom-call | bytes 10137600 | tf_op jit(solution)/shard_map/finish/pallas_call | solution.py:31
  (29 shorter events, 0.2 us)
Async XLA Ops:
  1.6 9.6 %collective-permute-start.1 = (f32[4,48,128]{2,1,0:T(8,128)S(1)}, f32[4,48,128]{2,1,0:T(8,128)S(1)}, u32[]{:S(2)}, u32[]{:S(2)}) collective-permute-start(f32[4,48,128]{2,1,0:T(8,128)S(1)} %get-tuple-element.86), channel_id=1, source_target_pairs={{0,0},{8,16},{16,8},{24,24},{1,1},{9,17},{17,9},{25,25},{2,2},{10,... | collective-permute-start | bytes 294920 | tf_op jit(solution)/shard_map/ppermute | solution.py:90
  2.3 9.0 %collective-permute-start = (f32[4,48,128]{2,1,0:T(8,128)S(1)}, f32[4,48,128]{2,1,0:T(8,128)S(1)}, u32[]{:S(2)}, u32[]{:S(2)}) collective-permute-start(f32[4,48,128]{2,1,0:T(8,128)S(1)} %get-tuple-element.87), channel_id=1, source_target_pairs={{0,8},{8,0},{16,24},{24,16},{1,9},{9,1},{17,25},{25,17},{2,10},{10... | collective-permute-start | bytes 294920 | tf_op jit(solution)/shard_map/ppermute | solution.py:90
  8.2 1.3 %copy-start = (f32[48,48,128]{2,1,0:T(8,128)S(1)}, f32[48,48,128]{2,1,0:T(8,128)}, u32[]{:S(2)}) copy-start(f32[48,48,128]{2,1,0:T(8,128)} %refs_7_.1) | copy-start | bytes 3538948
  9.5 1.1 %copy-start.2 = (bf16[48,48,128]{2,1,0:T(8,128)(2,1)S(1)}, bf16[48,48,128]{2,1,0:T(8,128)(2,1)}, u32[]{:S(2)}) copy-start(bf16[48,48,128]{2,1,0:T(8,128)(2,1)} %refs_2_.5) | copy-start | bytes 1769476
  11.1 0.7 %copy-start.5 = (f32[3]{0:T(128)S(1)}, f32[3]{0:T(128)}, u32[]{:S(2)}) copy-start(f32[3]{0:T(128)} %param.12) | copy-start | bytes 40
  11.1 0.8 %copy-start.6 = (f32[72,72]{1,0:T(8,128)S(1)}, f32[72,72]{1,0:T(8,128)}, u32[]{:S(2)}) copy-start(f32[72,72]{1,0:T(8,128)} %refs_3_) | copy-start | bytes 62212
  11.1 0.8 %copy-start.7 = (f32[56,56]{1,0:T(8,128)S(1)}, f32[56,56]{1,0:T(8,128)}, u32[]{:S(2)}) copy-start(f32[56,56]{1,0:T(8,128)} %refs_1_.6) | copy-start | bytes 37636
  11.1 0.8 %copy-start.8 = (f32[56,56]{1,0:T(8,128)S(1)}, f32[56,56]{1,0:T(8,128)}, u32[]{:S(2)}) copy-start(f32[56,56]{1,0:T(8,128)} %refs_2_.3) | copy-start | bytes 37636
  11.1 0.8 %copy-start.9 = (f32[16,16]{1,0:T(8,128)S(1)}, f32[16,16]{1,0:T(8,128)}, u32[]{:S(2)}) copy-start(f32[16,16]{1,0:T(8,128)} %refs_6_.1) | copy-start | bytes 3076
  11.1 0.7 %copy-start.10 = (f32[56]{0:T(128)S(1)}, f32[56]{0:T(128)}, u32[]{:S(2)}) copy-start(f32[56]{0:T(128)} %param.17) | copy-start | bytes 676
  11.1 0.7 %copy-start.11 = (f32[72]{0:T(128)S(1)}, f32[72]{0:T(128)}, u32[]{:S(2)}) copy-start(f32[72]{0:T(128)} %param.18) | copy-start | bytes 868
  11.4 1.4 %collective-permute-start.2 = (f32[192,128]{1,0:T(8,128)S(1)}, f32[192,128]{1,0:T(8,128)S(1)}, u32[]{:S(2)}, u32[]{:S(2)}) collective-permute-start(f32[192,128]{1,0:T(8,128)S(1)} %pack_z_rest.1), channel_id=1, source_target_pairs={{0,1},{1,0},{2,3},{3,2},{4,5},{5,4},{6,7},{7,6},{8,9},{9,8},{10,11... | collective-permute-start | bytes 294920 | tf_op jit(solution)/shard_map/ppermute | solution.py:77
  11.9 3.1 %copy-start.1 = (f32[48,48,128]{2,1,0:T(8,128)S(1)}, f32[48,48,128]{2,1,0:T(8,128)}, u32[]{:S(2)}) copy-start(f32[48,48,128]{2,1,0:T(8,128)} %refs_7_.1) | copy-start | bytes 3538948
  12.8 6.0 %collective-permute-start.3 = (f32[288,128]{1,0:T(8,128)S(1)}, f32[288,128]{1,0:T(8,128)S(1)}, u32[]{:S(2)}, u32[]{:S(2)}) collective-permute-start(f32[288,128]{1,0:T(8,128)S(1)} %get-tuple-element.50), channel_id=1, source_target_pairs={{0,2},{2,0},{4,6},{6,4},{1,3},{3,1},{5,7},{7,5},{8,10},{10,8},{12,... | collective-permute-start | bytes 442376 | tf_op jit(solution)/shard_map/ppermute | solution.py:90
  14.3 4.4 %collective-permute-start.4 = (f32[288,128]{1,0:T(8,128)S(1)}, f32[288,128]{1,0:T(8,128)S(1)}, u32[]{:S(2)}, u32[]{:S(2)}) collective-permute-start(f32[288,128]{1,0:T(8,128)S(1)} %get-tuple-element.51), channel_id=1, source_target_pairs={{0,0},{2,4},{4,2},{6,6},{1,1},{3,5},{5,3},{7,7},{8,8},{10,12},{12,... | collective-permute-start | bytes 442376 | tf_op jit(solution)/shard_map/ppermute | solution.py:90
  15.0 3.7 %copy-start.3 = (bf16[48,48,128]{2,1,0:T(8,128)(2,1)S(1)}, bf16[48,48,128]{2,1,0:T(8,128)(2,1)}, u32[]{:S(2)}) copy-start(bf16[48,48,128]{2,1,0:T(8,128)(2,1)} %refs_2_.5) | copy-start | bytes 1769476
  15.0 3.7 %copy-start.4 = (f32[56]{0:T(128)S(1)}, f32[56]{0:T(128)}, u32[]{:S(2)}) copy-start(f32[56]{0:T(128)} %param.16) | copy-start | bytes 676
  22.9 6.2 %collective-permute-start.5 = (f32[384,128]{1,0:T(8,128)S(1)}, f32[384,128]{1,0:T(8,128)S(1)}, u32[]{:S(2)}, u32[]{:S(2)}) collective-permute-start(f32[384,128]{1,0:T(8,128)S(1)} %get-tuple-element.62), channel_id=1, source_target_pairs={{0,8},{8,0},{16,24},{24,16},{1,9},{9,1},{17,25},{25,17},{2,10},{10... | collective-permute-start | bytes 589832 | tf_op jit(solution)/shard_map/ppermute | solution.py:90
  24.5 4.6 %collective-permute-start.6 = (f32[384,128]{1,0:T(8,128)S(1)}, f32[384,128]{1,0:T(8,128)S(1)}, u32[]{:S(2)}, u32[]{:S(2)}) collective-permute-start(f32[384,128]{1,0:T(8,128)S(1)} %get-tuple-element.63), channel_id=1, source_target_pairs={{0,0},{8,16},{16,8},{24,24},{1,1},{9,17},{17,9},{25,25},{2,2},{10,... | collective-permute-start | bytes 589832 | tf_op jit(solution)/shard_map/ppermute | solution.py:90
  29.2 1.4 %collective-permute-start.7 = (f32[224,128]{1,0:T(8,128)S(1)}, f32[224,128]{1,0:T(8,128)S(1)}, u32[]{:S(2)}, u32[]{:S(2)}) collective-permute-start(f32[224,128]{1,0:T(8,128)S(1)} %pack_back_z.1.refs_1_), channel_id=1, source_target_pairs={{0,1},{1,0},{2,3},{3,2},{4,5},{5,4},{6,7},{7,6},{8,9},{9,8},{10,11... | collective-permute-start | bytes 344072 | tf_op jit(solution)/shard_map/ppermute | solution.py:77
  30.8 10.2 %collective-permute-start.8 = (f32[270,128]{1,0:T(8,128)S(1)}, f32[270,128]{1,0:T(8,128)S(1)}, u32[]{:S(2)}, u32[]{:S(2)}) collective-permute-start(f32[270,128]{1,0:T(8,128)S(1)} %get-tuple-element.69), channel_id=1, source_target_pairs={{0,2},{2,0},{4,6},{6,4},{1,3},{3,1},{5,7},{7,5},{8,10},{10,8},{12,... | collective-permute-start | bytes 414728 | tf_op jit(solution)/shard_map/ppermute | solution.py:90
  36.5 4.5 %collective-permute-start.9 = (f32[270,128]{1,0:T(8,128)S(1)}, f32[270,128]{1,0:T(8,128)S(1)}, u32[]{:S(2)}, u32[]{:S(2)}) collective-permute-start(f32[270,128]{1,0:T(8,128)S(1)} %get-tuple-element.70), channel_id=1, source_target_pairs={{0,0},{2,4},{4,2},{6,6},{1,1},{3,5},{5,3},{7,7},{8,8},{10,12},{12,... | collective-permute-start | bytes 414728 | tf_op jit(solution)/shard_map/ppermute | solution.py:90

commit v5 on v4

--- a/solution.py
+++ b/solution.py
@@ -356,16 +356,37 @@
     high, high_rims = z_back(sides, wide_y, back_a, back_b, bz, wide - RIM, RIM)
     first[0:ends] = jnp.where(even, high, low)
     second[0:ends] = jnp.where(even, low, high)
-    for side in range(sides):
-        low = sum(low_rims[side].values())
-        high = sum(high_rims[side].values())
-        at = ends + side * wide_y
-        first[at : at + wide_y] = jnp.where(even, high, low)
-        second[at : at + wide_y] = jnp.where(even, low, high)
+    third = fold_rows(wide_y)
+    for side in range(sides):
+        low = folded(sum(low_rims[side].values()), 0)
+        high = folded(sum(high_rims[side].values()), (wide - RIM) % GROUP * SLOT)
+        at = ends + side * third
+        first[at : at + third] = jnp.where(even, high, low)
+        second[at : at + third] = jnp.where(even, low, high)
     low, high = scale[0].astype(F32), scale[scale.shape[0] - 1].astype(F32)
-    at = ends + sides * wide_y
+    at = ends + sides * third
     first[at : at + ext_y] = jnp.where(even, high, low)
     second[at : at + ext_y] = jnp.where(even, low, high)
+
+
+def fold_rows(rows):
+    return (rows // 3 + 7) // 8 * 8
+
+
+def folded(value, start):
+    third, lanes = fold_rows(value.shape[0]), RIM * SLOT
+    value = pltpu.roll(value, LANES - start, 1) if start else value
+    last = jnp.concatenate([value[2 * third :], jnp.zeros((3 * third - value.shape[0], LANES), F32)], axis=0)
+    return value[:third] + pltpu.roll(value[third : 2 * third], lanes, 1) + pltpu.roll(last, 2 * lanes, 1)
+
+
+def unfolded(value, rows, start):
+    third, lanes = value.shape[0], RIM * SLOT
+    parts = [value, pltpu.roll(value, LANES - lanes, 1), pltpu.roll(value, LANES - 2 * lanes, 1)[: rows - 2 * third]]
+    whole = jnp.concatenate(parts, axis=0)
+    whole = pltpu.roll(whole, start, 1) if start else whole
+    lane = iota(whole.shape, 1)
+    return jnp.where((lane >= start) & (lane < start + lanes), whole, 0.0)
 
 
 def z_back(sides, wide_y, back_a, back_b, bz, start, count):
@@ -419,7 +440,7 @@
     for side in range(sides):
         for group in range((wide + GROUP - 1) // GROUP):
             part = slice(group * wide_y, (group + 1) * wide_y)
-            more = faces(side, group, slice(0, wide_y))
+            more = faces(side, group)
             out[side][part] = own[side][part] if more is None else own[side][part] + more
 
 
@@ -475,14 +496,13 @@
             return None
         return source(slice(at + rows.start, at + rows.stop))
 
-    def faces(side, group, rows):
-        lane = iota((rows.stop - rows.start, LANES), 1)
-        at = (RIM + side) * wide_y
-        rows = slice(at + rows.start, at + rows.stop)
+    def faces(side, group):
+        third = fold_rows(wide_y)
+        rows = slice(RIM * wide_y + side * third, RIM * wide_y + (side + 1) * third)
         if group == 0:
-            return jnp.where((lane >= (OV - 1) * SLOT) & (lane < 2 * OV * SLOT), low(rows), 0.0)
+            return unfolded(low(rows), wide_y, (OV - 1) * SLOT)
         if group == (wide + GROUP - 1) // GROUP - 1:
-            return jnp.where((lane >= high_lane) & (lane < high_lane + RIM * SLOT), high(rows), 0.0)
+            return unfolded(high(rows), wide_y, high_lane)
         return None
 
     return plane, faces
@@ -797,7 +817,7 @@
     *back, low, high = run(
         bind(solve_rest_kernel, sizes, sides),
         "solve_rest",
-        [field] * 2 + [shape([(RIM + sides) * wide_y + ext_y, depth])] * 2,
+        [field] * 2 + [shape([RIM * wide_y + sides * fold_rows(wide_y) + ext_y, depth])] * 2,
         [axes_row, x_values.reshape(1, -1), scale, *ys, *owns, *mats],
         [VMEM] * (7 + len(mats)),
         [edge] * 4 + [tall] * 2,
@@ -822,7 +842,6 @@
         [*back_xs, *own_rims],
         [VMEM] * (2 + sides),
     )
-    late_rims, own_rims = lax.optimization_barrier((rims, own_rims))
     other_rims = swap_sides(own_rims, sizes)
     field_x = run(
         bind(fold_x_kernel, sizes, wide_x, wide_y),
@@ -832,6 +851,16 @@
         [VMEM] * 3,
         flops=beside,
     )[0]
+    *faces, low, high = run(
+        bind(pack_back_y_kernel, sides, wide_x, wide_y),
+        "pack_back_y",
+        [rim_message] * sides + [shape([(planes + groups * sides) * RIM, depth])] * 2,
+        [field_x, *own_rims, *other_rims],
+        [VMEM] * (1 + 2 * sides),
+    )
+    back_ys = swap_ends(low, high, "gy", sizes)
+
+    faces, late_rims = lax.optimization_barrier((faces, rims))
     scale_block = pltpu.VMEM((planes, ext_y + 16, depth), F32)
     *weights, fixed = run(
         bind(weights_kernel, sizes, sides),
@@ -842,14 +871,6 @@
         [scale_block],
         flops=beside,
     )
-    *faces, low, high = run(
-        bind(pack_back_y_kernel, sides, wide_x, wide_y),
-        "pack_back_y",
-        [rim_message] * sides + [shape([(planes + groups * sides) * RIM, depth])] * 2,
-        [field_x, *own_rims, *other_rims],
-        [VMEM] * (1 + 2 * sides),
-    )
-    back_ys = swap_ends(low, high, "gy", sizes)
 
     parts = [shape([planes, ext_y + 16, depth]), shape([sides * groups * ext_y, LANES]), block]
     inner = run(

time: 59.3 us -> 58.7 us (0.990)
  waiting for transfers between devices: 5.84 us -> 5.15 us
    ppermute x8, waiting for transfers between devices: 5.37 us -> 3.51 us  [swap_ends(): received.append(lax.ppermute(message, axis, list(enumerate(partner))))]
    ppermute x2, waiting for transfers between devices: 0.47 us -> 1.63 us  [swap_sides(): return [lax.ppermute(messages[0], 'gz', [(0, 1), (1, 0)])]]
  transfers between devices with their start and end apart: 10 -> 10, of which waited for: 4 -> 4; matrix products, arithmetic and copies ran while one was open for 0% -> 0% of each run, Pallas kernels for 14% -> 15%
where the time goes in v5:
time: 58.7 us; the launch traced here: 58.4 us
  starting transfers between devices  17.4 us (30%)
  Pallas kernels  16.5 us (28%)
  blocking collectives  14.6 us (25%)
  waiting for transfers between devices  5.15 us (9%)
  local copies, waits for them, and re-layouts  3.74 us (6%)
  between operations  0.89 us (2%)
    ppermute x8, starting transfers between devices, swap_ends(): received.append(lax.ppermute(message, axis, list(enumerate(partner))))  17.4 us
    pallas_call x15, Pallas kernels, call(): pl.pallas_call(placed, out_shape=outs, in_specs=spaces, out_specs=out_spe...  16.5 us
    all_to_all x1, blocking collectives, body(): sums = lax.all_to_all(sums, MESH_AXES, 0, 0, tiled=True)  14.6 us
    ppermute x8, waiting for transfers between devices, swap_ends(): received.append(lax.ppermute(message, axis, list(enumerate(partner))))  3.51 us
    unnamed x24, local copies, waits for them, and re-layouts  2.78 us
    ppermute x2, waiting for transfers between devices, swap_sides(): return [lax.ppermute(messages[0], 'gz', [(0, 1), (1, 0)])]  1.63 us
  transfers between devices with their start and end apart: 10, of which 4 were waited for; matrix products, arithmetic and copies ran while one was open for 0% of the time, Pallas kernels for 15%

profile of v5, /device:TPU:0, one launch (start us, length us, event | category | flops | bytes accessed | tf_op | source)
XLA Modules:
  0.0 58.4 jit_solution(10880046331127384832)
XLA Ops:
  0.6 1.0 %constant_dynamic-slice_fusion = (f32[4,48,128]{2,1,0:T(8,128)S(1)}, f32[4,48,128]{2,1,0:T(8,128)S(1)}) fusion(f32[48,48,128]{2,1,0:T(8,128)} %refs_7_.1, s32[]{:T(128)S(6)} %select_n.10, s32[]{:T(128)S(6)} %select_n.9), kind=kLoop, calls=%fused_computation | loop fusion | bytes 393224 | tf_op jit(solution)/shard_map/dynamic_slice | solution.py:755
  1.6 0.7 %collective-permute-start.1 = (f32[4,48,128]{2,1,0:T(8,128)S(1)}, f32[4,48,128]{2,1,0:T(8,128)S(1)}, u32[]{:S(2)}, u32[]{:S(2)}) collective-permute-start(f32[4,48,128]{2,1,0:T(8,128)S(1)} %get-tuple-element.86), channel_id=1, source_target_pairs={{0,0},{8,16},{16,8},{24,24},{1,1},{9,17},{17,9},{25,25},{2,2},{10,... | collective-permute-start | bytes 294920 | tf_op jit(solution)/shard_map/ppermute | solution.py:90
  2.3 5.9 %collective-permute-start = (f32[4,48,128]{2,1,0:T(8,128)S(1)}, f32[4,48,128]{2,1,0:T(8,128)S(1)}, u32[]{:S(2)}, u32[]{:S(2)}) collective-permute-start(f32[4,48,128]{2,1,0:T(8,128)S(1)} %get-tuple-element.87), channel_id=1, source_target_pairs={{0,8},{8,0},{16,24},{24,16},{1,9},{9,1},{17,25},{25,17},{2,10},{10... | collective-permute-start | bytes 294920 | tf_op jit(solution)/shard_map/ppermute | solution.py:90
  8.2 1.3 %copy-done = f32[48,48,128]{2,1,0:T(8,128)S(1)} copy-done((f32[48,48,128]{2,1,0:T(8,128)S(1)}, f32[48,48,128]{2,1,0:T(8,128)}, u32[]{:S(2)}) %copy-start) | copy-done | bytes 1179672
  9.5 1.1 %copy-done.2 = bf16[48,48,128]{2,1,0:T(8,128)(2,1)S(1)} copy-done((bf16[48,48,128]{2,1,0:T(8,128)(2,1)S(1)}, bf16[48,48,128]{2,1,0:T(8,128)(2,1)}, u32[]{:S(2)}) %copy-start.2) | copy-done | bytes 589848
  10.5 0.5 pack_z_own.1.refs_2_
  11.1 0.1 pack_y_own.1
  11.2 0.1 pack_z_rest.1
  11.5 0.3 copy-done.5
  11.7 0.1 copy-done.6
  11.9 0.4 prepare.1
  12.3 0.5 collective-permute-done.2.refs_2_.refs_3_.refs_7_
  12.8 1.6 %collective-permute-start.3 = (f32[288,128]{1,0:T(8,128)S(1)}, f32[288,128]{1,0:T(8,128)S(1)}, u32[]{:S(2)}, u32[]{:S(2)}) collective-permute-start(f32[288,128]{1,0:T(8,128)S(1)} %get-tuple-element.50), channel_id=1, source_target_pairs={{0,2},{2,0},{4,6},{6,4},{1,3},{3,1},{5,7},{7,5},{8,10},{10,8},{12,... | collective-permute-start | bytes 442376 | tf_op jit(solution)/shard_map/ppermute | solution.py:90
  14.3 0.7 %collective-permute-start.4 = (f32[288,128]{1,0:T(8,128)S(1)}, f32[288,128]{1,0:T(8,128)S(1)}, u32[]{:S(2)}, u32[]{:S(2)}) collective-permute-start(f32[288,128]{1,0:T(8,128)S(1)} %get-tuple-element.51), channel_id=1, source_target_pairs={{0,0},{2,4},{4,2},{6,6},{1,1},{3,5},{5,3},{7,7},{8,8},{10,12},{12,... | collective-permute-start | bytes 442376 | tf_op jit(solution)/shard_map/ppermute | solution.py:90
  15.0 2.4 %solve_own.1 = (f32[2688,128]{1,0:T(8,128)S(1)}, f32[2688,128]{1,0:T(8,128)S(1)}) custom-call(f32[48,48,128]{2,1,0:T(8,128)S(1)} %copy-done.1, f32[4,48,128]{2,1,0:T(8,128)S(1)} %collective-permute-done.refs_0_.refs_1_, f32[4,48,128]{2,1,0:T(8,128)S(1)} %collective-permute-done.1.refs_1_.refs_2_, ...), custom_call_target="tpu_custom_call" | custom-call | flops 4000000000 | bytes 4510720 | tf_op jit(solution)/shard_map/solve_own/pallas_call | solution.py:31
  17.4 1.4 %collective-permute-done.3.refs_3_.refs_5_ = f32[288,128]{1,0:T(8,128)S(1)} collective-permute-done((f32[288,128]{1,0:T(8,128)S(1)}, f32[288,128]{1,0:T(8,128)S(1)}, u32[]{:S(2)}, u32[]{:S(2)}) %collective-permute-start.3) | collective-permute-done | bytes 147488 | tf_op jit(solution)/shard_map/ppermute | solution.py:90
  18.8 4.3 %solve_rest.1 = (f32[3136,128]{1,0:T(8,128)S(1)}, f32[3136,128]{1,0:T(8,128)S(1)}, f32[352,128]{1,0:T(8,128)S(1)}, f32[352,128]{1,0:T(8,128)S(1)}) custom-call(f32[1,3]{1,0:T(1,128)S(1)} %bitcast.12, f32[1,56]{1,0:T(1,128)S(1)} %bitcast.10, bf16[48,48,128]{2,1,0:T(8,128)(2,1)S(1)} %copy-done.3, f32[288,128]{1,0:T(8,128)S(1)} %collective-permute-done.3.refs_3_.refs_5_, ...), custom_call_target="tpu_custom_call" | custom-call | bytes 7979244 | tf_op jit(solution)/shard_map/solve_rest/pallas_call | solution.py:31
  23.0 1.6 %collective-permute-start.5 = (f32[352,128]{1,0:T(8,128)S(1)}, f32[352,128]{1,0:T(8,128)S(1)}, u32[]{:S(2)}, u32[]{:S(2)}) collective-permute-start(f32[352,128]{1,0:T(8,128)S(1)} %get-tuple-element.62), channel_id=1, source_target_pairs={{0,8},{8,0},{16,24},{24,16},{1,9},{9,1},{17,25},{25,17},{2,10},{10... | collective-permute-start | bytes 540680 | tf_op jit(solution)/shard_map/ppermute | solution.py:90
  24.6 0.7 %collective-permute-start.6 = (f32[352,128]{1,0:T(8,128)S(1)}, f32[352,128]{1,0:T(8,128)S(1)}, u32[]{:S(2)}, u32[]{:S(2)}) collective-permute-start(f32[352,128]{1,0:T(8,128)S(1)} %get-tuple-element.63), channel_id=1, source_target_pairs={{0,0},{8,16},{16,8},{24,24},{1,1},{9,17},{17,9},{25,25},{2,2},{10,... | collective-permute-start | bytes 540680 | tf_op jit(solution)/shard_map/ppermute | solution.py:90
  25.3 1.4 %solve_tail.1 = (f32[2800,128]{1,0:T(8,128)S(1)}, f32[224,128]{1,0:T(8,128)S(1)}) custom-call(f32[3136,128]{1,0:T(8,128)S(1)} %get-tuple-element.64.refs_0_, f32[3136,128]{1,0:T(8,128)S(1)} %get-tuple-element.65.refs_1_, bf16[768,256]{1,0:T(8,128)(2,1)S(1)} %get-tuple-element.60.refs_12_.refs_2_), custom_call_target="tpu_custom_call" | custom-call | flops 2000000000 | bytes 5152768 | tf_op jit(solution)/shard_map/solve_tail/pallas_call | solution.py:31
  26.7 2.1 %collective-permute-done.5.refs_0_.refs_3_ = f32[352,128]{1,0:T(8,128)S(1)} collective-permute-done((f32[352,128]{1,0:T(8,128)S(1)}, f32[352,128]{1,0:T(8,128)S(1)}, u32[]{:S(2)}, u32[]{:S(2)}) %collective-permute-start.5) | collective-permute-done | bytes 180256 | tf_op jit(solution)/shard_map/ppermute | solution.py:90
  28.9 0.2 pack_back_z.1.refs_1_
  29.1 0.1 fold_x.1.refs_0_.refs_1_
  29.2 1.2 %collective-permute-done.7.refs_2_ = f32[224,128]{1,0:T(8,128)S(1)} collective-permute-done((f32[224,128]{1,0:T(8,128)S(1)}, f32[224,128]{1,0:T(8,128)S(1)}, u32[]{:S(2)}, u32[]{:S(2)}) %collective-permute-start.7) | collective-permute-done | bytes 114720 | tf_op jit(solution)/shard_map/ppermute | solution.py:77
  30.4 0.2 pack_back_y.1
  30.6 5.7 %collective-permute-start.8 = (f32[270,128]{1,0:T(8,128)S(1)}, f32[270,128]{1,0:T(8,128)S(1)}, u32[]{:S(2)}, u32[]{:S(2)}) collective-permute-start(f32[270,128]{1,0:T(8,128)S(1)} %get-tuple-element.68), channel_id=1, source_target_pairs={{0,2},{2,0},{4,6},{6,4},{1,3},{3,1},{5,7},{7,5},{8,10},{10,8},{12,... | collective-permute-start | bytes 414728 | tf_op jit(solution)/shard_map/ppermute | solution.py:90
  36.3 0.7 %collective-permute-start.9 = (f32[270,128]{1,0:T(8,128)S(1)}, f32[270,128]{1,0:T(8,128)S(1)}, u32[]{:S(2)}, u32[]{:S(2)}) collective-permute-start(f32[270,128]{1,0:T(8,128)S(1)} %get-tuple-element.69), channel_id=1, source_target_pairs={{0,0},{2,4},{4,2},{6,6},{1,1},{3,5},{5,3},{7,7},{8,8},{10,12},{12,... | collective-permute-start | bytes 414728 | tf_op jit(solution)/shard_map/ppermute | solution.py:90
  36.9 1.2 %weights.1 = (f32[49,48,128]{2,1,0:T(8,128)S(1)}, f32[48,56,128]{2,1,0:T(8,128)S(1)}, f32[48,48,128]{2,1,0:T(8,128)S(1)}, f32[48,48,128]{2,1,0:T(8,128)S(1)}, f32[1,128]{1,0:T(1,128)S(1)}) custom-call(f32[1,3]{1,0:T(1,128)S(1)} %bitcast.13, f32[48,48,128]{2,1,0:T(8,128)S(1)} %copy-done.1, bf16[48,48,128]{2,1,0:T(8,128)(2,1)S(1)} %copy-done.3, ...), custom_call_target="tpu_custom_call" | custom-call | flops 2000000000 | bytes 7463436 | tf_op jit(solution)/shard_map/weights/pallas_call | solution.py:31
  38.2 2.4 %inner.1 = (f32[50,64,128]{2,1,0:T(8,128)S(1)}, f32[192,128]{1,0:T(8,128)S(1)}, f32[48,48,128]{2,1,0:T(8,128)S(1)}, f32[24,128]{1,0:T(8,128)S(1)}) custom-call(f32[48,48,128]{2,1,0:T(8,128)S(1)} %copy-done.1, f32[2800,128]{1,0:T(8,128)S(1)} %fold_x.1.refs_0_.refs_1_, f32[224,128]{1,0:T(8,128)S(1)} %collective-permute-done.7.refs_2_, ...), custom_call_target="tpu_custom_call" | custom-call | flops 2000000000 | bytes 10711040 | tf_op jit(solution)/shard_map/inner/pallas_call | solution.py:31
  40.5 1.0 %outer.1 = (f32[50,64,128]{2,1,0:T(8,128)S(1)}, f32[192,128]{1,0:T(8,128)S(1)}, f32[48,48,128]{2,1,0:T(8,128)S(1)}, f32[32,128]{1,0:T(8,128)S(1)}) custom-call(f32[48,48,128]{2,1,0:T(8,128)S(1)} %copy-done.1, f32[270,128]{1,0:T(8,128)S(1)} %collective-permute-done.8.refs_1_, ...), custom_call_target="tpu_custom_call", output_to_operand_aliasing={{0}: (8, {}), {1}: (9, {}), {2}: (10, {})} | custom-call | bytes 12257792 | tf_op jit(solution)/shard_map/outer/pallas_call | solution.py:31
  41.5 14.6 %all_to_all.11 = f32[32,1,128]{2,1,0:T(1,128)S(1)} all-to-all(f32[32,1,128]{2,1,0:T(1,128)S(1)} %bitcast.9), channel_id=1, replica_groups=mesh['gx'=4,'gy'=4,'gz'=2] {'gx','gy','gz'}, dimensions={0} | all-to-all | bytes 32768 | tf_op jit(solution)/shard_map/all_to_all | solution.py:893
  56.1 2.2 %finish.1 = (f32[48,48,128]{2,1,0:T(8,128)}, f32[48,48,128]{2,1,0:T(8,128)}) custom-call(f32[32,128]{1,0:T(8,128)S(1)} %bitcast.8, f32[32,32]{1,0:T(8,128)S(1)} %get-tuple-element.83.refs_1_, f32[50,64,128]{2,1,0:T(8,128)S(1)} %get-tuple-element.84.refs_2_, f32[48,48,128]{2,1,0:T(8,128)S(1)} %get-tuple-element.85.refs_3_, ...), custom_call_target="tpu_custom_call" | custom-call | bytes 10137600 | tf_op jit(solution)/shard_map/finish/pallas_call | solution.py:31
  (29 shorter events, 0.2 us)
Async XLA Ops:
  1.6 9.6 %collective-permute-start.1 = (f32[4,48,128]{2,1,0:T(8,128)S(1)}, f32[4,48,128]{2,1,0:T(8,128)S(1)}, u32[]{:S(2)}, u32[]{:S(2)}) collective-permute-start(f32[4,48,128]{2,1,0:T(8,128)S(1)} %get-tuple-element.86), channel_id=1, source_target_pairs={{0,0},{8,16},{16,8},{24,24},{1,1},{9,17},{17,9},{25,25},{2,2},{10,... | collective-permute-start | bytes 294920 | tf_op jit(solution)/shard_map/ppermute | solution.py:90
  2.3 9.0 %collective-permute-start = (f32[4,48,128]{2,1,0:T(8,128)S(1)}, f32[4,48,128]{2,1,0:T(8,128)S(1)}, u32[]{:S(2)}, u32[]{:S(2)}) collective-permute-start(f32[4,48,128]{2,1,0:T(8,128)S(1)} %get-tuple-element.87), channel_id=1, source_target_pairs={{0,8},{8,0},{16,24},{24,16},{1,9},{9,1},{17,25},{25,17},{2,10},{10... | collective-permute-start | bytes 294920 | tf_op jit(solution)/shard_map/ppermute | solution.py:90
  8.2 1.3 %copy-start = (f32[48,48,128]{2,1,0:T(8,128)S(1)}, f32[48,48,128]{2,1,0:T(8,128)}, u32[]{:S(2)}) copy-start(f32[48,48,128]{2,1,0:T(8,128)} %refs_7_.1) | copy-start | bytes 3538948
  9.5 1.1 %copy-start.2 = (bf16[48,48,128]{2,1,0:T(8,128)(2,1)S(1)}, bf16[48,48,128]{2,1,0:T(8,128)(2,1)}, u32[]{:S(2)}) copy-start(bf16[48,48,128]{2,1,0:T(8,128)(2,1)} %refs_2_.5) | copy-start | bytes 1769476
  11.1 0.7 %copy-start.5 = (f32[3]{0:T(128)S(1)}, f32[3]{0:T(128)}, u32[]{:S(2)}) copy-start(f32[3]{0:T(128)} %param.12) | copy-start | bytes 40
  11.1 0.8 %copy-start.6 = (f32[72,72]{1,0:T(8,128)S(1)}, f32[72,72]{1,0:T(8,128)}, u32[]{:S(2)}) copy-start(f32[72,72]{1,0:T(8,128)} %refs_3_) | copy-start | bytes 62212
  11.1 0.8 %copy-start.7 = (f32[56,56]{1,0:T(8,128)S(1)}, f32[56,56]{1,0:T(8,128)}, u32[]{:S(2)}) copy-start(f32[56,56]{1,0:T(8,128)} %refs_1_.6) | copy-start | bytes 37636
  11.1 0.8 %copy-start.8 = (f32[56,56]{1,0:T(8,128)S(1)}, f32[56,56]{1,0:T(8,128)}, u32[]{:S(2)}) copy-start(f32[56,56]{1,0:T(8,128)} %refs_2_.3) | copy-start | bytes 37636
  11.1 0.8 %copy-start.9 = (f32[16,16]{1,0:T(8,128)S(1)}, f32[16,16]{1,0:T(8,128)}, u32[]{:S(2)}) copy-start(f32[16,16]{1,0:T(8,128)} %refs_6_.1) | copy-start | bytes 3076
  11.1 0.7 %copy-start.10 = (f32[56]{0:T(128)S(1)}, f32[56]{0:T(128)}, u32[]{:S(2)}) copy-start(f32[56]{0:T(128)} %param.17) | copy-start | bytes 676
  11.1 0.7 %copy-start.11 = (f32[72]{0:T(128)S(1)}, f32[72]{0:T(128)}, u32[]{:S(2)}) copy-start(f32[72]{0:T(128)} %param.18) | copy-start | bytes 868
  11.4 1.4 %collective-permute-start.2 = (f32[192,128]{1,0:T(8,128)S(1)}, f32[192,128]{1,0:T(8,128)S(1)}, u32[]{:S(2)}, u32[]{:S(2)}) collective-permute-start(f32[192,128]{1,0:T(8,128)S(1)} %pack_z_rest.1), channel_id=1, source_target_pairs={{0,1},{1,0},{2,3},{3,2},{4,5},{5,4},{6,7},{7,6},{8,9},{9,8},{10,11... | collective-permute-start | bytes 294920 | tf_op jit(solution)/shard_map/ppermute | solution.py:77
  11.9 3.1 %copy-start.1 = (f32[48,48,128]{2,1,0:T(8,128)S(1)}, f32[48,48,128]{2,1,0:T(8,128)}, u32[]{:S(2)}) copy-start(f32[48,48,128]{2,1,0:T(8,128)} %refs_7_.1) | copy-start | bytes 3538948
  12.8 6.0 %collective-permute-start.3 = (f32[288,128]{1,0:T(8,128)S(1)}, f32[288,128]{1,0:T(8,128)S(1)}, u32[]{:S(2)}, u32[]{:S(2)}) collective-permute-start(f32[288,128]{1,0:T(8,128)S(1)} %get-tuple-element.50), channel_id=1, source_target_pairs={{0,2},{2,0},{4,6},{6,4},{1,3},{3,1},{5,7},{7,5},{8,10},{10,8},{12,... | collective-permute-start | bytes 442376 | tf_op jit(solution)/shard_map/ppermute | solution.py:90
  14.3 4.4 %collective-permute-start.4 = (f32[288,128]{1,0:T(8,128)S(1)}, f32[288,128]{1,0:T(8,128)S(1)}, u32[]{:S(2)}, u32[]{:S(2)}) collective-permute-start(f32[288,128]{1,0:T(8,128)S(1)} %get-tuple-element.51), channel_id=1, source_target_pairs={{0,0},{2,4},{4,2},{6,6},{1,1},{3,5},{5,3},{7,7},{8,8},{10,12},{12,... | collective-permute-start | bytes 442376 | tf_op jit(solution)/shard_map/ppermute | solution.py:90
  15.0 3.7 %copy-start.3 = (bf16[48,48,128]{2,1,0:T(8,128)(2,1)S(1)}, bf16[48,48,128]{2,1,0:T(8,128)(2,1)}, u32[]{:S(2)}) copy-start(bf16[48,48,128]{2,1,0:T(8,128)(2,1)} %refs_2_.5) | copy-start | bytes 1769476
  15.0 3.7 %copy-start.4 = (f32[56]{0:T(128)S(1)}, f32[56]{0:T(128)}, u32[]{:S(2)}) copy-start(f32[56]{0:T(128)} %param.16) | copy-start | bytes 676
  23.0 5.8 %collective-permute-start.5 = (f32[352,128]{1,0:T(8,128)S(1)}, f32[352,128]{1,0:T(8,128)S(1)}, u32[]{:S(2)}, u32[]{:S(2)}) collective-permute-start(f32[352,128]{1,0:T(8,128)S(1)} %get-tuple-element.62), channel_id=1, source_target_pairs={{0,8},{8,0},{16,24},{24,16},{1,9},{9,1},{17,25},{25,17},{2,10},{10... | collective-permute-start | bytes 540680 | tf_op jit(solution)/shard_map/ppermute | solution.py:90
  24.6 4.2 %collective-permute-start.6 = (f32[352,128]{1,0:T(8,128)S(1)}, f32[352,128]{1,0:T(8,128)S(1)}, u32[]{:S(2)}, u32[]{:S(2)}) collective-permute-start(f32[352,128]{1,0:T(8,128)S(1)} %get-tuple-element.63), channel_id=1, source_target_pairs={{0,0},{8,16},{16,8},{24,24},{1,1},{9,17},{17,9},{25,25},{2,2},{10,... | collective-permute-start | bytes 540680 | tf_op jit(solution)/shard_map/ppermute | solution.py:90
  29.0 1.3 %collective-permute-start.7 = (f32[224,128]{1,0:T(8,128)S(1)}, f32[224,128]{1,0:T(8,128)S(1)}, u32[]{:S(2)}, u32[]{:S(2)}) collective-permute-start(f32[224,128]{1,0:T(8,128)S(1)} %pack_back_z.1.refs_1_), channel_id=1, source_target_pairs={{0,1},{1,0},{2,3},{3,2},{4,5},{5,4},{6,7},{7,6},{8,9},{9,8},{10,11... | collective-permute-start | bytes 344072 | tf_op jit(solution)/shard_map/ppermute | solution.py:77
  30.6 9.9 %collective-permute-start.8 = (f32[270,128]{1,0:T(8,128)S(1)}, f32[270,128]{1,0:T(8,128)S(1)}, u32[]{:S(2)}, u32[]{:S(2)}) collective-permute-start(f32[270,128]{1,0:T(8,128)S(1)} %get-tuple-element.68), channel_id=1, source_target_pairs={{0,2},{2,0},{4,6},{6,4},{1,3},{3,1},{5,7},{7,5},{8,10},{10,8},{12,... | collective-permute-start | bytes 414728 | tf_op jit(solution)/shard_map/ppermute | solution.py:90
  36.3 4.3 %collective-permute-start.9 = (f32[270,128]{1,0:T(8,128)S(1)}, f32[270,128]{1,0:T(8,128)S(1)}, u32[]{:S(2)}, u32[]{:S(2)}) collective-permute-start(f32[270,128]{1,0:T(8,128)S(1)} %get-tuple-element.69), channel_id=1, source_target_pairs={{0,0},{2,4},{4,2},{6,6},{1,1},{3,5},{5,3},{7,7},{8,8},{10,12},{12,... | collective-permute-start | bytes 414728 | tf_op jit(solution)/shard_map/ppermute | solution.py:90
